TPU v7x, 512 devices: a whole 4x4x16 slice. The times are simulated.
512 devices in a mesh: lon: 16 (over x, z_hi, core), lat: 32 (over z_lo, y).
Axes of the slice: x: 4, y: 4, z: 16 (z_hi: 2, z_lo: 8; z = z_hi * 8 + z_lo), core: 2. Of those that a mesh axis runs over, the one named last changes fastest.
Arguments:
- features: bfloat16 [256, 1440, 128], P('lat', 'lon'), may hold values from -6 to 6
- queries: bfloat16 [256, 1440, 128], P('lat', 'lon'), may hold values from -200 to 200
- attn_keys: bfloat16 [256, 1440, 128], P('lat', 'lon'), may hold values from -4.5 to 4.5
- attn_values: bfloat16 [256, 1440, 128], P('lat', 'lon'), may hold values from -6 to 6
- cotangent: bfloat16 [256, 1440, 128], P('lat', 'lon'), may hold values from -6 to 6
- conv_near: bfloat16 [3, 3, 128, 128], replicated, may hold values from -0.1875 to 0.1875
- conv_wide: bfloat16 [3, 3, 128, 128], replicated, may hold values from -0.1875 to 0.1875
- proj_qkv: bfloat16 [128, 384], replicated, may hold values from -0.5 to 0.5
- proj_out: bfloat16 [128, 128], replicated, may hold values from -0.5 to 0.5
Outputs:
- feature_grad: bfloat16 [256, 1440, 128], P('lat', 'lon')
- conv_near_grad: float32 [3, 3, 128, 128], replicated
- conv_wide_grad: float32 [3, 3, 128, 128], replicated
- proj_qkv_grad: float32 [128, 384], replicated
- proj_out_grad: float32 [128, 128], replicated
All inputs are finite; a program needn't handle non-finite values.
Results may differ from a plain program's by a relative error of at most 0.012.
Values may be sent and summed in bfloat16 or wider, within the bound.
No kernel may reach another device: no remote copies, remote signals or barrier semaphores. Data moves between devices by JAX's collectives and lax.ppermute only.
A program may use at most 64 MiB of HBM per device.

v0:
```python
import jax
import jax.numpy as jnp
from jax import lax
from jax.sharding import PartitionSpec as P

HEADS = 8


GELU_COEF = 0.7978845608028654
CUBIC_COEF = 0.044715


def padded_2(block, sides, width):
    for axis, dim in sides:
        count = lax.axis_size(axis)
        forward = [(i, i + 1) for i in range(count - 1)]
        forward.append((count - 1, 0))
        backward = [(target, source) for source, target in forward]
        low = lax.ppermute(
            lax.slice_in_dim(block, block.shape[dim] - width, None, axis=dim), axis, forward
        )
        high = lax.ppermute(lax.slice_in_dim(block, 0, width, axis=dim), axis, backward)
        block = jnp.concatenate([low, block, high], axis=dim)
    return block


def gelu_value(pre_act):
    tanh_val = jnp.tanh(GELU_COEF * (pre_act + CUBIC_COEF * pre_act * pre_act * pre_act))
    return 0.5 * pre_act * (1.0 + tanh_val)


def gelu_slope(pre_act):
    tanh_val = jnp.tanh(GELU_COEF * (pre_act + CUBIC_COEF * pre_act * pre_act * pre_act))
    inner_d = GELU_COEF * (1.0 + 3.0 * CUBIC_COEF * pre_act * pre_act)
    return 0.5 * (1.0 + tanh_val) + 0.5 * pre_act * (1.0 - tanh_val * tanh_val) * inner_d


def contract_rows(left, right):
    return lax.dot_general(
        left, right, (((0,), (0,)), ((), ())), preferred_element_type=jnp.float32
    )


def conv_taps(padded, weight, spread, row_count, col_count):
    channels = padded.shape[-1]
    total_sum = jnp.zeros((row_count * col_count, weight.shape[-1]), jnp.float32)
    for row_tap in range(3):
        for col_tap in range(3):
            window = padded[
                row_tap * spread : row_tap * spread + row_count,
                col_tap * spread : col_tap * spread + col_count,
            ]
            total_sum = total_sum + jnp.dot(
                window.reshape(-1, channels),
                weight[row_tap, col_tap],
                preferred_element_type=jnp.float32,
            )
    return total_sum.reshape(row_count, col_count, -1)


def conv_back(padded, weight, spread, row_count, col_count):
    channels = padded.shape[-1]
    total_sum = jnp.zeros((row_count * col_count, weight.shape[-2]), jnp.float32)
    for row_tap in range(3):
        for col_tap in range(3):
            row_at = (2 - row_tap) * spread
            col_at = (2 - col_tap) * spread
            window = padded[row_at : row_at + row_count, col_at : col_at + col_count]
            total_sum = total_sum + jnp.dot(
                window.reshape(-1, channels),
                weight[row_tap, col_tap].T,
                preferred_element_type=jnp.float32,
            )
    return total_sum.reshape(row_count, col_count, -1)


def weight_terms(padded, gradient, spread, row_count, col_count):
    channels = padded.shape[-1]
    flat_grad = gradient.reshape(-1, gradient.shape[-1])
    tap_list = []
    for row_tap in range(3):
        for col_tap in range(3):
            window = padded[
                row_tap * spread : row_tap * spread + row_count,
                col_tap * spread : col_tap * spread + col_count,
            ]
            tap_list.append(contract_rows(window.reshape(-1, channels), flat_grad))
    return jnp.stack(tap_list).reshape(3, 3, channels, -1)


def attend_head(query_h, key_h, value_h, dout_h):
    scale = query_h.shape[-1] ** (-0.5)
    scores = jnp.dot(query_h, key_h.T, preferred_element_type=jnp.float32) * scale
    top_val = jnp.max(scores, axis=1, keepdims=True)
    raised = jnp.exp(scores - top_val)
    probs = raised / jnp.sum(raised, axis=1, keepdims=True)
    probs_low = probs.astype(jnp.bfloat16)
    mixed = jnp.dot(probs_low, value_h, preferred_element_type=jnp.float32).astype(jnp.bfloat16)
    prob_grad = jnp.dot(dout_h, value_h.T, preferred_element_type=jnp.float32)
    delta_sum = jnp.sum(
        dout_h.astype(jnp.float32) * mixed.astype(jnp.float32), axis=1, keepdims=True
    )
    score_grad = (probs * (prob_grad - delta_sum) * scale).astype(jnp.bfloat16)
    query_grad = jnp.dot(score_grad, key_h, preferred_element_type=jnp.float32).astype(jnp.bfloat16)
    key_grad = contract_rows(score_grad, query_h).astype(jnp.bfloat16)
    value_grad = contract_rows(probs_low, dout_h).astype(jnp.bfloat16)
    return (mixed, query_grad, key_grad, value_grad)


def clear_poles(padded, width):
    lat_count = lax.axis_size("lat")
    position = lax.axis_index("lat")
    core = padded.shape[0] - 2 * width
    global_row = position * core + jnp.arange(padded.shape[0], dtype=jnp.int32) - width
    inside = (global_row >= 0) & (global_row < lat_count * core)
    return jnp.where(inside[:, None, None], padded, jnp.zeros_like(padded))


def on_device(
    features, queries, attn_keys, attn_values, cotangent, conv_near, conv_wide, proj_qkv, proj_out
):
    row_count, col_count, channels = features.shape
    head_width = channels // HEADS
    factor = float(row_count * col_count * lax.axis_size("lat") * lax.axis_size("lon")) ** (-0.5)

    def to_items(field):
        return (
            field.reshape(row_count, col_count, HEADS, head_width)
            .transpose(0, 2, 1, 3)
            .reshape(row_count * HEADS, col_count, head_width)
        )

    def from_items(field):
        return (
            field.reshape(row_count, HEADS, col_count, head_width)
            .transpose(0, 2, 1, 3)
            .reshape(row_count, col_count, channels)
        )

    pad_x = clear_poles(padded_2(features, (("lon", 1), ("lat", 0)), 1), 1)
    pre_near = conv_taps(pad_x, conv_near, 1, row_count, col_count)
    hidden_one = (features.astype(jnp.float32) + gelu_value(pre_near)).astype(jnp.bfloat16)
    pad_hidden = clear_poles(padded_2(hidden_one, (("lon", 1), ("lat", 0)), 4), 4)
    pre_wide = conv_taps(pad_hidden, conv_wide, 4, row_count, col_count)
    hidden_two = (hidden_one.astype(jnp.float32) + gelu_value(pre_wide)).astype(jnp.bfloat16)
    flat_cot = cotangent.reshape(-1, channels)
    out_grad = (
        jnp.dot(flat_cot, proj_out.T, preferred_element_type=jnp.float32)
        .astype(jnp.bfloat16)
        .reshape(row_count, col_count, channels)
    )
    moved_q, moved_k, moved_v, moved_d = (
        lax.all_to_all(to_items(queries), "lon", split_axis=0, concat_axis=1, tiled=True),
        lax.all_to_all(to_items(attn_keys), "lon", split_axis=0, concat_axis=1, tiled=True),
        lax.all_to_all(to_items(attn_values), "lon", split_axis=0, concat_axis=1, tiled=True),
        lax.all_to_all(to_items(out_grad), "lon", split_axis=0, concat_axis=1, tiled=True),
    )
    mixed, query_grad, key_grad, value_grad = lax.map(
        lambda pieces: attend_head(*pieces), (moved_q, moved_k, moved_v, moved_d)
    )
    band_m, band_q, band_k, band_v = (
        lax.all_to_all(mixed, "lon", split_axis=1, concat_axis=0, tiled=True),
        lax.all_to_all(query_grad, "lon", split_axis=1, concat_axis=0, tiled=True),
        lax.all_to_all(key_grad, "lon", split_axis=1, concat_axis=0, tiled=True),
        lax.all_to_all(value_grad, "lon", split_axis=1, concat_axis=0, tiled=True),
    )
    out_term = contract_rows(from_items(band_m).reshape(-1, channels), flat_cot) * factor
    stacked = jnp.concatenate(
        [from_items(band_q), from_items(band_k), from_items(band_v)], axis=-1
    ).reshape(-1, 3 * channels)
    attn_grad = (
        jnp.dot(stacked, proj_qkv.T, preferred_element_type=jnp.float32)
        .astype(jnp.bfloat16)
        .reshape(row_count, col_count, channels)
    )
    qkv_term = contract_rows(hidden_two.reshape(-1, channels), stacked) * factor
    outer_total = cotangent.astype(jnp.float32) + attn_grad.astype(jnp.float32)
    wide_grad = (outer_total * gelu_slope(pre_wide)).astype(jnp.bfloat16)
    pad_wide = clear_poles(padded_2(wide_grad, (("lon", 1), ("lat", 0)), 4), 4)
    near_total = outer_total + conv_back(pad_wide, conv_wide, 4, row_count, col_count)
    wide_term = weight_terms(pad_hidden, wide_grad, 4, row_count, col_count) * factor
    near_grad = (near_total * gelu_slope(pre_near)).astype(jnp.bfloat16)
    pad_near = clear_poles(padded_2(near_grad, (("lon", 1), ("lat", 0)), 1), 1)
    feature_grad = (near_total + conv_back(pad_near, conv_near, 1, row_count, col_count)).astype(
        jnp.bfloat16
    )
    near_term = weight_terms(pad_x, near_grad, 1, row_count, col_count) * factor
    near_sum, wide_sum, qkv_sum, out_sum = lax.psum(
        (near_term, wide_term, qkv_term, out_term), ("lon", "lat")
    )
    return (feature_grad, near_sum, wide_sum, qkv_sum, out_sum)


def solution(mesh):
    return jax.shard_map(
        on_device,
        mesh=mesh,
        in_specs=(
            P("lat", "lon", None),
            P("lat", "lon", None),
            P("lat", "lon", None),
            P("lat", "lon", None),
            P("lat", "lon", None),
            P(),
            P(),
            P(),
            P(),
        ),
        out_specs=(P("lat", "lon", None), P(), P(), P(), P()),
        check_vma=False,
    )
```

profile of v0, /device:TPU:1, one launch (start us, length us, event | category | flops | bytes accessed | tf_op | source)
XLA Modules:
  0.0 892.9 jit_solution(12902460496655913169)
XLA Ops:
  8.2 16.8 %collective-permute-start = (bf16[8,1,128]{2,1,0:T(2,128)(2,1)S(1)}, bf16[8,1,128]{2,1,0:T(2,128)(2,1)S(1)}, u32[]{:S(2)}, u32[]{:S(2)}) collective-permute-start(bf16[8,1,128]{2,1,0:T(2,128)(2,1)S(1)} %get-tuple-element.155), channel_id=1, source_target_pairs={{0,32},{32,64},{64,96},{96,128},{128,160},{160,192},{192,224},{224... | collective-permute-start | bytes 6152 | tf_op jit(solution)/shard_map/ppermute | solution.py:19
  30.2 14.6 %all-to-all-start.3 = ((bf16[64,90,16]{1,2,0:T(8,128)(2,1)}), bf16[64,90,16]{1,2,0:T(8,128)(2,1)S(1)}, u32[]{:S(2)}, u32[]{:S(2)}) async-start(bf16[64,90,16]{1,2,0:T(8,128)(2,1)} %bitcast.24), calls=%async_computation.3 | async-start | bytes 524288 | tf_op jit(solution)/shard_map/all_to_all | solution.py:156
  44.9 3.4 collective-permute-start.2
  48.3 10.8 %collective-permute-start.3 = (bf16[1,92,128]{2,1,0:T(8,128)(2,1)S(1)}, bf16[1,92,128]{2,1,0:T(8,128)(2,1)S(1)}, u32[]{:S(2)}, u32[]{:S(2)}) collective-permute-start(bf16[1,92,128]{2,1,0:T(8,128)(2,1)S(1)} %get-tuple-element.148), channel_id=1, source_target_pairs={{1,0},{2,1},{3,2},{4,3},{5,4},{6,5},{7,6},{8,7},{9,8},{10,9},{11,1... | collective-permute-start | bytes 70664 | tf_op jit(solution)/shard_map/ppermute | solution.py:22
  65.6 15.0 %all-to-all-start = ((bf16[64,90,16]{1,2,0:T(8,128)(2,1)}), bf16[64,90,16]{1,2,0:T(8,128)(2,1)S(1)}, u32[]{:S(2)}, u32[]{:S(2)}) async-start(bf16[64,90,16]{1,2,0:T(8,128)(2,1)} %bitcast.10), calls=%async_computation | async-start | bytes 524288 | tf_op jit(solution)/shard_map/all_to_all | solution.py:153
  81.3 15.2 %all-to-all-done = bf16[64,90,16]{1,2,0:T(8,128)(2,1)S(1)} async-done(((bf16[64,90,16]{1,2,0:T(8,128)(2,1)}), bf16[64,90,16]{1,2,0:T(8,128)(2,1)S(1)}, u32[]{:S(2)}, u32[]{:S(2)}) %all-to-all-start) | async-done | bytes 184352 | tf_op jit(solution)/shard_map/all_to_all | solution.py:153
  96.5 4.4 all-to-all-start.1
  101.4 12.2 %collective-permute-start.4 = (bf16[8,4,128]{2,1,0:T(4,128)(2,1)S(1)}, bf16[8,4,128]{2,1,0:T(4,128)(2,1)S(1)}, u32[]{:S(2)}, u32[]{:S(2)}) collective-permute-start(bf16[8,4,128]{2,1,0:T(4,128)(2,1)S(1)} %get-tuple-element.153), channel_id=1, source_target_pairs={{0,32},{32,64},{64,96},{96,128},{128,160},{160,192},{192,224},{224... | collective-permute-start | bytes 24584 | tf_op jit(solution)/shard_map/ppermute | solution.py:19
  116.6 10.8 %collective-permute-done.5 = bf16[8,4,128]{2,1,0:T(4,128)(2,1)S(1)} collective-permute-done((bf16[8,4,128]{2,1,0:T(4,128)(2,1)S(1)}, bf16[8,4,128]{2,1,0:T(4,128)(2,1)S(1)}, u32[]{:S(2)}, u32[]{:S(2)}) %collective-permute-start.5) | collective-permute-done | bytes 8224 | tf_op jit(solution)/shard_map/ppermute | solution.py:22
  127.4 6.8 all-to-all-start.2
  136.2 16.1 %collective-permute-start.7 = (bf16[4,98,128]{2,1,0:T(8,128)(2,1)S(1)}, bf16[4,98,128]{2,1,0:T(8,128)(2,1)S(1)}, u32[]{:S(2)}, u32[]{:S(2)}) collective-permute-start(bf16[4,98,128]{2,1,0:T(8,128)(2,1)S(1)} %get-tuple-element.144), channel_id=1, source_target_pairs={{1,0},{2,1},{3,2},{4,3},{5,4},{6,5},{7,6},{8,7},{9,8},{10,9},{11,1... | collective-permute-start | bytes 301064 | tf_op jit(solution)/shard_map/ppermute | solution.py:22
  152.3 5.6 collective-permute-done.6
  166.4 52.7 %while.16 = (s32[]{:T(128)}, bf16[4,1440,16]{1,2,0:T(8,128)(2,1)}, bf16[4,1440,16]{1,2,0:T(8,128)(2,1)}, bf16[4,1440,16]{1,2,0:T(8,128)(2,1)}, bf16[4,1440,16]{1...) while((s32[]{:T(128)}, bf16[4,1440,16]{1,2,0:T(8,128)(2,1)}, ...), condition=%wide.region_4.5_spmd, body=%wide.region_0.4_spmd.sunk | while | flops 425268000 | bytes 60513136 | solution.py:158
  219.1 2.8 copy.89
  224.1 11.7 %all-to-all-start.6 = ((bf16[16,2,2880]{2,1,0:T(2,128)(2,1)}), bf16[16,2,2880]{2,1,0:T(2,128)(2,1)S(1)}, u32[]{:S(2)}, u32[]{:S(2)}) async-start(bf16[16,2,2880]{2,1,0:T(2,128)(2,1)} %reshape.310), calls=%async_computation.6 | async-start | bytes 376832 | tf_op jit(solution)/shard_map/all_to_all | solution.py:165
  236.5 2.8 copy.81
  241.6 9.4 %all-to-all-done.6 = bf16[16,2,2880]{2,1,0:T(2,128)(2,1)S(1)} async-done(((bf16[16,2,2880]{2,1,0:T(2,128)(2,1)}), bf16[16,2,2880]{2,1,0:T(2,128)(2,1)S(1)}, u32[]{:S(2)}, u32[]{:S(2)}) %all-to-all-start.6) | async-done | bytes 184352 | tf_op jit(solution)/shard_map/all_to_all | solution.py:165
  251.0 8.3 all-to-all-start.4
  262.8 2.8 copy.85
  267.9 6.8 all-to-all-done.4
  274.7 7.7 all-to-all-start.5
  284.0 2.8 copy.100
  293.4 2.7 reshape.315
  299.4 14.4 %all-to-all-start.7 = ((bf16[16,2,2880]{2,1,0:T(2,128)(2,1)}), bf16[16,2,2880]{2,1,0:T(2,128)(2,1)}, u32[]{:S(2)}, u32[]{:S(2)}) async-start(bf16[16,2,2880]{2,1,0:T(2,128)(2,1)} %reshape.316), calls=%async_computation.7 | async-start | bytes 376832 | tf_op jit(solution)/shard_map/all_to_all | solution.py:162
  314.3 2.7 reshape.313
  323.5 12.2 %collective-permute-start.8 = (bf16[8,4,128]{2,1,0:T(4,128)(2,1)S(1)}, bf16[8,4,128]{2,1,0:T(4,128)(2,1)S(1)}, u32[]{:S(2)}, u32[]{:S(2)}) collective-permute-start(bf16[8,4,128]{2,1,0:T(4,128)(2,1)S(1)} %get-tuple-element.151), channel_id=1, source_target_pairs={{0,32},{32,64},{64,96},{96,128},{128,160},{160,192},{192,224},{224... | collective-permute-start | bytes 24584 | tf_op jit(solution)/shard_map/ppermute | solution.py:19
  341.8 2.7 reshape.317
  351.7 12.1 %collective-permute-start.11 = (bf16[4,98,128]{2,1,0:T(8,128)(2,1)S(1)}, bf16[4,98,128]{2,1,0:T(8,128)(2,1)S(1)}, u32[]{:S(2)}, u32[]{:S(2)}) collective-permute-start(bf16[4,98,128]{2,1,0:T(8,128)(2,1)S(1)} %get-tuple-element.142), channel_id=1, source_target_pairs={{1,0},{2,1},{3,2},{4,3},{5,4},{6,5},{7,6},{8,7},{9,8},{10,9},{11,1... | collective-permute-start | bytes 301064 | tf_op jit(solution)/shard_map/ppermute | solution.py:22
  374.7 10.7 %collective-permute-start.12 = (bf16[8,1,128]{2,1,0:T(2,128)(2,1)S(1)}, bf16[8,1,128]{2,1,0:T(2,128)(2,1)S(1)}, u32[]{:S(2)}, u32[]{:S(2)}) collective-permute-start(bf16[8,1,128]{2,1,0:T(2,128)(2,1)S(1)} %get-tuple-element.149), channel_id=1, source_target_pairs={{0,32},{32,64},{64,96},{96,128},{128,160},{160,192},{192,224},{224... | collective-permute-start | bytes 6152 | tf_op jit(solution)/shard_map/ppermute | solution.py:19
  389.6 9.4 %collective-permute-done.13 = bf16[8,1,128]{2,1,0:T(2,128)(2,1)S(1)} collective-permute-done((bf16[8,1,128]{2,1,0:T(2,128)(2,1)S(1)}, bf16[8,1,128]{2,1,0:T(2,128)(2,1)S(1)}, u32[]{:S(2)}, u32[]{:S(2)}) %collective-permute-start.13) | collective-permute-done | bytes 2080 | tf_op jit(solution)/shard_map/ppermute | solution.py:22
  401.0 12.7 %collective-permute-start.15 = (bf16[1,92,128]{2,1,0:T(8,128)(2,1)S(1)}, bf16[1,92,128]{2,1,0:T(8,128)(2,1)S(1)}, u32[]{:S(2)}, u32[]{:S(2)}) collective-permute-start(bf16[1,92,128]{2,1,0:T(8,128)(2,1)S(1)} %get-tuple-element.146), channel_id=1, source_target_pairs={{1,0},{2,1},{3,2},{4,3},{5,4},{6,5},{7,6},{8,7},{9,8},{10,9},{11,1... | collective-permute-start | bytes 70664 | tf_op jit(solution)/shard_map/ppermute | solution.py:22
  423.5 455.4 %all-reduce.3.cloned.1.call-done = (f32[3,3,128,128]{3,2,1,0:T(8,128)}, f32[3,3,128,128]{3,2,1,0:T(8,128)}, f32[128,384]{1,0:T(8,128)}, f32[128,128]{1,0:T(8,128)}) async-done(((f32[3,3,128,128]{3,2,1,0:T(8,128)}, f32[3,3,128,128]{3,2,1,0:T(8,128)}, f32[128,384]{1,0:T(8,128)}, f32[128,128]{1,0:T(8,128)}), (f32[3,3,128,128]{3,2,1,0:T(8,128)}, f32[3,3,128,128]{3,2,1,0:T(8,128)}, f32[128,384]{1,0:T(8,128)}, ...) | async-done | bytes 1441808 | tf_op jit(solution)/shard_map/psum | solution.py:188
  (284 shorter events, 155.3 us)
Async XLA Ops:
  7.2 312.4 %copy-start = (bf16[128,384]{1,0:T(8,128)(2,1)S(1)}, bf16[128,384]{1,0:T(8,128)(2,1)}, u32[]{:S(2)}) copy-start(bf16[128,384]{1,0:T(8,128)(2,1)} %param.18) | copy-start | bytes 294916
  8.2 36.7 %collective-permute-start = (bf16[8,1,128]{2,1,0:T(2,128)(2,1)S(1)}, bf16[8,1,128]{2,1,0:T(2,128)(2,1)S(1)}, u32[]{:S(2)}, u32[]{:S(2)}) collective-permute-start(bf16[8,1,128]{2,1,0:T(2,128)(2,1)S(1)} %get-tuple-element.155), channel_id=1, source_target_pairs={{0,32},{32,64},{64,96},{96,128},{128,160},{160,192},{192,224},{224... | collective-permute-start | bytes 6152 | tf_op jit(solution)/shard_map/ppermute | solution.py:19
  25.0 19.8 %collective-permute-start.1 = (bf16[8,1,128]{2,1,0:T(2,128)(2,1)S(1)}, bf16[8,1,128]{2,1,0:T(2,128)(2,1)S(1)}, u32[]{:S(2)}, u32[]{:S(2)}) collective-permute-start(bf16[8,1,128]{2,1,0:T(2,128)(2,1)S(1)} %get-tuple-element.156), channel_id=1, source_target_pairs={{32,0},{64,32},{96,64},{128,96},{160,128},{192,160},{224,192},{256... | collective-permute-start | bytes 6152 | tf_op jit(solution)/shard_map/ppermute | solution.py:22
  30.2 35.4 %all-to-all-start.3 = ((bf16[64,90,16]{1,2,0:T(8,128)(2,1)}), bf16[64,90,16]{1,2,0:T(8,128)(2,1)S(1)}, u32[]{:S(2)}, u32[]{:S(2)}) async-start(bf16[64,90,16]{1,2,0:T(8,128)(2,1)} %bitcast.24), calls=%async_computation.3 | async-start | bytes 524288 | tf_op jit(solution)/shard_map/all_to_all | solution.py:156
  44.9 17.8 %collective-permute-start.2 = (bf16[1,92,128]{2,1,0:T(8,128)(2,1)S(1)}, bf16[1,92,128]{2,1,0:T(8,128)(2,1)S(1)}, u32[]{:S(2)}, u32[]{:S(2)}) collective-permute-start(bf16[1,92,128]{2,1,0:T(8,128)(2,1)S(1)} %get-tuple-element.147), channel_id=1, source_target_pairs={{0,1},{1,2},{2,3},{3,4},{4,5},{5,6},{6,7},{7,8},{8,9},{9,10},{10,1... | collective-permute-start | bytes 70664 | tf_op jit(solution)/shard_map/ppermute | solution.py:19
  48.3 14.5 %collective-permute-start.3 = (bf16[1,92,128]{2,1,0:T(8,128)(2,1)S(1)}, bf16[1,92,128]{2,1,0:T(8,128)(2,1)S(1)}, u32[]{:S(2)}, u32[]{:S(2)}) collective-permute-start(bf16[1,92,128]{2,1,0:T(8,128)(2,1)S(1)} %get-tuple-element.148), channel_id=1, source_target_pairs={{1,0},{2,1},{3,2},{4,3},{5,4},{6,5},{7,6},{8,7},{9,8},{10,9},{11,1... | collective-permute-start | bytes 70664 | tf_op jit(solution)/shard_map/ppermute | solution.py:22
  64.9 50.7 %copy-start.20 = (bf16[8,90,128]{2,0,1:T(8,128)(2,1)S(1)}, bf16[8,90,128]{2,0,1:T(8,128)(2,1)}, u32[]{:S(2)}) copy-start(bf16[8,90,128]{2,0,1:T(8,128)(2,1)} %param.14) | copy-start | bytes 552964
  65.6 30.9 %all-to-all-start = ((bf16[64,90,16]{1,2,0:T(8,128)(2,1)}), bf16[64,90,16]{1,2,0:T(8,128)(2,1)S(1)}, u32[]{:S(2)}, u32[]{:S(2)}) async-start(bf16[64,90,16]{1,2,0:T(8,128)(2,1)} %bitcast.10), calls=%async_computation | async-start | bytes 524288 | tf_op jit(solution)/shard_map/all_to_all | solution.py:153
  96.5 30.9 %all-to-all-start.1 = ((bf16[64,90,16]{1,2,0:T(8,128)(2,1)}), bf16[64,90,16]{1,2,0:T(8,128)(2,1)S(1)}, u32[]{:S(2)}, u32[]{:S(2)}) async-start(bf16[64,90,16]{1,2,0:T(8,128)(2,1)} %bitcast.15), calls=%async_computation.1 | async-start | bytes 524288 | tf_op jit(solution)/shard_map/all_to_all | solution.py:154
  101.2 56.8 %copy-start.3 = (f32[8,90,128]{2,1,0:T(8,128)}, f32[8,90,128]{2,1,0:T(8,128)S(1)}, u32[]{:S(2)}) copy-start(f32[8,90,128]{2,1,0:T(8,128)S(1)} %reshape.255) | copy-start | bytes 1105924
  101.4 63.0 %copy-start.6 = (bf16[8,90,128]{2,1,0:T(8,128)(2,1)}, bf16[8,90,128]{2,1,0:T(8,128)(2,1)S(1)}, u32[]{:S(2)}) copy-start(bf16[8,90,128]{2,1,0:T(8,128)(2,1)S(1)} %add_convert_fusion.2) | copy-start | bytes 552964
  101.4 15.2 %collective-permute-start.4 = (bf16[8,4,128]{2,1,0:T(4,128)(2,1)S(1)}, bf16[8,4,128]{2,1,0:T(4,128)(2,1)S(1)}, u32[]{:S(2)}, u32[]{:S(2)}) collective-permute-start(bf16[8,4,128]{2,1,0:T(4,128)(2,1)S(1)} %get-tuple-element.153), channel_id=1, source_target_pairs={{0,32},{32,64},{64,96},{96,128},{128,160},{160,192},{192,224},{224... | collective-permute-start | bytes 24584 | tf_op jit(solution)/shard_map/ppermute | solution.py:19
  113.7 13.7 %collective-permute-start.5 = (bf16[8,4,128]{2,1,0:T(4,128)(2,1)S(1)}, bf16[8,4,128]{2,1,0:T(4,128)(2,1)S(1)}, u32[]{:S(2)}, u32[]{:S(2)}) collective-permute-start(bf16[8,4,128]{2,1,0:T(4,128)(2,1)S(1)} %get-tuple-element.154), channel_id=1, source_target_pairs={{32,0},{64,32},{96,64},{128,96},{160,128},{192,160},{224,192},{256... | collective-permute-start | bytes 24584 | tf_op jit(solution)/shard_map/ppermute | solution.py:22
  127.4 38.5 %all-to-all-start.2 = ((bf16[64,90,16]{1,2,0:T(8,128)(2,1)}), bf16[64,90,16]{1,2,0:T(8,128)(2,1)S(1)}, u32[]{:S(2)}, u32[]{:S(2)}) async-start(bf16[64,90,16]{1,2,0:T(8,128)(2,1)} %bitcast.20), calls=%async_computation.2 | async-start | bytes 524288 | tf_op jit(solution)/shard_map/all_to_all | solution.py:155
  134.3 23.7 %collective-permute-start.6 = (bf16[4,98,128]{2,1,0:T(8,128)(2,1)S(1)}, bf16[4,98,128]{2,1,0:T(8,128)(2,1)S(1)}, u32[]{:S(2)}, u32[]{:S(2)}) collective-permute-start(bf16[4,98,128]{2,1,0:T(8,128)(2,1)S(1)} %get-tuple-element.143), channel_id=1, source_target_pairs={{0,1},{1,2},{2,3},{3,4},{4,5},{5,6},{6,7},{7,8},{8,9},{9,10},{10,1... | collective-permute-start | bytes 301064 | tf_op jit(solution)/shard_map/ppermute | solution.py:19
  136.2 21.8 %collective-permute-start.7 = (bf16[4,98,128]{2,1,0:T(8,128)(2,1)S(1)}, bf16[4,98,128]{2,1,0:T(8,128)(2,1)S(1)}, u32[]{:S(2)}, u32[]{:S(2)}) collective-permute-start(bf16[4,98,128]{2,1,0:T(8,128)(2,1)S(1)} %get-tuple-element.144), channel_id=1, source_target_pairs={{1,0},{2,1},{3,2},{4,3},{5,4},{6,5},{7,6},{8,7},{9,8},{10,9},{11,1... | collective-permute-start | bytes 301064 | tf_op jit(solution)/shard_map/ppermute | solution.py:22
  166.4 69.4 %copy-start.10 = (bf16[3,3,128,128]{3,2,1,0:T(8,128)(2,1)S(1)}, bf16[3,3,128,128]{3,2,1,0:T(8,128)(2,1)}, u32[]{:S(2)}) copy-start(bf16[3,3,128,128]{3,2,1,0:T(8,128)(2,1)} %param.17) | copy-start | bytes 884740
  224.1 26.9 %all-to-all-start.6 = ((bf16[16,2,2880]{2,1,0:T(2,128)(2,1)}), bf16[16,2,2880]{2,1,0:T(2,128)(2,1)S(1)}, u32[]{:S(2)}, u32[]{:S(2)}) async-start(bf16[16,2,2880]{2,1,0:T(2,128)(2,1)} %reshape.310), calls=%async_computation.6 | async-start | bytes 376832 | tf_op jit(solution)/shard_map/all_to_all | solution.py:165
  239.3 44.2 %copy-start.17 = (bf16[720,128]{1,0:T(8,128)(2,1)S(1)}, bf16[720,128]{1,0:T(8,128)(2,1)}, u32[]{:S(2)}) copy-start(bf16[720,128]{1,0:T(8,128)(2,1)} %reshape.263) | copy-start | bytes 552964
  241.6 42.2 %copy-start.16 = (bf16[720,128]{1,0:T(8,128)(2,1)S(1)}, bf16[720,128]{1,0:T(8,128)(2,1)}, u32[]{:S(2)}) copy-start(bf16[720,128]{1,0:T(8,128)(2,1)} %reshape.264) | copy-start | bytes 552964
  251.0 23.6 %all-to-all-start.4 = ((bf16[16,2,2880]{2,1,0:T(2,128)(2,1)}), bf16[16,2,2880]{2,1,0:T(2,128)(2,1)S(1)}, u32[]{:S(2)}, u32[]{:S(2)}) async-start(bf16[16,2,2880]{2,1,0:T(2,128)(2,1)} %reshape.314), calls=%async_computation.4 | async-start | bytes 376832 | tf_op jit(solution)/shard_map/all_to_all | solution.py:163
  274.7 24.8 %all-to-all-start.5 = ((bf16[16,2,2880]{2,1,0:T(2,128)(2,1)}), bf16[16,2,2880]{2,1,0:T(2,128)(2,1)}, u32[]{:S(2)}, u32[]{:S(2)}) async-start(bf16[16,2,2880]{2,1,0:T(2,128)(2,1)} %reshape.312), calls=%async_computation.5 | async-start | bytes 376832 | tf_op jit(solution)/shard_map/all_to_all | solution.py:164
  299.4 42.3 %all-to-all-start.7 = ((bf16[16,2,2880]{2,1,0:T(2,128)(2,1)}), bf16[16,2,2880]{2,1,0:T(2,128)(2,1)}, u32[]{:S(2)}, u32[]{:S(2)}) async-start(bf16[16,2,2880]{2,1,0:T(2,128)(2,1)} %reshape.316), calls=%async_computation.7 | async-start | bytes 376832 | tf_op jit(solution)/shard_map/all_to_all | solution.py:162
  313.9 565.1 %all-reduce.3.cloned.1.call-start = ((), (), s32[]{:S(2)}) async-start(), calls=%async_computation.8 | async-start | bytes 2883584 | tf_op jit(solution)/shard_map/psum | solution.py:188
  323.5 23.5 %collective-permute-start.8 = (bf16[8,4,128]{2,1,0:T(4,128)(2,1)S(1)}, bf16[8,4,128]{2,1,0:T(4,128)(2,1)S(1)}, u32[]{:S(2)}, u32[]{:S(2)}) collective-permute-start(bf16[8,4,128]{2,1,0:T(4,128)(2,1)S(1)} %get-tuple-element.151), channel_id=1, source_target_pairs={{0,32},{32,64},{64,96},{96,128},{128,160},{160,192},{192,224},{224... | collective-permute-start | bytes 24584 | tf_op jit(solution)/shard_map/ppermute | solution.py:19
  335.8 13.7 %collective-permute-start.9 = (bf16[8,4,128]{2,1,0:T(4,128)(2,1)S(1)}, bf16[8,4,128]{2,1,0:T(4,128)(2,1)S(1)}, u32[]{:S(2)}, u32[]{:S(2)}) collective-permute-start(bf16[8,4,128]{2,1,0:T(4,128)(2,1)S(1)} %get-tuple-element.152), channel_id=1, source_target_pairs={{32,0},{64,32},{96,64},{128,96},{160,128},{192,160},{224,192},{256... | collective-permute-start | bytes 24584 | tf_op jit(solution)/shard_map/ppermute | solution.py:22
  349.6 15.4 %collective-permute-start.10 = (bf16[4,98,128]{2,1,0:T(8,128)(2,1)S(1)}, bf16[4,98,128]{2,1,0:T(8,128)(2,1)S(1)}, u32[]{:S(2)}, u32[]{:S(2)}) collective-permute-start(bf16[4,98,128]{2,1,0:T(8,128)(2,1)S(1)} %get-tuple-element.141), channel_id=1, source_target_pairs={{0,1},{1,2},{2,3},{3,4},{4,5},{5,6},{6,7},{7,8},{8,9},{9,10},{10,1... | collective-permute-start | bytes 301064 | tf_op jit(solution)/shard_map/ppermute | solution.py:19
  351.7 14.2 %collective-permute-start.11 = (bf16[4,98,128]{2,1,0:T(8,128)(2,1)S(1)}, bf16[4,98,128]{2,1,0:T(8,128)(2,1)S(1)}, u32[]{:S(2)}, u32[]{:S(2)}) collective-permute-start(bf16[4,98,128]{2,1,0:T(8,128)(2,1)S(1)} %get-tuple-element.142), channel_id=1, source_target_pairs={{1,0},{2,1},{3,2},{4,3},{5,4},{6,5},{7,6},{8,7},{9,8},{10,9},{11,1... | collective-permute-start | bytes 301064 | tf_op jit(solution)/shard_map/ppermute | solution.py:22
  374.7 14.9 %collective-permute-start.12 = (bf16[8,1,128]{2,1,0:T(2,128)(2,1)S(1)}, bf16[8,1,128]{2,1,0:T(2,128)(2,1)S(1)}, u32[]{:S(2)}, u32[]{:S(2)}) collective-permute-start(bf16[8,1,128]{2,1,0:T(2,128)(2,1)S(1)} %get-tuple-element.149), channel_id=1, source_target_pairs={{0,32},{32,64},{64,96},{96,128},{128,160},{160,192},{192,224},{224... | collective-permute-start | bytes 6152 | tf_op jit(solution)/shard_map/ppermute | solution.py:19
  385.4 13.6 %collective-permute-start.13 = (bf16[8,1,128]{2,1,0:T(2,128)(2,1)S(1)}, bf16[8,1,128]{2,1,0:T(2,128)(2,1)S(1)}, u32[]{:S(2)}, u32[]{:S(2)}) collective-permute-start(bf16[8,1,128]{2,1,0:T(2,128)(2,1)S(1)} %get-tuple-element.150), channel_id=1, source_target_pairs={{32,0},{64,32},{96,64},{128,96},{160,128},{192,160},{224,192},{256... | collective-permute-start | bytes 6152 | tf_op jit(solution)/shard_map/ppermute | solution.py:22
  399.0 15.6 %collective-permute-start.14 = (bf16[1,92,128]{2,1,0:T(8,128)(2,1)S(1)}, bf16[1,92,128]{2,1,0:T(8,128)(2,1)S(1)}, u32[]{:S(2)}, u32[]{:S(2)}) collective-permute-start(bf16[1,92,128]{2,1,0:T(8,128)(2,1)S(1)} %get-tuple-element.145), channel_id=1, source_target_pairs={{0,1},{1,2},{2,3},{3,4},{4,5},{5,6},{6,7},{7,8},{8,9},{9,10},{10,1... | collective-permute-start | bytes 70664 | tf_op jit(solution)/shard_map/ppermute | solution.py:19
  401.0 13.7 %collective-permute-start.15 = (bf16[1,92,128]{2,1,0:T(8,128)(2,1)S(1)}, bf16[1,92,128]{2,1,0:T(8,128)(2,1)S(1)}, u32[]{:S(2)}, u32[]{:S(2)}) collective-permute-start(bf16[1,92,128]{2,1,0:T(8,128)(2,1)S(1)} %get-tuple-element.146), channel_id=1, source_target_pairs={{1,0},{2,1},{3,2},{4,3},{5,4},{6,5},{7,6},{8,7},{9,8},{10,9},{11,1... | collective-permute-start | bytes 70664 | tf_op jit(solution)/shard_map/ppermute | solution.py:22
  (18 other events, 311.1 us)
Sparse Core Ops, SparseCore 0:
  414.7 464.1 all-reduce.2
where the time goes:
time: 899 us; the launch traced here: 893 us
  waiting for transfers between devices  516 us (57%)
  starting transfers between devices  204 us (23%)
  local copies, waits for them, and re-layouts  73.8 us (8%)
  matrix products  68.3 us (8%)
  between operations  15.7 us (2%)
  other arithmetic  14.5 us (2%)
    psum x1, waiting for transfers between devices, on_device(): lax.psum((near_term, wide_term, qkv_term, out_term), ('lon', 'lat'))  455 us
    ppermute x8, starting transfers between devices, padded_2(): lax.ppermute(lax.slice_in_dim(block, block.shape[dim] - width, None, axis...  61.3 us
    ppermute x8, starting transfers between devices, padded_2(): lax.ppermute(lax.slice_in_dim(block, 0, width, axis=dim), axis, backward)  59.5 us
    unnamed x68, local copies, waits for them, and re-layouts  33.1 us
    ppermute x8, waiting for transfers between devices, padded_2(): lax.ppermute(lax.slice_in_dim(block, 0, width, axis=dim), axis, backward)  23.5 us
    dot_general x28, matrix products, contract_rows(): lax.dot_general(left, right, (((0,), (0,)), ((), ())), preferred_element_...  21.6 us
  transfers between devices with their start and end apart: 25, of which 10 were waited for; matrix products, arithmetic and copies ran while one was open for 9% of the time, Pallas kernels for 0%

commit v1 on v0

v1 whole, which is shorter than its diff:
```python
import jax
import jax.numpy as jnp
from jax import lax
from jax.sharding import Mesh, PartitionSpec as P

HEADS = 8
GELU_COEF = 0.7978845608028654
CUBIC_COEF = 0.044715

LON_AXES = ("x", "zh", "core")
LAT_AXES = ("zl", "y")
PLANE = ("x", "core")
SWAP = [(0, 1), (1, 0)]


def gelu_value(pre_act):
    tanh_val = jnp.tanh(GELU_COEF * (pre_act + CUBIC_COEF * pre_act * pre_act * pre_act))
    return 0.5 * pre_act * (1.0 + tanh_val)


def gelu_slope(pre_act):
    tanh_val = jnp.tanh(GELU_COEF * (pre_act + CUBIC_COEF * pre_act * pre_act * pre_act))
    inner_d = GELU_COEF * (1.0 + 3.0 * CUBIC_COEF * pre_act * pre_act)
    return 0.5 * (1.0 + tanh_val) + 0.5 * pre_act * (1.0 - tanh_val * tanh_val) * inner_d


def contract_rows(left, right):
    return lax.dot_general(
        left, right, (((0,), (0,)), ((), ())), preferred_element_type=jnp.float32
    )


def conv_taps(padded, weight, spread, row_count, col_count):
    channels = padded.shape[-1]
    total_sum = jnp.zeros((row_count * col_count, weight.shape[-1]), jnp.float32)
    for row_tap in range(3):
        for col_tap in range(3):
            window = padded[
                row_tap * spread : row_tap * spread + row_count,
                col_tap * spread : col_tap * spread + col_count,
            ]
            total_sum = total_sum + jnp.dot(
                window.reshape(-1, channels),
                weight[row_tap, col_tap],
                preferred_element_type=jnp.float32,
            )
    return total_sum.reshape(row_count, col_count, -1)


def conv_back(padded, weight, spread, row_count, col_count):
    channels = padded.shape[-1]
    total_sum = jnp.zeros((row_count * col_count, weight.shape[-2]), jnp.float32)
    for row_tap in range(3):
        for col_tap in range(3):
            row_at = (2 - row_tap) * spread
            col_at = (2 - col_tap) * spread
            window = padded[row_at : row_at + row_count, col_at : col_at + col_count]
            total_sum = total_sum + jnp.dot(
                window.reshape(-1, channels),
                weight[row_tap, col_tap].T,
                preferred_element_type=jnp.float32,
            )
    return total_sum.reshape(row_count, col_count, -1)


def weight_terms(padded, gradient, spread, row_count, col_count):
    channels = padded.shape[-1]
    flat_grad = gradient.reshape(-1, gradient.shape[-1])
    tap_list = []
    for row_tap in range(3):
        for col_tap in range(3):
            window = padded[
                row_tap * spread : row_tap * spread + row_count,
                col_tap * spread : col_tap * spread + col_count,
            ]
            tap_list.append(contract_rows(window.reshape(-1, channels), flat_grad))
    return jnp.stack(tap_list).reshape(9 * channels, -1)


def exchange_lon(block, width):
    ring = [(i, (i + 1) % 16) for i in range(16)]
    low = lax.ppermute(block[:, -width:], LON_AXES, ring)
    high = lax.ppermute(block[:, :width], LON_AXES, [(b, a) for a, b in ring])
    return low, high


def exchange_lat(bottom, top):
    chain = [(i, i + 1) for i in range(31)]
    low = lax.ppermute(bottom, LAT_AXES, chain)
    high = lax.ppermute(top, LAT_AXES, [(b, a) for a, b in chain])
    return low, high


def inside_rows(lat_at, row_count, width):
    at = lat_at * row_count + jnp.arange(row_count + 2 * width, dtype=jnp.int32) - width
    return ((at >= 0) & (at < 32 * row_count))[:, None, None]


def attend_head(query_h, dout_h, key_h, value_h):
    scale = query_h.shape[-1] ** (-0.5)
    scores = jnp.dot(query_h, key_h.T, preferred_element_type=jnp.float32) * scale
    top_val = jnp.max(scores, axis=1, keepdims=True)
    raised = jnp.exp(scores - top_val)
    probs = raised / jnp.sum(raised, axis=1, keepdims=True)
    probs_low = probs.astype(jnp.bfloat16)
    mixed = jnp.dot(probs_low, value_h, preferred_element_type=jnp.float32).astype(jnp.bfloat16)
    prob_grad = jnp.dot(dout_h, value_h.T, preferred_element_type=jnp.float32)
    delta_sum = jnp.sum(
        dout_h.astype(jnp.float32) * mixed.astype(jnp.float32), axis=1, keepdims=True
    )
    score_grad = (probs * (prob_grad - delta_sum) * scale).astype(jnp.bfloat16)
    query_grad = jnp.dot(score_grad, key_h, preferred_element_type=jnp.float32).astype(jnp.bfloat16)
    key_grad = contract_rows(score_grad, query_h).astype(jnp.bfloat16)
    value_grad = contract_rows(probs_low, dout_h).astype(jnp.bfloat16)
    return (mixed, query_grad, key_grad, value_grad)


def reduce_all(terms):
    rows, channels = terms.shape
    part = rows // 32
    piece = part * channels // 16
    band = lax.all_to_all(
        terms.reshape(32, part, channels), ("x", "y", "core"), 0, 0, tiled=True
    )
    band = band.astype(jnp.float32).sum(0).astype(jnp.bfloat16).reshape(16, piece)
    band = lax.all_to_all(band, ("zh", "zl"), 0, 0, tiled=True)
    band = band.astype(jnp.float32).sum(0).astype(jnp.bfloat16)
    band = lax.all_to_all(
        jnp.broadcast_to(band[None], (16, piece)), ("zh", "zl"), 0, 0, tiled=True
    ).reshape(part, channels)
    return lax.all_to_all(
        jnp.broadcast_to(band[None], (32, part, channels)), ("x", "y", "core"), 0, 0, tiled=True
    ).reshape(rows, channels)


def on_device(
    features, queries, attn_keys, attn_values, cotangent, conv_near, conv_wide, proj_qkv, proj_out
):
    rows, cols, channels = features.shape
    head_width = channels // HEADS
    factor = float(rows * cols * 512) ** (-0.5)
    lat_at = lax.axis_index(LAT_AXES)

    def to_rows(field):
        return lax.all_to_all(field, PLANE, 0, 0, tiled=True)

    def by_head(field):
        return field.reshape(-1, HEADS, head_width).transpose(1, 0, 2)

    def merge_heads(field):
        return field.transpose(1, 0, 2).reshape(-1, channels)

    kv_own = to_rows(jnp.concatenate([attn_keys, attn_values], axis=1))
    kv_far = lax.ppermute(kv_own, "zh", SWAP)
    qc_own = to_rows(jnp.concatenate([queries, cotangent], axis=1))

    low, high = exchange_lon(features, 10)
    cot_low, cot_high = exchange_lon(cotangent, 5)
    feat_x = jnp.concatenate([low, features, high], axis=1)
    cot_x = jnp.concatenate([cot_low, cotangent, cot_high], axis=1)
    low, high = exchange_lat(
        jnp.concatenate([feat_x[-5:], jnp.pad(cot_x[-1:], ((0, 0), (0, 10), (0, 0)))], axis=0),
        jnp.concatenate([feat_x[:5], jnp.pad(cot_x[:1], ((0, 0), (0, 10), (0, 0)))], axis=0),
    )
    feat_x = jnp.concatenate([low[:5], feat_x, high[:5]], axis=0)
    cot_near = jnp.concatenate([low[5:, 4:96], cot_x[:, 4:96], high[5:, 4:96]], axis=0)

    pre_near = conv_taps(feat_x, conv_near, 1, rows + 8, cols + 18)
    hidden_one = (feat_x[1:-1, 1:-1].astype(jnp.float32) + gelu_value(pre_near)).astype(
        jnp.bfloat16
    )
    hidden_one = jnp.where(inside_rows(lat_at, rows, 4), hidden_one, jnp.zeros_like(hidden_one))
    pre_wide = conv_taps(hidden_one, conv_wide, 4, rows, cols + 10)
    hidden_two = (
        hidden_one[4:-4, 9:-9].astype(jnp.float32) + gelu_value(pre_wide[:, 5:-5])
    ).astype(jnp.bfloat16)
    hid_own = to_rows(hidden_two)
    hid_far = lax.ppermute(hid_own, "zh", SWAP)

    row_q = qc_own[:, :cols].reshape(-1, channels)
    row_c = qc_own[:, cols:].reshape(-1, channels)
    row_k = jnp.concatenate([kv_own[:, :cols], kv_far[:, :cols]], axis=0).reshape(-1, channels)
    row_v = jnp.concatenate([kv_own[:, cols:], kv_far[:, cols:]], axis=0).reshape(-1, channels)
    out_grad = jnp.dot(row_c, proj_out.T, preferred_element_type=jnp.float32).astype(jnp.bfloat16)
    mixed, query_grad, key_grad, value_grad = lax.map(
        lambda pieces: attend_head(*pieces),
        (by_head(row_q), by_head(out_grad), by_head(row_k), by_head(row_v)),
    )
    mixed, query_grad = merge_heads(mixed), merge_heads(query_grad)
    key_grad, value_grad = merge_heads(key_grad), merge_heads(value_grad)
    half = rows * cols
    far_kv = jnp.concatenate([key_grad[half:], value_grad[half:]], axis=1)
    far_part = jnp.dot(far_kv, proj_qkv[:, channels:].T, preferred_element_type=jnp.float32)
    from_far = lax.ppermute(far_part.astype(jnp.bfloat16), "zh", SWAP)
    own_qkv = jnp.concatenate([query_grad, key_grad[:half], value_grad[:half]], axis=1)
    own_part = jnp.dot(own_qkv, proj_qkv.T, preferred_element_type=jnp.float32)
    attn_grad = (own_part + from_far.astype(jnp.float32)).astype(jnp.bfloat16)
    attn_grad = lax.all_to_all(
        attn_grad.reshape(rows, cols, channels), PLANE, 0, 0, tiled=True
    )
    out_term = contract_rows(mixed, row_c)
    hid_flat = hid_own.reshape(-1, channels)
    far_flat = hid_far.reshape(-1, channels)
    query_term = contract_rows(hid_flat, query_grad)
    kv_term = contract_rows(hid_flat, own_qkv[:, channels:]) + contract_rows(far_flat, far_kv)

    low, high = exchange_lon(attn_grad, 5)
    attn_x = jnp.concatenate([low, attn_grad, high], axis=1)
    outer_x = cot_x.astype(jnp.float32) + attn_x.astype(jnp.float32)
    wide_x = (outer_x * gelu_slope(pre_wide)).astype(jnp.bfloat16)
    low, high = exchange_lat(
        jnp.concatenate([wide_x[-5:], attn_x[-1:]], axis=0),
        jnp.concatenate([wide_x[:5], attn_x[:1]], axis=0),
    )
    wide_all = jnp.concatenate([low[:5], wide_x, high[:5]], axis=0)
    attn_near = jnp.concatenate([low[5:, 4:96], attn_x[:, 4:96], high[5:, 4:96]], axis=0)
    near_total = (cot_near.astype(jnp.float32) + attn_near.astype(jnp.float32)) + conv_back(
        wide_all, conv_wide, 4, rows + 2, cols + 2
    )
    near_grad = (near_total * gelu_slope(pre_near[3:-3, 8:-8])).astype(jnp.bfloat16)
    near_grad = jnp.where(inside_rows(lat_at, rows, 1), near_grad, jnp.zeros_like(near_grad))
    feature_grad = (
        near_total[1:-1, 1:-1] + conv_back(near_grad, conv_near, 1, rows, cols)
    ).astype(jnp.bfloat16)
    wide_term = weight_terms(hidden_one[:, 5:-5], wide_x[:, 5:-5], 4, rows, cols)
    near_term = weight_terms(feat_x[4:-4, 9:-9], near_grad[1:-1, 1:-1], 1, rows, cols)

    terms = jnp.concatenate(
        [near_term, wide_term, query_term, kv_term[:, :channels], kv_term[:, channels:], out_term]
    )
    sums = reduce_all((terms * factor).astype(jnp.bfloat16)).astype(jnp.float32)
    taps = 9 * channels
    near_sum = sums[:taps].reshape(3, 3, channels, channels)
    wide_sum = sums[taps : 2 * taps].reshape(3, 3, channels, channels)
    qkv_sum = jnp.concatenate(
        [sums[2 * taps + i * channels : 2 * taps + (i + 1) * channels] for i in range(3)], axis=1
    )
    out_sum = sums[2 * taps + 3 * channels :]
    return (feature_grad, near_sum, wide_sum, qkv_sum, out_sum)


def solution(mesh):
    grid = Mesh(mesh.devices.reshape(4, 2, 2, 8, 4), LON_AXES + LAT_AXES)
    field = P(LAT_AXES, LON_AXES, None)
    return jax.shard_map(
        on_device,
        mesh=grid,
        in_specs=(field,) * 5 + (P(),) * 4,
        out_specs=(field, P(), P(), P(), P()),
        check_vma=False,
    )
```

time: 899 us -> 445 us (0.49)
  waiting for transfers between devices: 516 us -> 72.6 us
  starting transfers between devices: 204 us -> 167 us
  matrix products: 68.3 us -> 101 us
  other arithmetic: 14.5 us -> 30.7 us
  between operations: 15.7 us -> 2.17 us
    psum x1 -> x0, waiting for transfers between devices: 455 us -> none  [on_device(): lax.psum((near_term, wide_term, qkv_term, out_term), ('lon', 'lat'))]
    ppermute x16 -> x13, starting transfers between devices: 121 us -> 80.3 us  [the longest x3 36.6 us: exchange_lon(): low = lax.ppermute(block[:, -width:], LON_AXES, ring)]
    unnamed x68 -> x132, local copies, waits for them, and re-layouts: 33.1 us -> 11.5 us
    all_to_all x8, waiting for transfers between devices: 31.4 us -> 52.7 us  [the longest x1 12.2 us: reduce_all(): lax.all_to_all(jnp.broadcast_to(band[None], (32, part, channels)), ('x',...]
    dot_general x28 -> x38, matrix products: 21.6 us -> 36.4 us  [contract_rows(): lax.dot_general(left, right, (((0,), (0,)), ((), ())), preferred_element_...]
    slice x6 -> x25, local copies, waits for them, and re-layouts: 0.08 us -> 13.5 us  [the longest x2 2.11 us: on_device(): high[5:, 4:96]]
    reshape x18, local copies, waits for them, and re-layouts: 5.98 us -> 17.6 us  [conv_taps(): window.reshape(-1, channels)]
    while x4 -> x0, local copies, waits for them, and re-layouts: 11.2 us -> none  [on_device(): lax.map(lambda pieces: attend_head(*pieces), (moved_q, moved_k, moved_v,...]
  transfers between devices with their start and end apart: 25 -> 21, of which waited for: 10 -> 12; matrix products, arithmetic and copies ran while one was open for 9% -> 36% of each run, Pallas kernels for 0% -> 0%
where the time goes in v1:
time: 445 us; the launch traced here: 441 us
  starting transfers between devices  167 us (38%)
  matrix products  101 us (23%)
  waiting for transfers between devices  72.6 us (16%)
  local copies, waits for them, and re-layouts  67.3 us (15%)
  other arithmetic  30.7 us (7%)
    ppermute x3, starting transfers between devices, exchange_lon(): low = lax.ppermute(block[:, -width:], LON_AXES, ring)  36.6 us
    dot_general x38, matrix products, contract_rows(): lax.dot_general(left, right, (((0,), (0,)), ((), ())), preferred_element_...  36.4 us
    all_to_all x1, starting transfers between devices, reduce_all(): lax.all_to_all(terms.reshape(32, part, channels), ('x', 'y', 'core'), 0,...  31.3 us
    all_to_all x3, starting transfers between devices, to_rows(): return lax.all_to_all(field, PLANE, 0, 0, tiled=True)  21.1 us
    all_to_all x1, starting transfers between devices, reduce_all(): band = lax.all_to_all(band, ('zh', 'zl'), 0, 0, tiled=True)  18.2 us
    reshape x18, local copies, waits for them, and re-layouts, conv_taps(): window.reshape(-1, channels)  17.6 us
    ppermute x2, starting transfers between devices, exchange_lat(): low = lax.ppermute(bottom, LAT_AXES, chain)  14.7 us
    dot_general x8, matrix products, attend_head(): jnp.dot(query_h, key_h.T, preferred_element_type=jnp.float32) * scale  12.7 us
  transfers between devices with their start and end apart: 21, of which 12 were waited for; matrix products, arithmetic and copies ran while one was open for 36% of the time, Pallas kernels for 0%

profile of v1, /device:TPU:1, one launch (start us, length us, event | category | flops | bytes accessed | tf_op | source)
XLA Modules:
  0.0 440.6 jit_solution(10576461820316388224)
XLA Ops:
  1.6 16.8 %collective-permute-start = (bf16[8,10,128]{2,1,0:T(8,128)(2,1)S(1)}, bf16[8,10,128]{2,1,0:T(8,128)(2,1)S(1)}, u32[]{:S(2)}, u32[]{:S(2)}) collective-permute-start(bf16[8,10,128]{2,1,0:T(8,128)(2,1)S(1)} %get-tuple-element.172), channel_id=1, source_target_pairs={{0,32},{32,64},{64,96},{96,128},{128,160},{160,192},{192,224},{224... | collective-permute-start | bytes 61448 | tf_op jit(solution)/shard_map/ppermute | solution.py:82
  18.5 1.9 collective-permute-start.1
  21.4 12.5 %collective-permute-start.2 = (bf16[8,5,128]{2,1,0:T(8,128)(2,1)S(1)}, bf16[8,5,128]{2,1,0:T(8,128)(2,1)S(1)}, u32[]{:S(2)}, u32[]{:S(2)}) collective-permute-start(bf16[8,5,128]{2,1,0:T(8,128)(2,1)S(1)} %get-tuple-element.174), channel_id=1, source_target_pairs={{0,32},{32,64},{64,96},{96,128},{128,160},{160,192},{192,224},{224... | collective-permute-start | bytes 30728 | tf_op jit(solution)/shard_map/ppermute | solution.py:82
  33.9 1.9 collective-permute-start.3
  37.6 10.6 %all-to-all-start = ((bf16[8,180,128]{2,1,0:T(8,128)(2,1)}), bf16[8,180,128]{2,1,0:T(8,128)(2,1)}, u32[]{:S(2)}, u32[]{:S(2)}) async-start(bf16[8,180,128]{2,1,0:T(8,128)(2,1)} %pad_maximum_fusion.5), calls=%async_computation | async-start | bytes 753664 | tf_op jit(solution)/shard_map/all_to_all | solution.py:145
  51.6 4.0 collective-permute-start.4
  63.7 1.9 reshape.239
  67.5 1.9 reshape.237
  88.7 5.7 %all-to-all-start.1 = ((bf16[8,180,128]{2,1,0:T(8,128)(2,1)}), bf16[8,180,128]{2,1,0:T(8,128)(2,1)S(1)}, u32[]{:S(2)}, u32[]{:S(2)}) async-start(bf16[8,180,128]{2,1,0:T(8,128)(2,1)} %pad_maximum_fusion.6), calls=%async_computation.1 | async-start | bytes 753664 | tf_op jit(solution)/shard_map/all_to_all | solution.py:145
  96.5 5.9 %all-to-all-done.1 = bf16[8,180,128]{2,1,0:T(8,128)(2,1)S(1)} async-done(((bf16[8,180,128]{2,1,0:T(8,128)(2,1)}), bf16[8,180,128]{2,1,0:T(8,128)(2,1)S(1)}, u32[]{:S(2)}, u32[]{:S(2)}) %all-to-all-start.1) | async-done | bytes 368672 | tf_op jit(solution)/shard_map/all_to_all | solution.py:145
  102.3 4.8 %all-to-all-start.3 = ((bf16[8,90,128]{2,1,0:T(8,128)(2,1)}), bf16[8,90,128]{2,1,0:T(8,128)(2,1)}, u32[]{:S(2)}, u32[]{:S(2)}) async-start(bf16[8,90,128]{2,1,0:T(8,128)(2,1)} %fusion.85), calls=%async_computation.3 | async-start | bytes 393216 | tf_op jit(solution)/shard_map/all_to_all | solution.py:145
  107.1 6.5 %collective-permute-start.6 = (bf16[8,180,128]{2,1,0:T(8,128)(2,1)S(1)}, bf16[8,180,128]{2,1,0:T(8,128)(2,1)}, u32[]{:S(2)}, u32[]{:S(2)}) collective-permute-start(bf16[8,180,128]{2,1,0:T(8,128)(2,1)S(1)} %all-to-all-done.1), channel_id=1, source_target_pairs={{0,64},{64,0},{1,65},{65,1},{2,66},{66,2},{3,67},{67,3},{4,68},{68... | collective-permute-start | bytes 1105928 | tf_op jit(solution)/shard_map/ppermute | solution.py:154
  116.5 7.7 %collective-permute-start.12 = (bf16[8,90,128]{2,1,0:T(8,128)(2,1)}, bf16[8,90,128]{2,1,0:T(8,128)(2,1)}, u32[]{:S(2)}, u32[]{:S(2)}) collective-permute-start(bf16[8,90,128]{2,1,0:T(8,128)(2,1)} %all-to-all-done.3), channel_id=1, source_target_pairs={{0,64},{64,0},{1,65},{65,1},{2,66},{66,2},{3,67},{67,3},{4,68},{68... | collective-permute-start | bytes 552968 | tf_op jit(solution)/shard_map/ppermute | solution.py:178
  124.2 3.9 collective-permute-done.6
  133.9 93.9 %while.16 = (s32[]{:T(128)}, bf16[8,720,16]{1,2,0:T(8,128)(2,1)}, bf16[8,720,16]{1,2,0:T(8,128)(2,1)}, bf16[8,1440,16]{1,2,0:T(8,128)(2,1)}, bf16[8,1440,16]{1,2...) while((s32[]{:T(128)}, bf16[8,720,16]{1,2,0:T(8,128)(2,1)}, ...), condition=%wide.region_4.5_spmd, body=%wide.region_0.4_spmd.sunk | while | flops 213693840 | bytes 36481520 | solution.py:185
  232.4 6.4 %collective-permute-start.7 = (bf16[720,128]{1,0:T(8,128)(2,1)}, bf16[720,128]{1,0:T(8,128)(2,1)}, u32[]{:S(2)}, u32[]{:S(2)}) collective-permute-start(bf16[720,128]{1,0:T(8,128)(2,1)} %convolution_convert_fusion.4), channel_id=1, source_target_pairs={{0,64},{64,0},{1,65},{65,1},{2,66},{66,2},{3,67},{67,3},{4,68},{68... | collective-permute-start | bytes 552968 | tf_op jit(solution)/shard_map/ppermute | solution.py:194
  245.3 2.9 collective-permute-done.7
  250.4 6.4 %all-to-all-start.2 = ((bf16[8,90,128]{2,1,0:T(8,128)(2,1)}), bf16[8,90,128]{2,1,0:T(8,128)(2,1)S(1)}, u32[]{:S(2)}, u32[]{:S(2)}) async-start(bf16[8,90,128]{2,1,0:T(8,128)(2,1)} %reshape.231), calls=%async_computation.2 | async-start | bytes 393216 | tf_op jit(solution)/shard_map/all_to_all | solution.py:198
  258.1 4.6 %all-to-all-done.2 = bf16[8,90,128]{2,1,0:T(8,128)(2,1)S(1)} async-done(((bf16[8,90,128]{2,1,0:T(8,128)(2,1)}), bf16[8,90,128]{2,1,0:T(8,128)(2,1)S(1)}, u32[]{:S(2)}, u32[]{:S(2)}) %all-to-all-start.2) | async-done | bytes 184352 | tf_op jit(solution)/shard_map/all_to_all | solution.py:198
  262.7 7.3 %collective-permute-start.8 = (bf16[8,5,128]{2,1,0:T(8,128)(2,1)S(1)}, bf16[8,5,128]{2,1,0:T(8,128)(2,1)S(1)}, u32[]{:S(2)}, u32[]{:S(2)}) collective-permute-start(bf16[8,5,128]{2,1,0:T(8,128)(2,1)S(1)} %get-tuple-element.170), channel_id=1, source_target_pairs={{0,32},{32,64},{64,96},{96,128},{128,160},{160,192},{192,224},{224... | collective-permute-start | bytes 30728 | tf_op jit(solution)/shard_map/ppermute | solution.py:82
  270.0 1.9 collective-permute-start.9
  272.0 1.9 convolution_add_fusion.32
  273.8 10.1 %collective-permute-done.9 = bf16[8,5,128]{2,1,0:T(8,128)(2,1)S(1)} collective-permute-done((bf16[8,5,128]{2,1,0:T(8,128)(2,1)S(1)}, bf16[8,5,128]{2,1,0:T(8,128)(2,1)S(1)}, u32[]{:S(2)}, u32[]{:S(2)}) %collective-permute-start.9) | collective-permute-done | bytes 10272 | tf_op jit(solution)/shard_map/ppermute | solution.py:83
  286.7 10.7 %collective-permute-start.10 = (bf16[6,100,128]{2,1,0:T(8,128)(2,1)S(1)}, bf16[6,100,128]{2,1,0:T(8,128)(2,1)S(1)}, u32[]{:S(2)}, u32[]{:S(2)}) collective-permute-start(bf16[6,100,128]{2,1,0:T(8,128)(2,1)S(1)} %pad_maximum_fusion.20), channel_id=1, source_target_pairs={{0,1},{1,2},{2,3},{3,4},{4,5},{5,6},{6,7},{7,8},{8,9},{9,10},{10,1... | collective-permute-start | bytes 460808 | tf_op jit(solution)/shard_map/ppermute | solution.py:89
  323.6 31.3 %all-to-all-start.4 = ((bf16[32,88,128]{2,1,0:T(8,128)(2,1)}), bf16[32,88,128]{2,1,0:T(8,128)(2,1)S(1)}, u32[]{:S(2)}, u32[]{:S(2)}) async-start(bf16[32,88,128]{2,1,0:T(8,128)(2,1)} %bitcast.81), calls=%async_computation.4 | async-start | bytes 1441792 | tf_op jit(solution)/shard_map/all_to_all | solution.py:122
  360.4 8.1 %all-to-all-done.4 = bf16[32,88,128]{2,1,0:T(8,128)(2,1)S(1)} async-done(((bf16[32,88,128]{2,1,0:T(8,128)(2,1)}), bf16[32,88,128]{2,1,0:T(8,128)(2,1)S(1)}, u32[]{:S(2)}, u32[]{:S(2)}) %all-to-all-start.4) | async-done | bytes 720928 | tf_op jit(solution)/shard_map/all_to_all | solution.py:122
  370.7 18.2 %all-to-all-start.5 = ((bf16[16,2,352]{2,1,0:T(2,128)(2,1)}), bf16[16,2,352]{2,1,0:T(2,128)(2,1)S(1)}, u32[]{:S(2)}, u32[]{:S(2)}) async-start(bf16[16,2,352]{2,1,0:T(2,128)(2,1)} %reshape.299), calls=%async_computation.5 | async-start | bytes 49152 | tf_op jit(solution)/shard_map/all_to_all | solution.py:126
  389.3 11.2 %all-to-all-done.5 = bf16[16,2,352]{2,1,0:T(2,128)(2,1)S(1)} async-done(((bf16[16,2,352]{2,1,0:T(2,128)(2,1)}), bf16[16,2,352]{2,1,0:T(2,128)(2,1)S(1)}, u32[]{:S(2)}, u32[]{:S(2)}) %all-to-all-start.5) | async-done | bytes 22560 | tf_op jit(solution)/shard_map/all_to_all | solution.py:126
  402.1 3.5 all-to-all-start.6
  406.0 10.8 %all-to-all-done.6 = bf16[16,2,352]{2,1,0:T(2,128)(2,1)S(1)} async-done(((bf16[16,2,352]{2,1,0:T(2,128)(2,1)}), bf16[16,2,352]{2,1,0:T(2,128)(2,1)S(1)}, u32[]{:S(2)}, u32[]{:S(2)}) %all-to-all-start.6) | async-done | bytes 22560 | tf_op jit(solution)/shard_map/all_to_all | solution.py:128
  418.2 6.3 %all-to-all-start.7 = ((bf16[32,88,128]{2,1,0:T(8,128)(2,1)}), bf16[32,88,128]{2,1,0:T(8,128)(2,1)S(1)}, u32[]{:S(2)}, u32[]{:S(2)}) async-start(bf16[32,88,128]{2,1,0:T(8,128)(2,1)} %broadcast_in_dim.60), calls=%async_computation.7 | async-start | bytes 1441792 | tf_op jit(solution)/shard_map/all_to_all | solution.py:131
  425.8 12.2 %all-to-all-done.7 = bf16[32,88,128]{2,1,0:T(8,128)(2,1)S(1)} async-done(((bf16[32,88,128]{2,1,0:T(8,128)(2,1)}), bf16[32,88,128]{2,1,0:T(8,128)(2,1)S(1)}, u32[]{:S(2)}, u32[]{:S(2)}) %all-to-all-start.7) | async-done | bytes 720928 | tf_op jit(solution)/shard_map/all_to_all | solution.py:131
  (392 shorter events, 198.7 us)
Async XLA Ops:
  0.6 112.9 %copy-start = (bf16[128,128]{1,0:T(8,128)(2,1)S(1)}, bf16[128,128]{1,0:T(8,128)(2,1)}, u32[]{:S(2)}) copy-start(bf16[128,128]{1,0:T(8,128)(2,1)} %param.19) | copy-start | bytes 98308
  1.6 47.9 %collective-permute-start = (bf16[8,10,128]{2,1,0:T(8,128)(2,1)S(1)}, bf16[8,10,128]{2,1,0:T(8,128)(2,1)S(1)}, u32[]{:S(2)}, u32[]{:S(2)}) collective-permute-start(bf16[8,10,128]{2,1,0:T(8,128)(2,1)S(1)} %get-tuple-element.172), channel_id=1, source_target_pairs={{0,32},{32,64},{64,96},{96,128},{128,160},{160,192},{192,224},{224... | collective-permute-start | bytes 61448 | tf_op jit(solution)/shard_map/ppermute | solution.py:82
  18.5 31.7 %collective-permute-start.1 = (bf16[8,10,128]{2,1,0:T(8,128)(2,1)S(1)}, bf16[8,10,128]{2,1,0:T(8,128)(2,1)S(1)}, u32[]{:S(2)}, u32[]{:S(2)}) collective-permute-start(bf16[8,10,128]{2,1,0:T(8,128)(2,1)S(1)} %get-tuple-element.173), channel_id=1, source_target_pairs={{32,0},{64,32},{96,64},{128,96},{160,128},{192,160},{224,192},{256... | collective-permute-start | bytes 61448 | tf_op jit(solution)/shard_map/ppermute | solution.py:83
  21.3 34.3 %copy-start.44 = (bf16[8,90,128]{2,0,1:T(8,128)(2,1)S(1)}, bf16[8,90,128]{2,0,1:T(8,128)(2,1)}, u32[]{:S(2)}) copy-start(bf16[8,90,128]{2,0,1:T(8,128)(2,1)} %param.13) | copy-start | bytes 552964
  21.4 26.8 %collective-permute-start.2 = (bf16[8,5,128]{2,1,0:T(8,128)(2,1)S(1)}, bf16[8,5,128]{2,1,0:T(8,128)(2,1)S(1)}, u32[]{:S(2)}, u32[]{:S(2)}) collective-permute-start(bf16[8,5,128]{2,1,0:T(8,128)(2,1)S(1)} %get-tuple-element.174), channel_id=1, source_target_pairs={{0,32},{32,64},{64,96},{96,128},{128,160},{160,192},{192,224},{224... | collective-permute-start | bytes 30728 | tf_op jit(solution)/shard_map/ppermute | solution.py:82
  33.9 14.3 %collective-permute-start.3 = (bf16[8,5,128]{2,1,0:T(8,128)(2,1)S(1)}, bf16[8,5,128]{2,1,0:T(8,128)(2,1)S(1)}, u32[]{:S(2)}, u32[]{:S(2)}) collective-permute-start(bf16[8,5,128]{2,1,0:T(8,128)(2,1)S(1)} %get-tuple-element.175), channel_id=1, source_target_pairs={{32,0},{64,32},{96,64},{128,96},{160,128},{192,160},{224,192},{256... | collective-permute-start | bytes 30728 | tf_op jit(solution)/shard_map/ppermute | solution.py:83
  36.8 19.0 %copy-start.45 = (bf16[8,90,128]{2,0,1:T(8,128)(2,1)S(1)}, bf16[8,90,128]{2,0,1:T(8,128)(2,1)}, u32[]{:S(2)}) copy-start(bf16[8,90,128]{2,0,1:T(8,128)(2,1)} %param.14) | copy-start | bytes 552964
  37.6 51.1 %all-to-all-start = ((bf16[8,180,128]{2,1,0:T(8,128)(2,1)}), bf16[8,180,128]{2,1,0:T(8,128)(2,1)}, u32[]{:S(2)}, u32[]{:S(2)}) async-start(bf16[8,180,128]{2,1,0:T(8,128)(2,1)} %pad_maximum_fusion.5), calls=%async_computation | async-start | bytes 753664 | tf_op jit(solution)/shard_map/all_to_all | solution.py:145
  50.3 7.7 %collective-permute-start.5 = (bf16[6,110,128]{2,1,0:T(8,128)(2,1)S(1)}, bf16[6,110,128]{2,1,0:T(8,128)(2,1)S(1)}, u32[]{:S(2)}, u32[]{:S(2)}) collective-permute-start(bf16[6,110,128]{2,1,0:T(8,128)(2,1)S(1)} %fusion.115), channel_id=1, source_target_pairs={{1,0},{2,1},{3,2},{4,3},{5,4},{6,5},{7,6},{8,7},{9,8},{10,9},{11,1... | collective-permute-start | bytes 506888 | tf_op jit(solution)/shard_map/ppermute | solution.py:90
  51.6 7.3 %collective-permute-start.4 = (bf16[6,110,128]{2,1,0:T(8,128)(2,1)S(1)}, bf16[6,110,128]{2,1,0:T(8,128)(2,1)S(1)}, u32[]{:S(2)}, u32[]{:S(2)}) collective-permute-start(bf16[6,110,128]{2,1,0:T(8,128)(2,1)S(1)} %fusion.114), channel_id=1, source_target_pairs={{0,1},{1,2},{2,3},{3,4},{4,5},{5,6},{6,7},{7,8},{8,9},{9,10},{10,1... | collective-permute-start | bytes 506888 | tf_op jit(solution)/shard_map/ppermute | solution.py:89
  88.7 13.6 %all-to-all-start.1 = ((bf16[8,180,128]{2,1,0:T(8,128)(2,1)}), bf16[8,180,128]{2,1,0:T(8,128)(2,1)S(1)}, u32[]{:S(2)}, u32[]{:S(2)}) async-start(bf16[8,180,128]{2,1,0:T(8,128)(2,1)} %pad_maximum_fusion.6), calls=%async_computation.1 | async-start | bytes 753664 | tf_op jit(solution)/shard_map/all_to_all | solution.py:145
  96.4 34.5 %copy-start.7 = (bf16[720,128]{1,0:T(8,128)(2,1)}, bf16[720,128]{1,0:T(8,128)(2,1)S(1)}, u32[]{:S(2)}) copy-start(bf16[720,128]{1,0:T(8,128)(2,1)S(1)} %reshape.228) | copy-start | bytes 552964
  102.3 14.2 %all-to-all-start.3 = ((bf16[8,90,128]{2,1,0:T(8,128)(2,1)}), bf16[8,90,128]{2,1,0:T(8,128)(2,1)}, u32[]{:S(2)}, u32[]{:S(2)}) async-start(bf16[8,90,128]{2,1,0:T(8,128)(2,1)} %fusion.85), calls=%async_computation.3 | async-start | bytes 393216 | tf_op jit(solution)/shard_map/all_to_all | solution.py:145
  107.1 21.0 %collective-permute-start.6 = (bf16[8,180,128]{2,1,0:T(8,128)(2,1)S(1)}, bf16[8,180,128]{2,1,0:T(8,128)(2,1)}, u32[]{:S(2)}, u32[]{:S(2)}) collective-permute-start(bf16[8,180,128]{2,1,0:T(8,128)(2,1)S(1)} %all-to-all-done.1), channel_id=1, source_target_pairs={{0,64},{64,0},{1,65},{65,1},{2,66},{66,2},{3,67},{67,3},{4,68},{68... | collective-permute-start | bytes 1105928 | tf_op jit(solution)/shard_map/ppermute | solution.py:154
  116.5 127.1 %collective-permute-start.12 = (bf16[8,90,128]{2,1,0:T(8,128)(2,1)}, bf16[8,90,128]{2,1,0:T(8,128)(2,1)}, u32[]{:S(2)}, u32[]{:S(2)}) collective-permute-start(bf16[8,90,128]{2,1,0:T(8,128)(2,1)} %all-to-all-done.3), channel_id=1, source_target_pairs={{0,64},{64,0},{1,65},{65,1},{2,66},{66,2},{3,67},{67,3},{4,68},{68... | collective-permute-start | bytes 552968 | tf_op jit(solution)/shard_map/ppermute | solution.py:178
  133.9 97.5 %copy-start.58 = (bf16[128,384]{1,0:T(8,128)(2,1)S(1)}, bf16[128,384]{1,0:T(8,128)(2,1)}, u32[]{:S(2)}) copy-start(bf16[128,384]{1,0:T(8,128)(2,1)} %param.18) | copy-start | bytes 294916
  229.6 18.6 %copy-start.41 = (bf16[8,720,16]{1,2,0:T(8,128)(2,1)S(1)}, bf16[8,720,16]{1,2,0:T(8,128)(2,1)}, u32[]{:S(2)}) copy-start(bf16[8,720,16]{1,2,0:T(8,128)(2,1)} %get-tuple-element.55) | copy-start | bytes 552964
  232.4 15.8 %collective-permute-start.7 = (bf16[720,128]{1,0:T(8,128)(2,1)}, bf16[720,128]{1,0:T(8,128)(2,1)}, u32[]{:S(2)}, u32[]{:S(2)}) collective-permute-start(bf16[720,128]{1,0:T(8,128)(2,1)} %convolution_convert_fusion.4), channel_id=1, source_target_pairs={{0,64},{64,0},{1,65},{65,1},{2,66},{66,2},{3,67},{67,3},{4,68},{68... | collective-permute-start | bytes 552968 | tf_op jit(solution)/shard_map/ppermute | solution.py:194
  243.6 30.3 %copy-start.29 = (bf16[720,128]{1,0:T(8,128)(2,1)}, bf16[720,128]{1,0:T(8,128)(2,1)S(1)}, u32[]{:S(2)}) copy-start(bf16[720,128]{1,0:T(8,128)(2,1)S(1)} %reshape.274) | copy-start | bytes 552964
  248.2 35.7 %copy-start.55 = (bf16[8,5,128]{2,1,0:T(8,128)(2,1)S(1)}, bf16[8,5,128]{2,1,0:T(8,128)(2,1)}, u32[]{:S(2)}) copy-start(bf16[8,5,128]{2,1,0:T(8,128)(2,1)} %copy-done.54) | copy-start | bytes 30724
  248.2 35.7 %copy-start.57 = (bf16[8,5,128]{2,1,0:T(8,128)(2,1)S(1)}, bf16[8,5,128]{2,1,0:T(8,128)(2,1)}, u32[]{:S(2)}) copy-start(bf16[8,5,128]{2,1,0:T(8,128)(2,1)} %copy-done.56) | copy-start | bytes 30724
  250.4 12.3 %all-to-all-start.2 = ((bf16[8,90,128]{2,1,0:T(8,128)(2,1)}), bf16[8,90,128]{2,1,0:T(8,128)(2,1)S(1)}, u32[]{:S(2)}, u32[]{:S(2)}) async-start(bf16[8,90,128]{2,1,0:T(8,128)(2,1)} %reshape.231), calls=%async_computation.2 | async-start | bytes 393216 | tf_op jit(solution)/shard_map/all_to_all | solution.py:198
  262.7 11.1 %collective-permute-start.8 = (bf16[8,5,128]{2,1,0:T(8,128)(2,1)S(1)}, bf16[8,5,128]{2,1,0:T(8,128)(2,1)S(1)}, u32[]{:S(2)}, u32[]{:S(2)}) collective-permute-start(bf16[8,5,128]{2,1,0:T(8,128)(2,1)S(1)} %get-tuple-element.170), channel_id=1, source_target_pairs={{0,32},{32,64},{64,96},{96,128},{128,160},{160,192},{192,224},{224... | collective-permute-start | bytes 30728 | tf_op jit(solution)/shard_map/ppermute | solution.py:82
  270.0 13.9 %collective-permute-start.9 = (bf16[8,5,128]{2,1,0:T(8,128)(2,1)S(1)}, bf16[8,5,128]{2,1,0:T(8,128)(2,1)S(1)}, u32[]{:S(2)}, u32[]{:S(2)}) collective-permute-start(bf16[8,5,128]{2,1,0:T(8,128)(2,1)S(1)} %get-tuple-element.171), channel_id=1, source_target_pairs={{32,0},{64,32},{96,64},{128,96},{160,128},{192,160},{224,192},{256... | collective-permute-start | bytes 30728 | tf_op jit(solution)/shard_map/ppermute | solution.py:83
  285.4 14.2 %collective-permute-start.11 = (bf16[6,100,128]{2,1,0:T(8,128)(2,1)S(1)}, bf16[6,100,128]{2,1,0:T(8,128)(2,1)S(1)}, u32[]{:S(2)}, u32[]{:S(2)}) collective-permute-start(bf16[6,100,128]{2,1,0:T(8,128)(2,1)S(1)} %pad_maximum_fusion.21), channel_id=1, source_target_pairs={{1,0},{2,1},{3,2},{4,3},{5,4},{6,5},{7,6},{8,7},{9,8},{10,9},{11,1... | collective-permute-start | bytes 460808 | tf_op jit(solution)/shard_map/ppermute | solution.py:90
  286.7 13.7 %collective-permute-start.10 = (bf16[6,100,128]{2,1,0:T(8,128)(2,1)S(1)}, bf16[6,100,128]{2,1,0:T(8,128)(2,1)S(1)}, u32[]{:S(2)}, u32[]{:S(2)}) collective-permute-start(bf16[6,100,128]{2,1,0:T(8,128)(2,1)S(1)} %pad_maximum_fusion.20), channel_id=1, source_target_pairs={{0,1},{1,2},{2,3},{3,4},{4,5},{5,6},{6,7},{7,8},{8,9},{9,10},{10,1... | collective-permute-start | bytes 460808 | tf_op jit(solution)/shard_map/ppermute | solution.py:89
  323.6 33.7 %copy-start.16 = (bf16[3,3,128,128]{3,2,1,0:T(8,128)(2,1)S(1)}, bf16[3,3,128,128]{3,2,1,0:T(8,128)(2,1)}, u32[]{:S(2)}) copy-start(bf16[3,3,128,128]{3,2,1,0:T(8,128)(2,1)} %param.16) | copy-start | bytes 884740
  323.6 44.9 %all-to-all-start.4 = ((bf16[32,88,128]{2,1,0:T(8,128)(2,1)}), bf16[32,88,128]{2,1,0:T(8,128)(2,1)S(1)}, u32[]{:S(2)}, u32[]{:S(2)}) async-start(bf16[32,88,128]{2,1,0:T(8,128)(2,1)} %bitcast.81), calls=%async_computation.4 | async-start | bytes 1441792 | tf_op jit(solution)/shard_map/all_to_all | solution.py:122
  357.5 31.4 %copy-start.31 = (bf16[720,128]{1,0:T(8,128)(2,1)S(1)}, bf16[720,128]{1,0:T(8,128)(2,1)}, u32[]{:S(2)}) copy-start(bf16[720,128]{1,0:T(8,128)(2,1)} %reshape.267) | copy-start | bytes 552964
  370.7 29.7 %all-to-all-start.5 = ((bf16[16,2,352]{2,1,0:T(2,128)(2,1)}), bf16[16,2,352]{2,1,0:T(2,128)(2,1)S(1)}, u32[]{:S(2)}, u32[]{:S(2)}) async-start(bf16[16,2,352]{2,1,0:T(2,128)(2,1)} %reshape.299), calls=%async_computation.5 | async-start | bytes 49152 | tf_op jit(solution)/shard_map/all_to_all | solution.py:126
  402.1 14.7 %all-to-all-start.6 = ((bf16[16,2,352]{2,1,0:T(2,128)(2,1)}), bf16[16,2,352]{2,1,0:T(2,128)(2,1)S(1)}, u32[]{:S(2)}, u32[]{:S(2)}) async-start(bf16[16,2,352]{2,1,0:T(2,128)(2,1)} %reshape.301), calls=%async_computation.6 | async-start | bytes 49152 | tf_op jit(solution)/shard_map/all_to_all | solution.py:128
  418.2 19.8 %all-to-all-start.7 = ((bf16[32,88,128]{2,1,0:T(8,128)(2,1)}), bf16[32,88,128]{2,1,0:T(8,128)(2,1)S(1)}, u32[]{:S(2)}, u32[]{:S(2)}) async-start(bf16[32,88,128]{2,1,0:T(8,128)(2,1)} %broadcast_in_dim.60), calls=%async_computation.7 | async-start | bytes 1441792 | tf_op jit(solution)/shard_map/all_to_all | solution.py:131
  (48 other events, 172.8 us)

commit v2 on v1

v2 whole, which is shorter than its diff:
```python
import functools

import jax
import jax.numpy as jnp
from jax import lax
from jax.experimental import pallas as pl
from jax.experimental.pallas import tpu as pltpu
from jax.sharding import Mesh, PartitionSpec as P

HEADS = 8
COLS = 90
GROWN = 96
EDGE = 5
GELU_COEF = 0.7978845608028654
CUBIC_COEF = 0.044715

LON_AXES = ("x", "zh", "core")
LAT_AXES = ("zl", "y")
PLANE = ("x", "core")
SWAP = [(0, 1), (1, 0)]


def gelu_value(pre_act):
    tanh_val = jnp.tanh(GELU_COEF * (pre_act + CUBIC_COEF * pre_act * pre_act * pre_act))
    return 0.5 * pre_act * (1.0 + tanh_val)


def gelu_slope(pre_act):
    tanh_val = jnp.tanh(GELU_COEF * (pre_act + CUBIC_COEF * pre_act * pre_act * pre_act))
    inner_d = GELU_COEF * (1.0 + 3.0 * CUBIC_COEF * pre_act * pre_act)
    return 0.5 * (1.0 + tanh_val) + 0.5 * pre_act * (1.0 - tanh_val * tanh_val) * inner_d


def contract_rows(left, right):
    return lax.dot_general(
        left, right, (((0,), (0,)), ((), ())), preferred_element_type=jnp.float32
    )


def exchange_lon(left, right):
    at_zero = lax.axis_index("core") == 0
    inner = lax.ppermute(jnp.where(at_zero, right, left), "core", SWAP)
    pairs = [(i, (i + 1) % 16 if i % 2 else (i - 1) % 16) for i in range(16)]
    outer = lax.ppermute(jnp.where(at_zero, left, right), LON_AXES, pairs)
    return jnp.where(at_zero, outer, inner), jnp.where(at_zero, inner, outer)


def exchange_lat(bottom, top):
    chain = [(i, i + 1) for i in range(31)]
    low = lax.ppermute(bottom, LAT_AXES, chain)
    high = lax.ppermute(top, LAT_AXES, [(b, a) for a, b in chain])
    return low, high


def attend_rows(qc_ref, kv_ref, far_ref, proj_ref, qkv_ref, part_ref, away_ref, send_ref,
                term_ref, own_ref, farg_ref,
                out_s, keep_s, grad_s, key_s, value_s, query_s, mixed_s):
    blocks = qc_ref.shape[0]
    wide = qc_ref.shape[1] // 2
    rows = blocks * wide
    cols = 2 * rows
    channels = qc_ref.shape[2]
    width = channels // HEADS
    chunk = 256
    low = jnp.bfloat16

    def rows_of(ref, at):
        return ref[:, at : at + wide, :].reshape(rows, channels)

    out_s[...] = lax.dot_general(
        rows_of(qc_ref, wide), proj_ref[...], (((1,), (1,)), ((), ())),
        preferred_element_type=jnp.float32,
    ).astype(low)
    for ref in (key_s, value_s, query_s, mixed_s):
        ref[...] = jnp.zeros_like(ref)
    lane_k = lax.broadcasted_iota(jnp.int32, (cols, channels), 1)
    filler = lax.broadcasted_iota(jnp.int32, (cols, channels), 0) % wide >= COLS
    lane_q = lax.broadcasted_iota(jnp.int32, (chunk, channels), 1)

    def one_head(head, carry):
        first = (head * width + width) % channels
        here_k = lane_k // width == head
        here_q = lane_q // width == head
        keys = jnp.concatenate([rows_of(kv_ref, 0), rows_of(far_ref, 0)], axis=0)
        values = jnp.concatenate([rows_of(kv_ref, wide), rows_of(far_ref, wide)], axis=0)
        spare = jnp.where((lane_k == first) & filler, -1e30, 0.0)
        keys_h = jnp.where(here_k, keys.astype(jnp.float32), spare).astype(low)
        ones = jnp.where((lane_k == first) | (lane_k == first + 1), 1.0, 0.0)
        values_h = jnp.where(here_k, values.astype(jnp.float32), ones).astype(low)
        query_n, dout_n = [], []
        for i in range(rows // chunk):
            at = i * chunk
            query = rows_of(qc_ref, 0)[at : at + chunk].astype(jnp.float32) * 0.25
            query_h = jnp.where(here_q, query, jnp.where(lane_q == first, 1.0, 0.0)).astype(low)
            dout = jnp.where(here_q, out_s[at : at + chunk, :].astype(jnp.float32), 0.0)
            scores = lax.dot_general(
                query_h, keys_h, (((1,), (1,)), ((), ())), preferred_element_type=jnp.float32
            )
            top = jnp.max(scores, axis=1, keepdims=True)
            raised = jnp.exp(scores - top).astype(low)
            keep_s[at : at + chunk, :] = raised
            mixed = jnp.dot(raised, values_h, preferred_element_type=jnp.float32)
            total = jnp.sum(jnp.where(lane_q == first, mixed, 0.0), axis=1, keepdims=True)
            share = 1.0 / total
            mixed = jnp.where(here_q, mixed * share, 0.0)
            mixed_s[at : at + chunk, :] += mixed
            delta = jnp.sum(dout * mixed, axis=1, keepdims=True)
            high = delta.astype(low).astype(jnp.float32)
            dout_x = jnp.where(
                lane_q == first, -high, jnp.where(lane_q == first + 1, high - delta, dout)
            ).astype(low)
            prob_grad = lax.dot_general(
                dout_x, values_h, (((1,), (1,)), ((), ())), preferred_element_type=jnp.float32
            )
            score_grad = raised * prob_grad.astype(low)
            grad_s[at : at + chunk, :] = score_grad
            query_s[at : at + chunk, :] += (
                jnp.dot(score_grad, keys_h, preferred_element_type=jnp.float32) * (0.25 * share)
            )
            query_n.append((jnp.where(here_q, query, 0.0) * share).astype(low))
            dout_n.append((dout * share).astype(low))
        key_s[...] += lax.dot_general(
            grad_s[...], jnp.concatenate(query_n, axis=0), (((0,), (0,)), ((), ())),
            preferred_element_type=jnp.float32,
        )
        value_s[...] += lax.dot_general(
            keep_s[...], jnp.concatenate(dout_n, axis=0), (((0,), (0,)), ((), ())),
            preferred_element_type=jnp.float32,
        )
        return carry

    lax.fori_loop(0, HEADS, one_head, 0)
    own_ref[:, :channels] = query_s[...].astype(low)
    own_ref[:, channels : 2 * channels] = key_s[:rows, :].astype(low)
    own_ref[:, 2 * channels :] = value_s[:rows, :].astype(low)
    farg_ref[:, :channels] = key_s[rows:, :].astype(low)
    farg_ref[:, channels:] = value_s[rows:, :].astype(low)
    own_part = lax.dot_general(
        own_ref[...], qkv_ref[...], (((1,), (1,)), ((), ())), preferred_element_type=jnp.float32
    )
    far_part = lax.dot_general(
        farg_ref[...], qkv_ref[:, channels:], (((1,), (1,)), ((), ())),
        preferred_element_type=jnp.float32,
    )
    part_ref[...] = own_part.reshape(blocks, wide, channels)
    away_ref[...] = far_part.reshape(blocks, wide, channels)
    query_s[...] = far_part
    for block in range(blocks):
        edge = 0 if block % 2 == 0 else COLS - EDGE
        query_s[block * wide + COLS : block * wide + COLS + EDGE, :] = part_ref[
            block, edge : edge + EDGE, :
        ]
    send_ref[...] = query_s[...].astype(low).reshape(blocks, wide, channels)
    term_ref[...] = lax.dot_general(
        mixed_s[...].astype(low), rows_of(qc_ref, wide), (((0,), (0,)), ((), ())),
        preferred_element_type=jnp.float32,
    )


def attention(qc_own, kv_own, kv_far, proj_out, proj_qkv):
    blocks, double, channels = qc_own.shape
    wide = double // 2
    rows = blocks * wide
    low = jnp.bfloat16
    shapes = [
        ((blocks, wide, channels), jnp.float32),
        ((blocks, wide, channels), jnp.float32),
        ((blocks, wide, channels), low),
        ((channels, channels), jnp.float32),
        ((rows, 3 * channels), low),
        ((rows, 2 * channels), low),
    ]
    return pl.pallas_call(
        attend_rows,
        out_shape=[jax.ShapeDtypeStruct(s, t) for s, t in shapes],
        in_specs=[pl.BlockSpec(memory_space=pltpu.VMEM)] * 5,
        out_specs=[pl.BlockSpec(memory_space=pltpu.VMEM)] * 6,
        scratch_shapes=[
            pltpu.VMEM((rows, channels), low),
            pltpu.VMEM((rows, 2 * rows), low),
            pltpu.VMEM((rows, 2 * rows), low),
            pltpu.VMEM((2 * rows, channels), jnp.float32),
            pltpu.VMEM((2 * rows, channels), jnp.float32),
            pltpu.VMEM((rows, channels), jnp.float32),
            pltpu.VMEM((rows, channels), jnp.float32),
        ],
        compiler_params=pltpu.CompilerParams(vmem_limit_bytes=48 * 1024 * 1024),
        cost_estimate=pl.CostEstimate(
            flops=12 * rows * 2 * rows * channels * HEADS,
            bytes_accessed=16 * rows * channels,
            transcendentals=HEADS * rows * 2 * rows,
        ),
        name="attend_rows",
    )(qc_own, kv_own, kv_far, proj_out, proj_qkv)


def row_inside(lat_ref, shape, width):
    at = lat_ref[0] * 8 + lax.broadcasted_iota(jnp.int32, shape, 0) - width
    return (at >= 0) & (at < 256)


def three(ref, starts, count):
    return jnp.concatenate(
        [ref[:, at : at + count, :].astype(jnp.bfloat16) for at in starts], axis=2
    )


def forward_block(lat_ref, feat_ref, near_ref, wide_ref, two_ref, one_ref, nslope_ref, wslope_ref,
                  feat_s, one_s, wide_s):
    channels = feat_ref.shape[2]
    low = jnp.bfloat16
    cols = 112
    feat_s[...] = feat_ref[...].astype(jnp.float32)
    feat_3 = three(feat_s, (0, 1, 2), cols)
    total = jnp.zeros((16 * cols, channels), jnp.float32)
    for tap in range(3):
        weight = near_ref[tap].reshape(3 * channels, channels)
        total += jnp.dot(
            feat_3[tap : tap + 16].reshape(16 * cols, 3 * channels), weight,
            preferred_element_type=jnp.float32,
        )
    pre_near = total.reshape(16, cols, channels)
    nslope_ref[...] = gelu_slope(pre_near[3:13])
    one = (feat_s[1:17, 1 : 1 + cols, :] + gelu_value(pre_near)).astype(low)
    one = jnp.where(row_inside(lat_ref, one.shape, 4), one.astype(jnp.float32), 0.0)
    one_ref[...] = one.astype(low)
    one_s[...] = jnp.zeros_like(one_s)
    one_s[:, :cols, :] = one
    one_3 = three(one_s, (0, 4, 8), cols)
    total = jnp.zeros((8 * cols, channels), jnp.float32)
    for tap in range(3):
        weight = wide_ref[tap].reshape(3 * channels, channels)
        total += jnp.dot(
            one_3[4 * tap : 4 * tap + 8].reshape(8 * cols, 3 * channels), weight,
            preferred_element_type=jnp.float32,
        )
    pre_wide = total.reshape(8, cols, channels)
    wslope_ref[...] = gelu_slope(pre_wide)
    wide_s[...] = gelu_value(pre_wide)
    two = one_s[4:12, 9 : 9 + GROWN, :] + wide_s[:, EDGE : EDGE + GROWN, :]
    valid = lax.broadcasted_iota(jnp.int32, two.shape, 1) < COLS
    two_ref[...] = jnp.where(valid, two, 0.0).astype(low)


def forward(lat_at, feat_x, conv_near, conv_wide):
    channels = feat_x.shape[2]
    shapes = [
        ((8, GROWN, channels), jnp.bfloat16),
        ((16, 112, channels), jnp.bfloat16),
        ((10, 112, channels), jnp.float32),
        ((8, 112, channels), jnp.float32),
    ]
    return pl.pallas_call(
        forward_block,
        out_shape=[jax.ShapeDtypeStruct(s, t) for s, t in shapes],
        in_specs=[pl.BlockSpec(memory_space=pltpu.SMEM)]
        + [pl.BlockSpec(memory_space=pltpu.VMEM)] * 3,
        out_specs=[pl.BlockSpec(memory_space=pltpu.VMEM)] * 4,
        scratch_shapes=[
            pltpu.VMEM((18, 128, channels), jnp.float32),
            pltpu.VMEM((16, 128, channels), jnp.float32),
            pltpu.VMEM((8, 112, channels), jnp.float32),
        ],
        compiler_params=pltpu.CompilerParams(vmem_limit_bytes=40 * 1024 * 1024),
        cost_estimate=pl.CostEstimate(
            flops=6 * 10**9, bytes_accessed=4 * 10**6, transcendentals=2 * 10**5
        ),
        name="forward_block",
    )(lat_at, feat_x, conv_near, conv_wide)


def backward_block(lat_ref, wide_ref, attn_ref, cot_ref, nslope_ref, one_ref, feat_ref, near_ref,
                   dil_ref, out_ref, term_ref, wide_s, outer_s, slope_s, one_s, feat_s, total_s,
                   near_s, *, factor):
    channels = wide_ref.shape[2]
    low = jnp.bfloat16
    cols = GROWN

    def transposed(ref, tap):
        return jnp.concatenate([ref[tap, i] for i in range(3)], axis=1)

    wide_s[...] = wide_ref[...].astype(jnp.float32)
    outer_s[...] = cot_ref[...].astype(jnp.float32) + attn_ref[...].astype(jnp.float32)
    slope_s[...] = nslope_ref[...]
    one_s[...] = one_ref[...].astype(jnp.float32)
    feat_s[...] = feat_ref[...].astype(jnp.float32)
    wide_3 = three(wide_s, (8, 4, 0), cols)
    total = jnp.zeros((10 * cols, channels), jnp.float32)
    for tap in range(3):
        at = 8 - 4 * tap
        total += lax.dot_general(
            wide_3[at : at + 10].reshape(10 * cols, 3 * channels), transposed(dil_ref, tap),
            (((1,), (1,)), ((), ())), preferred_element_type=jnp.float32,
        )
    near_total = total.reshape(10, cols, channels) + outer_s[:, 4 : 4 + cols, :]
    near_grad = (near_total * slope_s[:, 8 : 8 + cols, :]).astype(low).astype(jnp.float32)
    near_grad = jnp.where(row_inside(lat_ref, near_grad.shape, 1), near_grad, 0.0)
    for ref, value in ((total_s, near_total), (near_s, near_grad)):
        ref[...] = jnp.zeros_like(ref)
        ref[:, :cols, :] = value
    near_3 = three(near_s, (2, 1, 0), cols)
    total = jnp.zeros((8 * cols, channels), jnp.float32)
    for tap in range(3):
        at = 2 - tap
        total += lax.dot_general(
            near_3[at : at + 8].reshape(8 * cols, 3 * channels), transposed(near_ref, tap),
            (((1,), (1,)), ((), ())), preferred_element_type=jnp.float32,
        )
    feature = (total.reshape(8, cols, channels) + total_s[1:9, 1 : 1 + cols, :]).astype(low)
    out_ref[...] = feature[:, :COLS, :]

    valid = lax.broadcasted_iota(jnp.int32, (8, cols, channels), 1) < COLS
    own_near = jnp.where(valid, near_s[1:9, 1 : 1 + cols, :], 0.0)
    own_near = own_near.astype(low).reshape(8 * cols, channels)
    own_wide = jnp.where(valid, wide_s[5:13, EDGE : EDGE + cols, :], 0.0)
    own_wide = own_wide.astype(low).reshape(8 * cols, channels)
    feat_3 = three(feat_s, (9, 10, 11), cols)
    one_3 = three(one_s, (5, 9, 13), cols)
    long = 3 * channels
    for tap in range(3):
        for left, right, at in (
            (feat_3[4 + tap : 12 + tap], own_near, tap * long),
            (one_3[4 * tap : 4 * tap + 8], own_wide, (3 + tap) * long),
        ):
            term = contract_rows(left.reshape(8 * cols, long), right)
            term_ref[at : at + long, :] = (term * factor).astype(low)


def backward(lat_at, wide_all, attn_near, cot_near, near_slope, hidden_one, feat_x, conv_near,
             conv_wide, factor):
    channels = feat_x.shape[2]
    low = jnp.bfloat16
    shapes = [((8, COLS, channels), low), ((18 * channels, channels), low)]
    grown = [(18, 112), (10, 112), (10, 112), (16, 112), (18, 128), (10, 112), (10, 112)]
    return pl.pallas_call(
        functools.partial(backward_block, factor=factor),
        out_shape=[jax.ShapeDtypeStruct(s, t) for s, t in shapes],
        in_specs=[pl.BlockSpec(memory_space=pltpu.SMEM)]
        + [pl.BlockSpec(memory_space=pltpu.VMEM)] * 8,
        out_specs=[pl.BlockSpec(memory_space=pltpu.VMEM)] * 2,
        scratch_shapes=[pltpu.VMEM(g + (channels,), jnp.float32) for g in grown],
        compiler_params=pltpu.CompilerParams(vmem_limit_bytes=44 * 1024 * 1024),
        cost_estimate=pl.CostEstimate(
            flops=6 * 10**9, bytes_accessed=4 * 10**6, transcendentals=0
        ),
        name="backward_block",
    )(lat_at, wide_all, attn_near, cot_near, near_slope, hidden_one, feat_x, conv_near, conv_wide)


def reduce_all(terms):
    rows, channels = terms.shape
    part = rows // 32
    piece = part * channels // 16
    band = lax.all_to_all(
        terms.reshape(32, part, channels), ("x", "y", "core"), 0, 0, tiled=True
    )
    band = band.astype(jnp.float32).sum(0).astype(jnp.bfloat16).reshape(16, piece)
    band = lax.all_to_all(band, ("zh", "zl"), 0, 0, tiled=True)
    band = band.astype(jnp.float32).sum(0).astype(jnp.bfloat16)
    band = lax.all_to_all(
        jnp.broadcast_to(band[None], (16, piece)), ("zh", "zl"), 0, 0, tiled=True
    ).reshape(part, channels)
    return lax.all_to_all(
        jnp.broadcast_to(band[None], (32, part, channels)), ("x", "y", "core"), 0, 0, tiled=True
    ).reshape(rows, channels)


def on_device(
    features, queries, attn_keys, attn_values, cotangent, conv_near, conv_wide, proj_qkv, proj_out
):
    rows, cols, channels = features.shape
    factor = float(rows * cols * 512) ** (-0.5)
    lat_at = lax.axis_index(LAT_AXES).astype(jnp.int32).reshape(1)
    half_at = lax.axis_index("zh")

    def to_rows(*fields):
        grown = [jnp.pad(f, ((0, 0), (0, GROWN - f.shape[1]), (0, 0))) for f in fields]
        return lax.all_to_all(jnp.concatenate(grown, axis=1), PLANE, 0, 0, tiled=True)

    kv_own = to_rows(attn_keys, attn_values)
    kv_far = lax.ppermute(kv_own, "zh", SWAP)

    features, cotangent, kv_own = lax.optimization_barrier((features, cotangent, kv_own))
    blank = jnp.zeros((rows, 1, channels), features.dtype)
    low, high = exchange_lon(
        jnp.concatenate([features[:, :10], cotangent[:, :EDGE], blank], axis=1),
        jnp.concatenate([features[:, -10:], cotangent[:, -EDGE:], blank], axis=1),
    )
    qc_own = to_rows(queries, cotangent)
    feat_x = jnp.concatenate(
        [low[:, :10], features, high[:, :10], jnp.zeros((rows, 18, channels), features.dtype)],
        axis=1,
    )
    cot_x = jnp.concatenate(
        [low[:, 10:15], cotangent, high[:, 10:15], jnp.zeros((rows, 28, channels), features.dtype)],
        axis=1,
    )
    low, high = exchange_lat(
        jnp.concatenate([feat_x[-5:], cot_x[-1:]], axis=0),
        jnp.concatenate([feat_x[:5], cot_x[:1]], axis=0),
    )
    feat_x = jnp.concatenate([low[:5], feat_x, high[:5]], axis=0)
    cot_near = jnp.concatenate([low[5:], cot_x, high[5:]], axis=0)[:, :112]

    feat_x, kv_far = lax.optimization_barrier((feat_x, kv_far))
    hidden_two, hidden_one, near_slope, wide_slope = forward(lat_at, feat_x, conv_near, conv_wide)
    hid_own = to_rows(hidden_two)
    hid_far = lax.ppermute(hid_own, "zh", SWAP)

    own_part, far_part, sent, out_term, own_qkv, far_kv = attention(
        qc_own, kv_own, kv_far, proj_out, proj_qkv
    )
    from_far = lax.ppermute(sent, "zh", SWAP)
    whole = (own_part + from_far.astype(jnp.float32)).astype(jnp.bfloat16)
    whole = whole.reshape(4, 2, GROWN, channels)
    away = far_part.reshape(4, 2, GROWN, channels)
    edge = from_far.reshape(4, 2, GROWN, channels)[:, :, COLS : COLS + EDGE].astype(jnp.float32)
    edge_low = (edge[:, 0] + away[:, 0, :EDGE]).astype(jnp.bfloat16)
    edge_high = (edge[:, 1] + away[:, 1, COLS - EDGE : COLS]).astype(jnp.bfloat16)
    left = jnp.where(half_at == 1, edge_high, jnp.roll(edge_high, 1, axis=0))
    right = jnp.where(half_at == 0, edge_low, jnp.roll(edge_low, -1, axis=0))
    left = jnp.stack([left, whole[:, 0, COLS - EDGE : COLS]], axis=1)
    right = jnp.stack([whole[:, 1, :EDGE], right], axis=1)
    blank = jnp.zeros((4, 2, 12, channels), jnp.bfloat16)
    attn_x = jnp.concatenate([left, whole[:, :, :COLS], right, blank], axis=2)
    attn_x = lax.all_to_all(attn_x.reshape(8, 112, channels), PLANE, 0, 0, tiled=True)
    hid_flat = hid_own.reshape(-1, channels)
    far_flat = hid_far.reshape(-1, channels)
    query_term = contract_rows(hid_flat, own_qkv[:, :channels])
    kv_term = contract_rows(hid_flat, own_qkv[:, channels:]) + contract_rows(far_flat, far_kv)

    outer_x = cot_x[:, :112].astype(jnp.float32) + attn_x.astype(jnp.float32)
    wide_x = (outer_x * wide_slope).astype(jnp.bfloat16)
    low, high = exchange_lat(
        jnp.concatenate([wide_x[-5:], attn_x[-1:]], axis=0),
        jnp.concatenate([wide_x[:5], attn_x[:1]], axis=0),
    )
    wide_all = jnp.concatenate([low[:5], wide_x, high[:5]], axis=0)
    attn_near = jnp.concatenate([low[5:], attn_x, high[5:]], axis=0)
    feature_grad, conv_terms = backward(
        lat_at, wide_all, attn_near, cot_near, near_slope, hidden_one, feat_x, conv_near,
        conv_wide, factor,
    )

    others = jnp.concatenate([query_term, kv_term[:, :channels], kv_term[:, channels:], out_term])
    terms = jnp.concatenate([conv_terms, (others * factor).astype(jnp.bfloat16)])
    sums = reduce_all(terms).astype(jnp.float32)
    taps = 9 * channels
    near_sum = sums[:taps].reshape(3, 3, channels, channels)
    wide_sum = sums[taps : 2 * taps].reshape(3, 3, channels, channels)
    qkv_sum = jnp.concatenate(
        [sums[2 * taps + i * channels : 2 * taps + (i + 1) * channels] for i in range(3)], axis=1
    )
    out_sum = sums[2 * taps + 3 * channels :]
    return (feature_grad, near_sum, wide_sum, qkv_sum, out_sum)


def solution(mesh):
    grid = Mesh(mesh.devices.reshape(4, 2, 2, 8, 4), LON_AXES + LAT_AXES)
    field = P(LAT_AXES, LON_AXES, None)
    return jax.shard_map(
        on_device,
        mesh=grid,
        in_specs=(field,) * 5 + (P(),) * 4,
        out_specs=(field, P(), P(), P(), P()),
        check_vma=False,
    )
```

time: 445 us -> 289 us (0.65)
  matrix products: 101 us -> 3.56 us
  blocking collectives: 0 us -> 90.3 us
  starting transfers between devices: 167 us -> 79.2 us
  local copies, waits for them, and re-layouts: 67.3 us -> 11.9 us
  Pallas kernels: 0 us -> 49.4 us
  waiting for transfers between devices: 72.6 us -> 44 us
  other arithmetic: 30.7 us -> 8.45 us
    all_to_all x0 -> x3, blocking collectives: none -> 90.3 us  [the longest x1 48.7 us: reduce_all(): lax.all_to_all(terms.reshape(32, part, channels), ('x', 'y', 'core'), 0,...]
    dot_general x71 -> x0, matrix products: 64.4 us -> none  [the longest x8 12.7 us: attend_head(): jnp.dot(query_h, key_h.T, preferred_element_type=jnp.float32) * scale]
    pallas_call x0 -> x3, Pallas kernels: none -> 49.4 us  [the longest x1 43.9 us: attention(): pl.pallas_call(attend_rows, out_shape=[jax.ShapeDtypeStruct(s, t) for s,...]
    all_to_all x7 -> x4, starting transfers between devices: 80.5 us -> 33.2 us  [the longest x3 27.1 us: to_rows(): lax.all_to_all(jnp.concatenate(grown, axis=1), PLANE, 0, 0, tiled=True)]
    ppermute x7 -> x3, starting transfers between devices: 48.8 us -> 15.8 us  [the longest x1 11.7 us: exchange_lon(): outer = lax.ppermute(jnp.where(at_zero, left, right), LON_AXES, pairs)]
    dot_general x38 -> x3, matrix products: 36.4 us -> 3.56 us  [contract_rows(): lax.dot_general(left, right, (((0,), (0,)), ((), ())), preferred_element_...]
    reshape x44 -> x0, local copies, waits for them, and re-layouts: 31.9 us -> none  [the longest x18 17.6 us: conv_taps(): window.reshape(-1, channels)]
    all_to_all x7 -> x4, waiting for transfers between devices: 40.5 us -> 13 us  [the longest x3 8.03 us: to_rows(): lax.all_to_all(jnp.concatenate(grown, axis=1), PLANE, 0, 0, tiled=True)]
  transfers between devices with their start and end apart: 21 -> 14, of which waited for: 12 -> 8; matrix products, arithmetic and copies ran while one was open for 36% -> 3% of each run, Pallas kernels for 0% -> 16%
where the time goes in v2:
time: 289 us; the launch traced here: 288 us
  blocking collectives  90.3 us (31%)
  starting transfers between devices  79.2 us (27%)
  Pallas kernels  49.4 us (17%)
  waiting for transfers between devices  44 us (15%)
  local copies, waits for them, and re-layouts  11.9 us (4%)
  other arithmetic  8.45 us (3%)
  matrix products  3.56 us (1%)
    all_to_all x1, blocking collectives, reduce_all(): lax.all_to_all(terms.reshape(32, part, channels), ('x', 'y', 'core'), 0,...  48.7 us
    pallas_call x1, Pallas kernels, attention(): pl.pallas_call(attend_rows, out_shape=[jax.ShapeDtypeStruct(s, t) for s,...  43.9 us
    all_to_all x1, blocking collectives, reduce_all(): band = lax.all_to_all(band, ('zh', 'zl'), 0, 0, tiled=True)  27.8 us
    all_to_all x3, starting transfers between devices, to_rows(): lax.all_to_all(jnp.concatenate(grown, axis=1), PLANE, 0, 0, tiled=True)  27.1 us
    ppermute x1, waiting for transfers between devices, on_device(): kv_far = lax.ppermute(kv_own, 'zh', SWAP)  14.2 us
    all_to_all x1, blocking collectives, reduce_all(): lax.all_to_all(jnp.broadcast_to(band[None], (16, piece)), ('zh', 'zl'), 0...  13.8 us
    all_to_all x1, waiting for transfers between devices, reduce_all(): lax.all_to_all(jnp.broadcast_to(band[None], (32, part, channels)), ('x',...  12.8 us
    ppermute x1, starting transfers between devices, on_device(): hid_far = lax.ppermute(hid_own, 'zh', SWAP)  12.1 us
  transfers between devices with their start and end apart: 14, of which 8 were waited for; matrix products, arithmetic and copies ran while one was open for 3% of the time, Pallas kernels for 16%

profile of v2, /device:TPU:1, one launch (start us, length us, event | category | flops | bytes accessed | tf_op | source)
XLA Modules:
  0.0 288.1 jit_solution(17365374022980880489)
XLA Ops:
  1.6 1.0 copy.37
  3.4 10.2 %all-to-all-start = ((bf16[8,192,128]{2,1,0:T(8,128)(2,1)}), bf16[8,192,128]{2,1,0:T(8,128)(2,1)S(1)}, u32[]{:S(2)}, u32[]{:S(2)}) async-start(bf16[8,192,128]{2,1,0:T(8,128)(2,1)} %fusion.4), calls=%async_computation | async-start | bytes 786432 | tf_op jit(solution)/shard_map/all_to_all | solution.py:378
  13.7 8.0 %all-to-all-done.kv_ref = bf16[8,192,128]{2,1,0:T(8,128)(2,1)S(1)} async-done(((bf16[8,192,128]{2,1,0:T(8,128)(2,1)}), bf16[8,192,128]{2,1,0:T(8,128)(2,1)S(1)}, u32[]{:S(2)}, u32[]{:S(2)}) %all-to-all-start) | async-done | bytes 393248 | tf_op jit(solution)/shard_map/all_to_all | solution.py:378
  22.0 11.7 %collective-permute-start = (bf16[8,16,128]{2,1,0:T(8,128)(2,1)S(1)}, bf16[8,16,128]{2,1,0:T(8,128)(2,1)S(1)}, u32[]{:S(2)}, u32[]{:S(2)}) collective-permute-start(bf16[8,16,128]{2,1,0:T(8,128)(2,1)S(1)} %get-tuple-element.78), channel_id=1, source_target_pairs={{0,480},{32,64},{64,32},{96,128},{128,96},{160,192},{192,160},{224... | collective-permute-start | bytes 98312 | tf_op jit(solution)/shard_map/ppermute | solution.py:44
  33.7 2.1 collective-permute-start.1
  36.0 2.8 collective-permute-start.4
  39.1 2.3 collective-permute-start.2
  41.5 1.3 collective-permute-start.3
  43.6 3.9 %all-to-all-start.1 = ((bf16[8,192,128]{2,1,0:T(8,128)(2,1)}), bf16[8,192,128]{2,1,0:T(8,128)(2,1)S(1)}, u32[]{:S(2)}, u32[]{:S(2)}) async-start(bf16[8,192,128]{2,1,0:T(8,128)(2,1)} %fusion.5), calls=%async_computation.1 | async-start | bytes 786432 | tf_op jit(solution)/shard_map/all_to_all | solution.py:378
  49.5 14.2 %collective-permute-done.4.far_ref = bf16[8,192,128]{2,1,0:T(8,128)(2,1)S(1)} collective-permute-done((bf16[8,192,128]{2,1,0:T(8,128)(2,1)S(1)}, bf16[8,192,128]{2,1,0:T(8,128)(2,1)S(1)}, u32[]{:S(2)}, u32[]{:S(2)}) %collective-permute-start.4) | collective-permute-done | bytes 393248 | tf_op jit(solution)/shard_map/ppermute | solution.py:381
  63.7 3.2 %forward_block.1 = (bf16[8,96,128]{2,1,0:T(8,128)(2,1)}, bf16[16,112,128]{2,1,0:T(8,128)(2,1)S(1)}, f32[10,112,128]{2,1,0:T(8,128)S(1)}, f32[8,112,128]{2,1,0:T(8,128)S(1)}) custom-call(s32[1]{0:T(128)} %bitcast.lat_ref, bf16[18,128,128]{2,1,0:T(8,128)(2,1)S(1)} %pad_maximum_fusion.1.feat_ref, bf16[3,3,128,128]{3,2,1,0:T(8,128)(2,1)S(1)} %copy-done.5, ...), custom_call_target="tpu_custom_call" | custom-call | flops 6000000000 | bytes 4000000 | tf_op jit(solution)/shard_map/forward_block/pallas_call | solution.py:253
  68.5 13.0 %all-to-all-start.3 = ((bf16[8,96,128]{2,1,0:T(8,128)(2,1)}), bf16[8,96,128]{2,1,0:T(8,128)(2,1)}, u32[]{:S(2)}, u32[]{:S(2)}) async-start(bf16[8,96,128]{2,1,0:T(8,128)(2,1)} %get-tuple-element.35), calls=%async_computation.3 | async-start | bytes 393216 | tf_op jit(solution)/shard_map/all_to_all | solution.py:378
  81.5 1.0 copy-done.4
  83.4 43.9 %attend_rows.1 = (f32[8,96,128]{2,1,0:T(8,128)S(1)}, f32[8,96,128]{2,1,0:T(8,128)S(1)}, bf16[8,96,128]{2,1,0:T(8,128)(2,1)}, f32[128,128]{1,0:T(8,128)S(1)}, bf1...) custom-call(bf16[8,192,128]{2,1,0:T(8,128)(2,1)S(1)} %all-to-all-done.1.qc_ref, ...), custom_call_target="tpu_custom_call" | custom-call | flops 14495514624 | bytes 1572864 | tf_op jit(solution)/shard_map/attend_rows/pallas_call | solution.py:173
  128.6 1.9 collective-permute-start.5
  130.6 1.2 fusion.10
  131.7 12.1 %collective-permute-start.8 = (bf16[8,96,128]{2,1,0:T(8,128)(2,1)}, bf16[8,96,128]{2,1,0:T(8,128)(2,1)}, u32[]{:S(2)}, u32[]{:S(2)}) collective-permute-start(bf16[8,96,128]{2,1,0:T(8,128)(2,1)} %all-to-all-done.3), channel_id=1, source_target_pairs={{0,64},{64,0},{1,65},{65,1},{2,66},{66,2},{3,67},{67,3},{4,68},{68... | collective-permute-start | bytes 589832 | tf_op jit(solution)/shard_map/ppermute | solution.py:408
  143.8 1.2 fusion.18
  146.9 1.0 add_convert_fusion
  148.7 6.0 %all-to-all-start.2 = ((bf16[8,112,128]{2,1,0:T(8,128)(2,1)}), bf16[8,112,128]{2,1,0:T(8,128)(2,1)S(1)}, u32[]{:S(2)}, u32[]{:S(2)}) async-start(bf16[8,112,128]{2,1,0:T(8,128)(2,1)} %bitcast.4), calls=%async_computation.2 | async-start | bytes 458752 | tf_op jit(solution)/shard_map/all_to_all | solution.py:426
  154.7 1.2 convolution_add_fusion
  155.9 5.0 %all-to-all-done.2 = bf16[8,112,128]{2,1,0:T(8,128)(2,1)S(1)} async-done(((bf16[8,112,128]{2,1,0:T(8,128)(2,1)}), bf16[8,112,128]{2,1,0:T(8,128)(2,1)S(1)}, u32[]{:S(2)}, u32[]{:S(2)}) %all-to-all-start.2) | async-done | bytes 229408 | tf_op jit(solution)/shard_map/all_to_all | solution.py:426
  161.1 1.3 collective-permute-start.7
  162.4 4.2 %collective-permute-start.6 = (bf16[6,112,128]{2,1,0:T(8,128)(2,1)S(1)}, bf16[6,112,128]{2,1,0:T(8,128)(2,1)S(1)}, u32[]{:S(2)}, u32[]{:S(2)}) collective-permute-start(bf16[6,112,128]{2,1,0:T(8,128)(2,1)S(1)} %pad_maximum_fusion.15), channel_id=1, source_target_pairs={{0,1},{1,2},{2,3},{3,4},{4,5},{5,6},{6,7},{7,8},{8,9},{9,10},{10,1... | collective-permute-start | bytes 516104 | tf_op jit(solution)/shard_map/ppermute | solution.py:50
  166.7 1.1 collective-permute-done.7
  169.0 2.3 backward_block.1
  171.3 48.7 %all_to_all.46 = bf16[32,88,128]{2,1,0:T(8,128)(2,1)S(1)} all-to-all(bf16[32,88,128]{2,1,0:T(8,128)(2,1)S(1)} %bitcast.22), channel_id=1, replica_groups=mesh['x'=4,'zh'=2,'core'=2,'zl'=8,'y'=4] {'x','y','core'}, dimensions={0} | all-to-all | bytes 1441792 | tf_op jit(solution)/shard_map/all_to_all | solution.py:354
  221.6 27.8 %all_to_all.47 = bf16[16,2,352]{2,1,0:T(2,128)(2,1)S(1)} all-to-all(bf16[16,2,352]{2,1,0:T(2,128)(2,1)S(1)} %reshape.84), channel_id=1, replica_groups=mesh['x'=4,'zh'=2,'core'=2,'zl'=8,'y'=4] {'zh','zl'}, dimensions={0} | all-to-all | bytes 45056 | tf_op jit(solution)/shard_map/all_to_all | solution.py:358
  250.5 13.8 %all_to_all.48 = bf16[16,2,352]{2,1,0:T(2,128)(2,1)S(1)} all-to-all(bf16[16,2,352]{2,1,0:T(2,128)(2,1)S(1)} %reshape.86), channel_id=1, replica_groups=mesh['x'=4,'zh'=2,'core'=2,'zl'=8,'y'=4] {'zh','zl'}, dimensions={0} | all-to-all | bytes 45056 | tf_op jit(solution)/shard_map/all_to_all | solution.py:360
  265.7 6.2 %all-to-all-start.7 = ((bf16[32,88,128]{2,1,0:T(8,128)(2,1)}), bf16[32,88,128]{2,1,0:T(8,128)(2,1)S(1)}, u32[]{:S(2)}, u32[]{:S(2)}) async-start(bf16[32,88,128]{2,1,0:T(8,128)(2,1)} %broadcast_in_dim.31), calls=%async_computation.7 | async-start | bytes 1441792 | tf_op jit(solution)/shard_map/all_to_all | solution.py:363
  272.7 12.8 %all-to-all-done.7 = bf16[32,88,128]{2,1,0:T(8,128)(2,1)S(1)} async-done(((bf16[32,88,128]{2,1,0:T(8,128)(2,1)}), bf16[32,88,128]{2,1,0:T(8,128)(2,1)S(1)}, u32[]{:S(2)}, u32[]{:S(2)}) %all-to-all-start.7) | async-done | bytes 720928 | tf_op jit(solution)/shard_map/all_to_all | solution.py:363
  286.3 1.1 fusion.23
  (116 shorter events, 19.1 us)
Async XLA Ops:
  0.6 21.1 %copy-start.17 = (bf16[8,90,128]{2,0,1:T(8,128)(2,1)S(1)}, bf16[8,90,128]{2,0,1:T(8,128)(2,1)}, u32[]{:S(2)}) copy-start(bf16[8,90,128]{2,0,1:T(8,128)(2,1)} %param.13) | copy-start | bytes 552964
  1.6 20.2 %copy-start.18 = (bf16[8,90,128]{2,0,1:T(8,128)(2,1)S(1)}, bf16[8,90,128]{2,0,1:T(8,128)(2,1)}, u32[]{:S(2)}) copy-start(bf16[8,90,128]{2,0,1:T(8,128)(2,1)} %param.9) | copy-start | bytes 552964
  2.6 33.3 %copy-start.19 = (bf16[8,90,128]{2,0,1:T(8,128)(2,1)S(1)}, bf16[8,90,128]{2,0,1:T(8,128)(2,1)}, u32[]{:S(2)}) copy-start(bf16[8,90,128]{2,0,1:T(8,128)(2,1)} %param.10) | copy-start | bytes 552964
  3.4 18.3 %all-to-all-start = ((bf16[8,192,128]{2,1,0:T(8,128)(2,1)}), bf16[8,192,128]{2,1,0:T(8,128)(2,1)S(1)}, u32[]{:S(2)}, u32[]{:S(2)}) async-start(bf16[8,192,128]{2,1,0:T(8,128)(2,1)} %fusion.4), calls=%async_computation | async-start | bytes 786432 | tf_op jit(solution)/shard_map/all_to_all | solution.py:378
  22.0 16.9 %collective-permute-start = (bf16[8,16,128]{2,1,0:T(8,128)(2,1)S(1)}, bf16[8,16,128]{2,1,0:T(8,128)(2,1)S(1)}, u32[]{:S(2)}, u32[]{:S(2)}) collective-permute-start(bf16[8,16,128]{2,1,0:T(8,128)(2,1)S(1)} %get-tuple-element.78), channel_id=1, source_target_pairs={{0,480},{32,64},{64,32},{96,128},{128,96},{160,192},{192,160},{224... | collective-permute-start | bytes 98312 | tf_op jit(solution)/shard_map/ppermute | solution.py:44
  33.7 5.1 %collective-permute-start.1 = (bf16[8,16,128]{2,1,0:T(8,128)(2,1)S(1)}, bf16[8,16,128]{2,1,0:T(8,128)(2,1)S(1)}, u32[]{:S(2)}, u32[]{:S(2)}) collective-permute-start(bf16[8,16,128]{2,1,0:T(8,128)(2,1)S(1)} %get-tuple-element.79), channel_id=1, source_target_pairs={{0,32},{32,0},{1,33},{33,1},{2,34},{34,2},{3,35},{35,3},{4,36},{36... | collective-permute-start | bytes 98312 | tf_op jit(solution)/shard_map/ppermute | solution.py:42
  36.0 27.7 %collective-permute-start.4 = (bf16[8,192,128]{2,1,0:T(8,128)(2,1)S(1)}, bf16[8,192,128]{2,1,0:T(8,128)(2,1)S(1)}, u32[]{:S(2)}, u32[]{:S(2)}) collective-permute-start(bf16[8,192,128]{2,1,0:T(8,128)(2,1)S(1)} %all-to-all-done.kv_ref), channel_id=1, source_target_pairs={{0,64},{64,0},{1,65},{65,1},{2,66},{66,2},{3,67},{67,3},{4,68},{68... | collective-permute-start | bytes 1179656 | tf_op jit(solution)/shard_map/ppermute | solution.py:381
  39.1 9.1 %collective-permute-start.2 = (bf16[6,128,128]{2,1,0:T(8,128)(2,1)S(1)}, bf16[6,128,128]{2,1,0:T(8,128)(2,1)S(1)}, u32[]{:S(2)}, u32[]{:S(2)}) collective-permute-start(bf16[6,128,128]{2,1,0:T(8,128)(2,1)S(1)} %get-tuple-element.62), channel_id=1, source_target_pairs={{0,1},{1,2},{2,3},{3,4},{4,5},{5,6},{6,7},{7,8},{8,9},{9,10},{10,1... | collective-permute-start | bytes 589832 | tf_op jit(solution)/shard_map/ppermute | solution.py:50
  41.5 7.8 %collective-permute-start.3 = (bf16[6,128,128]{2,1,0:T(8,128)(2,1)S(1)}, bf16[6,128,128]{2,1,0:T(8,128)(2,1)S(1)}, u32[]{:S(2)}, u32[]{:S(2)}) collective-permute-start(bf16[6,128,128]{2,1,0:T(8,128)(2,1)S(1)} %get-tuple-element.63), channel_id=1, source_target_pairs={{1,0},{2,1},{3,2},{4,3},{5,4},{6,5},{7,6},{8,7},{9,8},{10,9},{11,1... | collective-permute-start | bytes 589832 | tf_op jit(solution)/shard_map/ppermute | solution.py:51
  43.6 24.9 %all-to-all-start.1 = ((bf16[8,192,128]{2,1,0:T(8,128)(2,1)}), bf16[8,192,128]{2,1,0:T(8,128)(2,1)S(1)}, u32[]{:S(2)}, u32[]{:S(2)}) async-start(bf16[8,192,128]{2,1,0:T(8,128)(2,1)} %fusion.5), calls=%async_computation.1 | async-start | bytes 786432 | tf_op jit(solution)/shard_map/all_to_all | solution.py:378
  48.3 15.5 %copy-start.5 = (bf16[3,3,128,128]{3,2,1,0:T(8,128)(2,1)S(1)}, bf16[3,3,128,128]{3,2,1,0:T(8,128)(2,1)}, u32[]{:S(2)}) copy-start(bf16[3,3,128,128]{3,2,1,0:T(8,128)(2,1)} %near_ref.3) | copy-start | bytes 884740
  48.3 15.5 %copy-start.7 = (bf16[3,3,128,128]{3,2,1,0:T(8,128)(2,1)S(1)}, bf16[3,3,128,128]{3,2,1,0:T(8,128)(2,1)}, u32[]{:S(2)}) copy-start(bf16[3,3,128,128]{3,2,1,0:T(8,128)(2,1)} %dil_ref.1) | copy-start | bytes 884740
  63.7 3.2 %copy-start.3 = (bf16[8,192,128]{2,1,0:T(8,128)(2,1)}, bf16[8,192,128]{2,1,0:T(8,128)(2,1)S(1)}, u32[]{:S(2)}) copy-start(bf16[8,192,128]{2,1,0:T(8,128)(2,1)S(1)} %collective-permute-done.4.far_ref) | copy-start | bytes 1179652
  63.7 17.8 %copy-start.10 = (bf16[128,128]{1,0:T(8,128)(2,1)S(1)}, bf16[128,128]{1,0:T(8,128)(2,1)}, u32[]{:S(2)}) copy-start(bf16[128,128]{1,0:T(8,128)(2,1)} %proj_ref.1) | copy-start | bytes 98308
  66.9 0.8 copy-start.11
  67.7 0.8 copy-start.13
  68.5 62.1 %all-to-all-start.3 = ((bf16[8,96,128]{2,1,0:T(8,128)(2,1)}), bf16[8,96,128]{2,1,0:T(8,128)(2,1)}, u32[]{:S(2)}, u32[]{:S(2)}) async-start(bf16[8,96,128]{2,1,0:T(8,128)(2,1)} %get-tuple-element.35), calls=%async_computation.3 | async-start | bytes 393216 | tf_op jit(solution)/shard_map/all_to_all | solution.py:378
  81.5 1.0 copy-start.4
  82.5 0.9 copy-start.9
  128.6 17.3 %collective-permute-start.5 = (bf16[8,96,128]{2,1,0:T(8,128)(2,1)}, bf16[8,96,128]{2,1,0:T(8,128)(2,1)S(1)}, u32[]{:S(2)}, u32[]{:S(2)}) collective-permute-start(bf16[8,96,128]{2,1,0:T(8,128)(2,1)} %get-tuple-element.26), channel_id=1, source_target_pairs={{0,64},{64,0},{1,65},{65,1},{2,66},{66,2},{3,67},{67,3},{4,68},{68... | collective-permute-start | bytes 589832 | tf_op jit(solution)/shard_map/ppermute | solution.py:413
  131.7 23.0 %collective-permute-start.8 = (bf16[8,96,128]{2,1,0:T(8,128)(2,1)}, bf16[8,96,128]{2,1,0:T(8,128)(2,1)}, u32[]{:S(2)}, u32[]{:S(2)}) collective-permute-start(bf16[8,96,128]{2,1,0:T(8,128)(2,1)} %all-to-all-done.3), channel_id=1, source_target_pairs={{0,64},{64,0},{1,65},{65,1},{2,66},{66,2},{3,67},{67,3},{4,68},{68... | collective-permute-start | bytes 589832 | tf_op jit(solution)/shard_map/ppermute | solution.py:408
  146.0 0.9 copy-start.16
  146.9 14.1 %copy-start.15 = (bf16[8,128,128]{2,1,0:T(8,128)(2,1)S(1)}, bf16[8,128,128]{2,1,0:T(8,128)(2,1)}, u32[]{:S(2)}) copy-start(bf16[8,128,128]{2,1,0:T(8,128)(2,1)} %pad_maximum_fusion.9) | copy-start | bytes 786436
  148.7 12.2 %all-to-all-start.2 = ((bf16[8,112,128]{2,1,0:T(8,128)(2,1)}), bf16[8,112,128]{2,1,0:T(8,128)(2,1)S(1)}, u32[]{:S(2)}, u32[]{:S(2)}) async-start(bf16[8,112,128]{2,1,0:T(8,128)(2,1)} %bitcast.4), calls=%async_computation.2 | async-start | bytes 458752 | tf_op jit(solution)/shard_map/all_to_all | solution.py:426
  160.9 5.7 %copy-start.1 = (f32[128,128]{1,0:T(8,128)S(1)}, f32[128,128]{1,0:T(8,128)}, u32[]{:S(2)}) copy-start(f32[128,128]{1,0:T(8,128)} %copy-done) | copy-start | bytes 196612
  161.1 6.8 %collective-permute-start.7 = (bf16[6,112,128]{2,1,0:T(8,128)(2,1)S(1)}, bf16[6,112,128]{2,1,0:T(8,128)(2,1)S(1)}, u32[]{:S(2)}, u32[]{:S(2)}) collective-permute-start(bf16[6,112,128]{2,1,0:T(8,128)(2,1)S(1)} %pad_maximum_fusion.16), channel_id=1, source_target_pairs={{1,0},{2,1},{3,2},{4,3},{5,4},{6,5},{7,6},{8,7},{9,8},{10,9},{11,1... | collective-permute-start | bytes 516104 | tf_op jit(solution)/shard_map/ppermute | solution.py:51
  162.4 6.3 %collective-permute-start.6 = (bf16[6,112,128]{2,1,0:T(8,128)(2,1)S(1)}, bf16[6,112,128]{2,1,0:T(8,128)(2,1)S(1)}, u32[]{:S(2)}, u32[]{:S(2)}) collective-permute-start(bf16[6,112,128]{2,1,0:T(8,128)(2,1)S(1)} %pad_maximum_fusion.15), channel_id=1, source_target_pairs={{0,1},{1,2},{2,3},{3,4},{4,5},{5,6},{6,7},{7,8},{8,9},{9,10},{10,1... | collective-permute-start | bytes 516104 | tf_op jit(solution)/shard_map/ppermute | solution.py:50
  166.7 2.2 copy-start.6
  166.7 2.2 copy-start.8
  166.7 2.2 copy-start.12
  166.7 2.2 copy-start.14
  265.7 19.8 %all-to-all-start.7 = ((bf16[32,88,128]{2,1,0:T(8,128)(2,1)}), bf16[32,88,128]{2,1,0:T(8,128)(2,1)S(1)}, u32[]{:S(2)}, u32[]{:S(2)}) async-start(bf16[32,88,128]{2,1,0:T(8,128)(2,1)} %broadcast_in_dim.31), calls=%async_computation.7 | async-start | bytes 1441792 | tf_op jit(solution)/shard_map/all_to_all | solution.py:363
  (2 other events, 1.4 us)

commit v3 on v2

--- a/solution.py
+++ b/solution.py
@@ -11,6 +11,7 @@
 COLS = 90
 GROWN = 96
 EDGE = 5
+CHUNK = 256
 GELU_COEF = 0.7978845608028654
 CUBIC_COEF = 0.044715
 
@@ -52,16 +53,13 @@
     return low, high
 
 
-def attend_rows(qc_ref, kv_ref, far_ref, proj_ref, qkv_ref, part_ref, away_ref, send_ref,
-                term_ref, own_ref, farg_ref,
-                out_s, keep_s, grad_s, key_s, value_s, query_s, mixed_s):
-    blocks = qc_ref.shape[0]
-    wide = qc_ref.shape[1] // 2
+def attend_rows(qc_ref, own_ref, far_ref, proj_ref, mixed_ref, grad_ref, away_ref,
+                out_s, keep_s, grad_s, pair_s, value_s, key_g, value_g, query_g, mixed_g, *, heads):
+    blocks, wide, channels = own_ref.shape
     rows = blocks * wide
     cols = 2 * rows
-    channels = qc_ref.shape[2]
     width = channels // HEADS
-    chunk = 256
+    chunk = CHUNK
     low = jnp.bfloat16
 
     def rows_of(ref, at):
@@ -70,8 +68,11 @@
     out_s[...] = lax.dot_general(
         rows_of(qc_ref, wide), proj_ref[...], (((1,), (1,)), ((), ())),
         preferred_element_type=jnp.float32,
-    ).astype(low)
-    for ref in (key_s, value_s, query_s, mixed_s):
+    )
+    pair = jnp.concatenate([rows_of(own_ref, 0), rows_of(far_ref, 0)], axis=0).astype(jnp.float32)
+    pair_s[...] = pair
+    value_s[...] = pltpu.roll(pair, channels // 2, 1)
+    for ref in (key_g, value_g, query_g, mixed_g):
         ref[...] = jnp.zeros_like(ref)
     lane_k = lax.broadcasted_iota(jnp.int32, (cols, channels), 1)
     filler = lax.broadcasted_iota(jnp.int32, (cols, channels), 0) % wide >= COLS
@@ -81,18 +82,17 @@
         first = (head * width + width) % channels
         here_k = lane_k // width == head
         here_q = lane_q // width == head
-        keys = jnp.concatenate([rows_of(kv_ref, 0), rows_of(far_ref, 0)], axis=0)
-        values = jnp.concatenate([rows_of(kv_ref, wide), rows_of(far_ref, wide)], axis=0)
         spare = jnp.where((lane_k == first) & filler, -1e30, 0.0)
-        keys_h = jnp.where(here_k, keys.astype(jnp.float32), spare).astype(low)
+        keys_h = jnp.where(here_k, pair_s[...], spare).astype(low)
         ones = jnp.where((lane_k == first) | (lane_k == first + 1), 1.0, 0.0)
-        values_h = jnp.where(here_k, values.astype(jnp.float32), ones).astype(low)
+        values_h = jnp.where(here_k, value_s[...], ones).astype(low)
         query_n, dout_n = [], []
         for i in range(rows // chunk):
             at = i * chunk
             query = rows_of(qc_ref, 0)[at : at + chunk].astype(jnp.float32) * 0.25
             query_h = jnp.where(here_q, query, jnp.where(lane_q == first, 1.0, 0.0)).astype(low)
-            dout = jnp.where(here_q, out_s[at : at + chunk, :].astype(jnp.float32), 0.0)
+            dout = out_s[at : at + chunk, :].astype(low).astype(jnp.float32)
+            dout = jnp.where(here_q, dout, 0.0)
             scores = lax.dot_general(
                 query_h, keys_h, (((1,), (1,)), ((), ())), preferred_element_type=jnp.float32
             )
@@ -103,7 +103,7 @@
             total = jnp.sum(jnp.where(lane_q == first, mixed, 0.0), axis=1, keepdims=True)
             share = 1.0 / total
             mixed = jnp.where(here_q, mixed * share, 0.0)
-            mixed_s[at : at + chunk, :] += mixed
+            mixed_g[at : at + chunk, :] += mixed
             delta = jnp.sum(dout * mixed, axis=1, keepdims=True)
             high = delta.astype(low).astype(jnp.float32)
             dout_x = jnp.where(
@@ -114,50 +114,88 @@
             )
             score_grad = raised * prob_grad.astype(low)
             grad_s[at : at + chunk, :] = score_grad
-            query_s[at : at + chunk, :] += (
+            query_g[at : at + chunk, :] += (
                 jnp.dot(score_grad, keys_h, preferred_element_type=jnp.float32) * (0.25 * share)
             )
             query_n.append((jnp.where(here_q, query, 0.0) * share).astype(low))
             dout_n.append((dout * share).astype(low))
-        key_s[...] += lax.dot_general(
+        key_g[...] += lax.dot_general(
             grad_s[...], jnp.concatenate(query_n, axis=0), (((0,), (0,)), ((), ())),
             preferred_element_type=jnp.float32,
         )
-        value_s[...] += lax.dot_general(
+        value_g[...] += lax.dot_general(
             keep_s[...], jnp.concatenate(dout_n, axis=0), (((0,), (0,)), ((), ())),
             preferred_element_type=jnp.float32,
         )
         return carry
 
-    lax.fori_loop(0, HEADS, one_head, 0)
-    own_ref[:, :channels] = query_s[...].astype(low)
-    own_ref[:, channels : 2 * channels] = key_s[:rows, :].astype(low)
-    own_ref[:, 2 * channels :] = value_s[:rows, :].astype(low)
-    farg_ref[:, :channels] = key_s[rows:, :].astype(low)
-    farg_ref[:, channels:] = value_s[rows:, :].astype(low)
+    lax.fori_loop(heads[0], heads[1], one_head, 0)
+    mixed_ref[...] = mixed_g[...].astype(low)
+    grad_ref[:, :channels] = query_g[...].astype(low)
+    grad_ref[:, channels : 2 * channels] = key_g[:rows, :].astype(low)
+    grad_ref[:, 2 * channels :] = value_g[:rows, :].astype(low)
+    away_ref[:, :channels] = key_g[rows:, :].astype(low)
+    away_ref[:, channels:] = value_g[rows:, :].astype(low)
+
+
+def attention(qc_own, kv_own, kv_far, proj_out, heads):
+    blocks, wide, channels = kv_own.shape
+    rows = blocks * wide
+    low = jnp.bfloat16
+    shapes = [(rows, channels), (rows, 3 * channels), (rows, 2 * channels)]
+    return pl.pallas_call(
+        functools.partial(attend_rows, heads=heads),
+        out_shape=[jax.ShapeDtypeStruct(s, low) for s in shapes],
+        in_specs=[pl.BlockSpec(memory_space=pltpu.VMEM)] * 4,
+        out_specs=[pl.BlockSpec(memory_space=pltpu.VMEM)] * 3,
+        scratch_shapes=[
+            pltpu.VMEM((rows, channels), jnp.float32),
+            pltpu.VMEM((rows, 2 * rows), low),
+            pltpu.VMEM((rows, 2 * rows), low),
+            pltpu.VMEM((2 * rows, channels), jnp.float32),
+            pltpu.VMEM((2 * rows, channels), jnp.float32),
+            pltpu.VMEM((2 * rows, channels), jnp.float32),
+            pltpu.VMEM((2 * rows, channels), jnp.float32),
+            pltpu.VMEM((rows, channels), jnp.float32),
+            pltpu.VMEM((rows, channels), jnp.float32),
+        ],
+        compiler_params=pltpu.CompilerParams(vmem_limit_bytes=48 * 1024 * 1024),
+        cost_estimate=pl.CostEstimate(
+            flops=12 * rows * 2 * rows * channels * (heads[1] - heads[0]),
+            bytes_accessed=16 * rows * channels,
+            transcendentals=(heads[1] - heads[0]) * rows * 2 * rows,
+        ),
+        name="attend_rows",
+    )(qc_own, kv_own, kv_far, proj_out)
+
+
+def gather_parts(first_refs, second_refs, cot_ref, qkv_ref, part_ref, away_ref, send_ref, term_ref,
+                 all_ref, far_ref, send_s):
+    channels = cot_ref.shape[2]
+    blocks, wide = cot_ref.shape[0], cot_ref.shape[1] // 2
+    rows = blocks * wide
+    low = jnp.bfloat16
+    mixed, own, far = (a[...] + b[...] for a, b in zip(first_refs, second_refs))
+    all_ref[...] = own
+    far_ref[...] = far
     own_part = lax.dot_general(
-        own_ref[...], qkv_ref[...], (((1,), (1,)), ((), ())), preferred_element_type=jnp.float32
+        own, qkv_ref[...], (((1,), (1,)), ((), ())), preferred_element_type=jnp.float32
     )
     far_part = lax.dot_general(
-        farg_ref[...], qkv_ref[:, channels:], (((1,), (1,)), ((), ())),
-        preferred_element_type=jnp.float32,
+        far, qkv_ref[:, channels:], (((1,), (1,)), ((), ())), preferred_element_type=jnp.float32
     )
     part_ref[...] = own_part.reshape(blocks, wide, channels)
     away_ref[...] = far_part.reshape(blocks, wide, channels)
-    query_s[...] = far_part
+    send_s[...] = far_part.reshape(blocks, wide, channels)
     for block in range(blocks):
         edge = 0 if block % 2 == 0 else COLS - EDGE
-        query_s[block * wide + COLS : block * wide + COLS + EDGE, :] = part_ref[
-            block, edge : edge + EDGE, :
-        ]
-    send_ref[...] = query_s[...].astype(low).reshape(blocks, wide, channels)
-    term_ref[...] = lax.dot_general(
-        mixed_s[...].astype(low), rows_of(qc_ref, wide), (((0,), (0,)), ((), ())),
-        preferred_element_type=jnp.float32,
-    )
-
-
-def attention(qc_own, kv_own, kv_far, proj_out, proj_qkv):
+        send_s[block, COLS : COLS + EDGE, :] = part_ref[block, edge : edge + EDGE, :]
+    send_ref[...] = send_s[...].astype(low)
+    cot = cot_ref[:, wide:, :].reshape(rows, channels)
+    term_ref[...] = contract_rows(mixed, cot)
+
+
+def combine(first, second, qc_own, proj_qkv):
     blocks, double, channels = qc_own.shape
     wide = double // 2
     rows = blocks * wide
@@ -170,28 +208,22 @@
         ((rows, 3 * channels), low),
         ((rows, 2 * channels), low),
     ]
+
+    def body(*refs):
+        gather_parts(refs[:3], refs[3:6], *refs[6:])
+
     return pl.pallas_call(
-        attend_rows,
+        body,
         out_shape=[jax.ShapeDtypeStruct(s, t) for s, t in shapes],
-        in_specs=[pl.BlockSpec(memory_space=pltpu.VMEM)] * 5,
+        in_specs=[pl.BlockSpec(memory_space=pltpu.VMEM)] * 8,
         out_specs=[pl.BlockSpec(memory_space=pltpu.VMEM)] * 6,
-        scratch_shapes=[
-            pltpu.VMEM((rows, channels), low),
-            pltpu.VMEM((rows, 2 * rows), low),
-            pltpu.VMEM((rows, 2 * rows), low),
-            pltpu.VMEM((2 * rows, channels), jnp.float32),
-            pltpu.VMEM((2 * rows, channels), jnp.float32),
-            pltpu.VMEM((rows, channels), jnp.float32),
-            pltpu.VMEM((rows, channels), jnp.float32),
-        ],
-        compiler_params=pltpu.CompilerParams(vmem_limit_bytes=48 * 1024 * 1024),
+        scratch_shapes=[pltpu.VMEM((blocks, wide, channels), jnp.float32)],
+        compiler_params=pltpu.CompilerParams(vmem_limit_bytes=24 * 1024 * 1024),
         cost_estimate=pl.CostEstimate(
-            flops=12 * rows * 2 * rows * channels * HEADS,
-            bytes_accessed=16 * rows * channels,
-            transcendentals=HEADS * rows * 2 * rows,
+            flops=12 * rows * channels * channels, bytes_accessed=5 * 10**6, transcendentals=0
         ),
-        name="attend_rows",
-    )(qc_own, kv_own, kv_far, proj_out, proj_qkv)
+        name="combine",
+    )(*first, *second, qc_own, proj_qkv)
 
 
 def row_inside(lat_ref, shape, width):
@@ -377,10 +409,18 @@
         grown = [jnp.pad(f, ((0, 0), (0, GROWN - f.shape[1]), (0, 0))) for f in fields]
         return lax.all_to_all(jnp.concatenate(grown, axis=1), PLANE, 0, 0, tiled=True)
 
-    kv_own = to_rows(attn_keys, attn_values)
-    kv_far = lax.ppermute(kv_own, "zh", SWAP)
-
-    features, cotangent, kv_own = lax.optimization_barrier((features, cotangent, kv_own))
+    side = channels // 2
+    kv_own = to_rows(
+        jnp.concatenate([attn_keys[..., :side], attn_values[..., :side]], axis=2),
+        jnp.concatenate([attn_values[..., side:], attn_keys[..., side:]], axis=2),
+    )
+    kv_one, kv_two = kv_own[:, :GROWN], kv_own[:, GROWN:]
+    far_one = lax.ppermute(kv_one, "zh", SWAP)
+    far_two = lax.ppermute(kv_two, "zh", SWAP)
+
+    features, cotangent, kv_one, kv_two = lax.optimization_barrier(
+        (features, cotangent, kv_one, kv_two)
+    )
     blank = jnp.zeros((rows, 1, channels), features.dtype)
     low, high = exchange_lon(
         jnp.concatenate([features[:, :10], cotangent[:, :EDGE], blank], axis=1),
@@ -395,6 +435,7 @@
         [low[:, 10:15], cotangent, high[:, 10:15], jnp.zeros((rows, 28, channels), features.dtype)],
         axis=1,
     )
+    feat_x, far_one = lax.optimization_barrier((feat_x, far_one))
     low, high = exchange_lat(
         jnp.concatenate([feat_x[-5:], cot_x[-1:]], axis=0),
         jnp.concatenate([feat_x[:5], cot_x[:1]], axis=0),
@@ -402,14 +443,14 @@
     feat_x = jnp.concatenate([low[:5], feat_x, high[:5]], axis=0)
     cot_near = jnp.concatenate([low[5:], cot_x, high[5:]], axis=0)[:, :112]
 
-    feat_x, kv_far = lax.optimization_barrier((feat_x, kv_far))
     hidden_two, hidden_one, near_slope, wide_slope = forward(lat_at, feat_x, conv_near, conv_wide)
     hid_own = to_rows(hidden_two)
     hid_far = lax.ppermute(hid_own, "zh", SWAP)
 
-    own_part, far_part, sent, out_term, own_qkv, far_kv = attention(
-        qc_own, kv_own, kv_far, proj_out, proj_qkv
-    )
+    first = attention(qc_own, kv_one, far_one, proj_out, (0, HEADS // 2))
+    second = attention(qc_own, kv_two, far_two, proj_out, (HEADS // 2, HEADS))
+    own_part, far_part, sent, out_term, own_qkv, far_kv = combine(first, second, qc_own, proj_qkv)
+    sent, hid_far = lax.optimization_barrier((sent, hid_far))
     from_far = lax.ppermute(sent, "zh", SWAP)
     whole = (own_part + from_far.astype(jnp.float32)).astype(jnp.bfloat16)
     whole = whole.reshape(4, 2, GROWN, channels)

time: 289 us -> 298 us (1.031)
  blocking collectives: 90.3 us -> 74.1 us
  starting transfers between devices: 79.2 us -> 94.1 us
  waiting for transfers between devices: 44 us -> 51.3 us
    ppermute x1, waiting for transfers between devices: 0.93 us -> 16.3 us  [on_device(): from_far = lax.ppermute(sent, 'zh', SWAP)]
    ppermute x1 -> x2, waiting for transfers between devices: 14.2 us -> 0.01 us  [the longest x1 0.01 us: on_device(): far_one = lax.ppermute(kv_one, 'zh', SWAP)]
    all_to_all x1, blocking collectives: 48.7 us -> 35.1 us  [reduce_all(): lax.all_to_all(terms.reshape(32, part, channels), ('x', 'y', 'core'), 0,...]
    ppermute x1 -> x2, starting transfers between devices: 2.79 us -> 14 us  [the longest x1 11 us: on_device(): far_one = lax.ppermute(kv_one, 'zh', SWAP)]
    ppermute x1, starting transfers between devices: 1.91 us -> 12.1 us  [on_device(): from_far = lax.ppermute(sent, 'zh', SWAP)]
    all_to_all x3, starting transfers between devices: 27.1 us -> 18.3 us  [to_rows(): lax.all_to_all(jnp.concatenate(grown, axis=1), PLANE, 0, 0, tiled=True)]
    ppermute x1, waiting for transfers between devices: 0.01 us -> 3.79 us  [on_device(): hid_far = lax.ppermute(hid_own, 'zh', SWAP)]
    unnamed x48 -> x62, local copies, waits for them, and re-layouts: 8.08 us -> 5.13 us
  transfers between devices with their start and end apart: 14 -> 15, of which waited for: 8 -> 8; matrix products, arithmetic and copies ran while one was open for 3% -> 3% of each run, Pallas kernels for 16% -> 16%
where the time goes in v3:
time: 298 us; the launch traced here: 297 us
  starting transfers between devices  94.1 us (32%)
  blocking collectives  74.1 us (25%)
  waiting for transfers between devices  51.3 us (17%)
  Pallas kernels  49.7 us (17%)
  local copies, waits for them, and re-layouts  14.3 us (5%)
  other arithmetic  9.08 us (3%)
    pallas_call x2, Pallas kernels, attention(): pl.pallas_call(functools.partial(attend_rows, heads=heads), out_shape=[ja...  43.6 us
    all_to_all x1, blocking collectives, reduce_all(): lax.all_to_all(terms.reshape(32, part, channels), ('x', 'y', 'core'), 0,...  35.1 us
    all_to_all x1, blocking collectives, reduce_all(): band = lax.all_to_all(band, ('zh', 'zl'), 0, 0, tiled=True)  25.2 us
    all_to_all x3, starting transfers between devices, to_rows(): lax.all_to_all(jnp.concatenate(grown, axis=1), PLANE, 0, 0, tiled=True)  18.3 us
    ppermute x1, waiting for transfers between devices, on_device(): from_far = lax.ppermute(sent, 'zh', SWAP)  16.3 us
    all_to_all x1, blocking collectives, reduce_all(): lax.all_to_all(jnp.broadcast_to(band[None], (16, piece)), ('zh', 'zl'), 0...  13.8 us
    all_to_all x1, waiting for transfers between devices, reduce_all(): lax.all_to_all(jnp.broadcast_to(band[None], (32, part, channels)), ('x',...  12.8 us
    ppermute x1, starting transfers between devices, exchange_lon(): outer = lax.ppermute(jnp.where(at_zero, left, right), LON_AXES, pairs)  12.3 us
  transfers between devices with their start and end apart: 15, of which 8 were waited for; matrix products, arithmetic and copies ran while one was open for 3% of the time, Pallas kernels for 16%

profile of v3, /device:TPU:1, one launch (start us, length us, event | category | flops | bytes accessed | tf_op | source)
XLA Modules:
  0.0 296.6 jit_solution(12980717494021051125)
XLA Ops:
  4.1 10.2 %all-to-all-start = ((bf16[8,192,128]{2,1,0:T(8,128)(2,1)}), bf16[8,192,128]{2,1,0:T(8,128)(2,1)S(1)}, u32[]{:S(2)}, u32[]{:S(2)}) async-start(bf16[8,192,128]{2,1,0:T(8,128)(2,1)} %pad_maximum_fusion.3), calls=%async_computation | async-start | bytes 786432 | tf_op jit(solution)/shard_map/all_to_all | solution.py:410
  15.1 7.3 %all-to-all-done = bf16[8,192,128]{2,1,0:T(8,128)(2,1)S(1)} async-done(((bf16[8,192,128]{2,1,0:T(8,128)(2,1)}), bf16[8,192,128]{2,1,0:T(8,128)(2,1)S(1)}, u32[]{:S(2)}, u32[]{:S(2)}) %all-to-all-start) | async-done | bytes 393248 | tf_op jit(solution)/shard_map/all_to_all | solution.py:410
  22.5 11.0 %collective-permute-start.2 = (bf16[8,96,128]{2,1,0:T(8,128)(2,1)S(1)}, bf16[8,96,128]{2,1,0:T(8,128)(2,1)S(1)}, u32[]{:S(2)}, u32[]{:S(2)}) collective-permute-start(bf16[8,96,128]{2,1,0:T(8,128)(2,1)S(1)} %get-tuple-element.33.own_ref), channel_id=1, source_target_pairs={{0,64},{64,0},{1,65},{65,1},{2,66},{66,2},{3,67},{67,3},{4,68},{68... | collective-permute-start | bytes 589832 | tf_op jit(solution)/shard_map/ppermute | solution.py:418
  33.5 3.0 %collective-permute-start.3 = (bf16[8,96,128]{2,1,0:T(8,128)(2,1)S(1)}, bf16[8,96,128]{2,1,0:T(8,128)(2,1)S(1)}, u32[]{:S(2)}, u32[]{:S(2)}) collective-permute-start(bf16[8,96,128]{2,1,0:T(8,128)(2,1)S(1)} %get-tuple-element.38.own_ref), channel_id=1, source_target_pairs={{0,64},{64,0},{1,65},{65,1},{2,66},{66,2},{3,67},{67,3},{4,68},{68... | collective-permute-start | bytes 589832 | tf_op jit(solution)/shard_map/ppermute | solution.py:419
  36.7 12.3 %collective-permute-start = (bf16[8,16,128]{2,1,0:T(8,128)(2,1)S(1)}, bf16[8,16,128]{2,1,0:T(8,128)(2,1)S(1)}, u32[]{:S(2)}, u32[]{:S(2)}) collective-permute-start(bf16[8,16,128]{2,1,0:T(8,128)(2,1)S(1)} %get-tuple-element.102), channel_id=1, source_target_pairs={{0,480},{32,64},{64,32},{96,128},{128,96},{160,192},{192,160},{224... | collective-permute-start | bytes 98312 | tf_op jit(solution)/shard_map/ppermute | solution.py:45
  49.0 1.9 collective-permute-start.1
  51.7 3.9 %all-to-all-start.1 = ((bf16[8,192,128]{2,1,0:T(8,128)(2,1)}), bf16[8,192,128]{2,1,0:T(8,128)(2,1)S(1)}, u32[]{:S(2)}, u32[]{:S(2)}) async-start(bf16[8,192,128]{2,1,0:T(8,128)(2,1)} %fusion.2), calls=%async_computation.1 | async-start | bytes 786432 | tf_op jit(solution)/shard_map/all_to_all | solution.py:410
  55.6 2.9 collective-permute-done
  60.2 1.3 collective-permute-start.5
  61.5 5.0 %collective-permute-start.4 = (bf16[6,128,128]{2,1,0:T(8,128)(2,1)S(1)}, bf16[6,128,128]{2,1,0:T(8,128)(2,1)S(1)}, u32[]{:S(2)}, u32[]{:S(2)}) collective-permute-start(bf16[6,128,128]{2,1,0:T(8,128)(2,1)S(1)} %get-tuple-element.82), channel_id=1, source_target_pairs={{0,1},{1,2},{2,3},{3,4},{4,5},{5,6},{6,7},{7,8},{8,9},{9,10},{10,1... | collective-permute-start | bytes 589832 | tf_op jit(solution)/shard_map/ppermute | solution.py:51
  66.5 21.8 %attend_rows.2 = (bf16[768,128]{1,0:T(8,128)(2,1)S(1)}, bf16[768,384]{1,0:T(8,128)(2,1)S(1)}, bf16[768,256]{1,0:T(8,128)(2,1)S(1)}) custom-call(bf16[8,192,128]{2,1,0:T(8,128)(2,1)S(1)} %all-to-all-done.1.qc_ref.refs_6_, bf16[8,96,128]{2,1,0:T(8,128)(2,1)S(1)} %get-tuple-element.33.own_ref, bf16[8,96,128]{2,1,0:T(8,128)(2,1)S(1)} %collective-permute-done.2.far_ref, ...), custom_call_target="tpu_custom_call" | custom-call | flops 7247757312 | bytes 1572864 | tf_op jit(solution)/shard_map/attend_rows/pallas_call | solution.py:146
  90.3 3.2 %forward_block.1 = (bf16[8,96,128]{2,1,0:T(8,128)(2,1)}, bf16[16,112,128]{2,1,0:T(8,128)(2,1)S(1)}, f32[10,112,128]{2,1,0:T(8,128)S(1)}, f32[8,112,128]{2,1,0:T(8,128)S(1)}) custom-call(s32[1]{0:T(128)} %bitcast.lat_ref, bf16[18,128,128]{2,1,0:T(8,128)(2,1)S(1)} %pad_maximum_fusion.1.feat_ref, bf16[3,3,128,128]{3,2,1,0:T(8,128)(2,1)S(1)} %copy-done.6, ...), custom_call_target="tpu_custom_call" | custom-call | flops 6000000000 | bytes 4000000 | tf_op jit(solution)/shard_map/forward_block/pallas_call | solution.py:285
  95.0 4.2 %all-to-all-start.2 = ((bf16[8,96,128]{2,1,0:T(8,128)(2,1)}), bf16[8,96,128]{2,1,0:T(8,128)(2,1)}, u32[]{:S(2)}, u32[]{:S(2)}) async-start(bf16[8,96,128]{2,1,0:T(8,128)(2,1)} %get-tuple-element.44), calls=%async_computation.2 | async-start | bytes 393216 | tf_op jit(solution)/shard_map/all_to_all | solution.py:410
  99.3 21.8 %attend_rows.3 = (bf16[768,128]{1,0:T(8,128)(2,1)S(1)}, bf16[768,384]{1,0:T(8,128)(2,1)S(1)}, bf16[768,256]{1,0:T(8,128)(2,1)S(1)}) custom-call(bf16[8,192,128]{2,1,0:T(8,128)(2,1)S(1)} %all-to-all-done.1.qc_ref.refs_6_, bf16[8,96,128]{2,1,0:T(8,128)(2,1)S(1)} %get-tuple-element.38.own_ref, bf16[8,96,128]{2,1,0:T(8,128)(2,1)S(1)} %collective-permute-done.3.far_ref, ...), custom_call_target="tpu_custom_call" | custom-call | flops 7247757312 | bytes 1572864 | tf_op jit(solution)/shard_map/attend_rows/pallas_call | solution.py:146
  123.1 1.4 slice.258
  125.4 12.0 %collective-permute-start.6 = (bf16[8,96,128]{2,1,0:T(8,128)(2,1)}, bf16[8,96,128]{2,1,0:T(8,128)(2,1)S(1)}, u32[]{:S(2)}, u32[]{:S(2)}) collective-permute-start(bf16[8,96,128]{2,1,0:T(8,128)(2,1)} %all-to-all-done.2), channel_id=1, source_target_pairs={{0,64},{64,0},{1,65},{65,1},{2,66},{66,2},{3,67},{67,3},{4,68},{68... | collective-permute-start | bytes 589832 | tf_op jit(solution)/shard_map/ppermute | solution.py:448
  137.4 1.2 fusion.11
  138.6 3.8 %collective-permute-done.6 = bf16[8,96,128]{2,1,0:T(8,128)(2,1)S(1)} collective-permute-done((bf16[8,96,128]{2,1,0:T(8,128)(2,1)}, bf16[8,96,128]{2,1,0:T(8,128)(2,1)S(1)}, u32[]{:S(2)}, u32[]{:S(2)}) %collective-permute-start.6) | collective-permute-done | bytes 196640 | tf_op jit(solution)/shard_map/ppermute | solution.py:448
  142.3 12.1 %collective-permute-start.7 = (bf16[8,96,128]{2,1,0:T(8,128)(2,1)}, bf16[8,96,128]{2,1,0:T(8,128)(2,1)S(1)}, u32[]{:S(2)}, u32[]{:S(2)}) collective-permute-start(bf16[8,96,128]{2,1,0:T(8,128)(2,1)} %copy-done.10), channel_id=1, source_target_pairs={{0,64},{64,0},{1,65},{65,1},{2,66},{66,2},{3,67},{67,3},{4,68},{68... | collective-permute-start | bytes 589832 | tf_op jit(solution)/shard_map/ppermute | solution.py:454
  154.5 1.2 fusion.21
  155.7 16.3 %collective-permute-done.7 = bf16[8,96,128]{2,1,0:T(8,128)(2,1)S(1)} collective-permute-done((bf16[8,96,128]{2,1,0:T(8,128)(2,1)}, bf16[8,96,128]{2,1,0:T(8,128)(2,1)S(1)}, u32[]{:S(2)}, u32[]{:S(2)}) %collective-permute-start.7) | collective-permute-done | bytes 196640 | tf_op jit(solution)/shard_map/ppermute | solution.py:454
  173.7 5.6 %all-to-all-start.3 = ((bf16[8,112,128]{2,1,0:T(8,128)(2,1)}), bf16[8,112,128]{2,1,0:T(8,128)(2,1)S(1)}, u32[]{:S(2)}, u32[]{:S(2)}) async-start(bf16[8,112,128]{2,1,0:T(8,128)(2,1)} %bitcast.4), calls=%async_computation.3 | async-start | bytes 458752 | tf_op jit(solution)/shard_map/all_to_all | solution.py:467
  179.5 5.9 %all-to-all-done.3 = bf16[8,112,128]{2,1,0:T(8,128)(2,1)S(1)} async-done(((bf16[8,112,128]{2,1,0:T(8,128)(2,1)}), bf16[8,112,128]{2,1,0:T(8,128)(2,1)S(1)}, u32[]{:S(2)}, u32[]{:S(2)}) %all-to-all-start.3) | async-done | bytes 229408 | tf_op jit(solution)/shard_map/all_to_all | solution.py:467
  185.6 1.3 collective-permute-start.9
  187.0 4.1 %collective-permute-start.8 = (bf16[6,112,128]{2,1,0:T(8,128)(2,1)S(1)}, bf16[6,112,128]{2,1,0:T(8,128)(2,1)S(1)}, u32[]{:S(2)}, u32[]{:S(2)}) collective-permute-start(bf16[6,112,128]{2,1,0:T(8,128)(2,1)S(1)} %pad_maximum_fusion.15), channel_id=1, source_target_pairs={{0,1},{1,2},{2,3},{3,4},{4,5},{5,6},{6,7},{7,8},{8,9},{9,10},{10,1... | collective-permute-start | bytes 516104 | tf_op jit(solution)/shard_map/ppermute | solution.py:51
  191.2 1.2 collective-permute-done.9
  193.7 2.3 backward_block.1
  196.1 35.1 %all_to_all.46 = bf16[32,88,128]{2,1,0:T(8,128)(2,1)S(1)} all-to-all(bf16[32,88,128]{2,1,0:T(8,128)(2,1)S(1)} %bitcast.22), channel_id=1, replica_groups=mesh['x'=4,'zh'=2,'core'=2,'zl'=8,'y'=4] {'x','y','core'}, dimensions={0} | all-to-all | bytes 1441792 | tf_op jit(solution)/shard_map/all_to_all | solution.py:386
  232.7 25.2 %all_to_all.47 = bf16[16,2,352]{2,1,0:T(2,128)(2,1)S(1)} all-to-all(bf16[16,2,352]{2,1,0:T(2,128)(2,1)S(1)} %reshape.84), channel_id=1, replica_groups=mesh['x'=4,'zh'=2,'core'=2,'zl'=8,'y'=4] {'zh','zl'}, dimensions={0} | all-to-all | bytes 45056 | tf_op jit(solution)/shard_map/all_to_all | solution.py:390
  259.0 13.8 %all_to_all.48 = bf16[16,2,352]{2,1,0:T(2,128)(2,1)S(1)} all-to-all(bf16[16,2,352]{2,1,0:T(2,128)(2,1)S(1)} %reshape.86), channel_id=1, replica_groups=mesh['x'=4,'zh'=2,'core'=2,'zl'=8,'y'=4] {'zh','zl'}, dimensions={0} | all-to-all | bytes 45056 | tf_op jit(solution)/shard_map/all_to_all | solution.py:392
  274.2 6.2 %all-to-all-start.7 = ((bf16[32,88,128]{2,1,0:T(8,128)(2,1)}), bf16[32,88,128]{2,1,0:T(8,128)(2,1)S(1)}, u32[]{:S(2)}, u32[]{:S(2)}) async-start(bf16[32,88,128]{2,1,0:T(8,128)(2,1)} %broadcast_in_dim.31), calls=%async_computation.7 | async-start | bytes 1441792 | tf_op jit(solution)/shard_map/all_to_all | solution.py:395
  281.2 12.8 %all-to-all-done.7 = bf16[32,88,128]{2,1,0:T(8,128)(2,1)S(1)} async-done(((bf16[32,88,128]{2,1,0:T(8,128)(2,1)}), bf16[32,88,128]{2,1,0:T(8,128)(2,1)S(1)}, u32[]{:S(2)}, u32[]{:S(2)}) %all-to-all-start.7) | async-done | bytes 720928 | tf_op jit(solution)/shard_map/all_to_all | solution.py:395
  (141 shorter events, 23.9 us)
Async XLA Ops:
  3.0 11.3 %copy-start.22 = (bf16[8,90,128]{2,0,1:T(8,128)(2,1)S(1)}, bf16[8,90,128]{2,0,1:T(8,128)(2,1)}, u32[]{:S(2)}) copy-start(bf16[8,90,128]{2,0,1:T(8,128)(2,1)} %param.10) | copy-start | bytes 552964
  3.3 33.2 %copy-start.23 = (bf16[8,90,128]{2,0,1:T(8,128)(2,1)S(1)}, bf16[8,90,128]{2,0,1:T(8,128)(2,1)}, u32[]{:S(2)}) copy-start(bf16[8,90,128]{2,0,1:T(8,128)(2,1)} %param.13) | copy-start | bytes 552964
  3.3 33.2 %copy-start.24 = (bf16[8,90,128]{2,0,1:T(8,128)(2,1)S(1)}, bf16[8,90,128]{2,0,1:T(8,128)(2,1)}, u32[]{:S(2)}) copy-start(bf16[8,90,128]{2,0,1:T(8,128)(2,1)} %param.9) | copy-start | bytes 552964
  4.1 18.3 %all-to-all-start = ((bf16[8,192,128]{2,1,0:T(8,128)(2,1)}), bf16[8,192,128]{2,1,0:T(8,128)(2,1)S(1)}, u32[]{:S(2)}, u32[]{:S(2)}) async-start(bf16[8,192,128]{2,1,0:T(8,128)(2,1)} %pad_maximum_fusion.3), calls=%async_computation | async-start | bytes 786432 | tf_op jit(solution)/shard_map/all_to_all | solution.py:410
  22.5 37.0 %collective-permute-start.2 = (bf16[8,96,128]{2,1,0:T(8,128)(2,1)S(1)}, bf16[8,96,128]{2,1,0:T(8,128)(2,1)S(1)}, u32[]{:S(2)}, u32[]{:S(2)}) collective-permute-start(bf16[8,96,128]{2,1,0:T(8,128)(2,1)S(1)} %get-tuple-element.33.own_ref), channel_id=1, source_target_pairs={{0,64},{64,0},{1,65},{65,1},{2,66},{66,2},{3,67},{67,3},{4,68},{68... | collective-permute-start | bytes 589832 | tf_op jit(solution)/shard_map/ppermute | solution.py:418
  33.5 65.8 %collective-permute-start.3 = (bf16[8,96,128]{2,1,0:T(8,128)(2,1)S(1)}, bf16[8,96,128]{2,1,0:T(8,128)(2,1)S(1)}, u32[]{:S(2)}, u32[]{:S(2)}) collective-permute-start(bf16[8,96,128]{2,1,0:T(8,128)(2,1)S(1)} %get-tuple-element.38.own_ref), channel_id=1, source_target_pairs={{0,64},{64,0},{1,65},{65,1},{2,66},{66,2},{3,67},{67,3},{4,68},{68... | collective-permute-start | bytes 589832 | tf_op jit(solution)/shard_map/ppermute | solution.py:419
  36.5 23.0 %copy-start.16 = (bf16[8,90,128]{2,1,0:T(8,128)(2,1)}, bf16[8,90,128]{2,1,0:T(8,128)(2,1)S(1)}, u32[]{:S(2)}) copy-start(bf16[8,90,128]{2,1,0:T(8,128)(2,1)S(1)} %copy.45) | copy-start | bytes 552964
  36.7 21.7 %collective-permute-start = (bf16[8,16,128]{2,1,0:T(8,128)(2,1)S(1)}, bf16[8,16,128]{2,1,0:T(8,128)(2,1)S(1)}, u32[]{:S(2)}, u32[]{:S(2)}) collective-permute-start(bf16[8,16,128]{2,1,0:T(8,128)(2,1)S(1)} %get-tuple-element.102), channel_id=1, source_target_pairs={{0,480},{32,64},{64,32},{96,128},{128,96},{160,192},{192,160},{224... | collective-permute-start | bytes 98312 | tf_op jit(solution)/shard_map/ppermute | solution.py:45
  49.0 9.4 %collective-permute-start.1 = (bf16[8,16,128]{2,1,0:T(8,128)(2,1)S(1)}, bf16[8,16,128]{2,1,0:T(8,128)(2,1)S(1)}, u32[]{:S(2)}, u32[]{:S(2)}) collective-permute-start(bf16[8,16,128]{2,1,0:T(8,128)(2,1)S(1)} %get-tuple-element.103), channel_id=1, source_target_pairs={{0,32},{32,0},{1,33},{33,1},{2,34},{34,2},{3,35},{35,3},{4,36},{36... | collective-permute-start | bytes 98312 | tf_op jit(solution)/shard_map/ppermute | solution.py:43
  51.7 14.8 %all-to-all-start.1 = ((bf16[8,192,128]{2,1,0:T(8,128)(2,1)}), bf16[8,192,128]{2,1,0:T(8,128)(2,1)S(1)}, u32[]{:S(2)}, u32[]{:S(2)}) async-start(bf16[8,192,128]{2,1,0:T(8,128)(2,1)} %fusion.2), calls=%async_computation.1 | async-start | bytes 786432 | tf_op jit(solution)/shard_map/all_to_all | solution.py:410
  58.5 8.1 %copy-start.11 = (bf16[128,128]{1,0:T(8,128)(2,1)S(1)}, bf16[128,128]{1,0:T(8,128)(2,1)}, u32[]{:S(2)}) copy-start(bf16[128,128]{1,0:T(8,128)(2,1)} %proj_ref.3) | copy-start | bytes 98308
  58.5 8.0 %copy-start.19 = (bf16[8,5,128]{2,1,0:T(8,128)(2,1)}, bf16[8,5,128]{2,1,0:T(8,128)(2,1)S(1)}, u32[]{:S(2)}) copy-start(bf16[8,5,128]{2,1,0:T(8,128)(2,1)S(1)} %slice.230) | copy-start | bytes 30724
  60.2 28.8 %collective-permute-start.5 = (bf16[6,128,128]{2,1,0:T(8,128)(2,1)}, bf16[6,128,128]{2,1,0:T(8,128)(2,1)}, u32[]{:S(2)}, u32[]{:S(2)}) collective-permute-start(bf16[6,128,128]{2,1,0:T(8,128)(2,1)} %get-tuple-element.83), channel_id=1, source_target_pairs={{1,0},{2,1},{3,2},{4,3},{5,4},{6,5},{7,6},{8,7},{9,8},{10,9},{11,1... | collective-permute-start | bytes 589832 | tf_op jit(solution)/shard_map/ppermute | solution.py:52
  61.5 28.6 %collective-permute-start.4 = (bf16[6,128,128]{2,1,0:T(8,128)(2,1)S(1)}, bf16[6,128,128]{2,1,0:T(8,128)(2,1)S(1)}, u32[]{:S(2)}, u32[]{:S(2)}) collective-permute-start(bf16[6,128,128]{2,1,0:T(8,128)(2,1)S(1)} %get-tuple-element.82), channel_id=1, source_target_pairs={{0,1},{1,2},{2,3},{3,4},{4,5},{5,6},{6,7},{7,8},{8,9},{9,10},{10,1... | collective-permute-start | bytes 589832 | tf_op jit(solution)/shard_map/ppermute | solution.py:51
  89.0 4.4 %copy-start = (bf16[768,256]{1,0:T(8,128)(2,1)}, bf16[768,256]{1,0:T(8,128)(2,1)S(1)}, u32[]{:S(2)}) copy-start(bf16[768,256]{1,0:T(8,128)(2,1)S(1)} %get-tuple-element.37.refs_2_) | copy-start | bytes 1179652
  95.0 30.3 %all-to-all-start.2 = ((bf16[8,96,128]{2,1,0:T(8,128)(2,1)}), bf16[8,96,128]{2,1,0:T(8,128)(2,1)}, u32[]{:S(2)}, u32[]{:S(2)}) async-start(bf16[8,96,128]{2,1,0:T(8,128)(2,1)} %get-tuple-element.44), calls=%async_computation.2 | async-start | bytes 393216 | tf_op jit(solution)/shard_map/all_to_all | solution.py:410
  99.3 21.9 %copy-start.1 = (bf16[768,256]{1,0:T(8,128)(2,1)S(1)}, bf16[768,256]{1,0:T(8,128)(2,1)}, u32[]{:S(2)}) copy-start(bf16[768,256]{1,0:T(8,128)(2,1)} %copy-done) | copy-start | bytes 1179652
  99.3 21.9 %copy-start.3 = (bf16[768,128]{1,0:T(8,128)(2,1)S(1)}, bf16[768,128]{1,0:T(8,128)(2,1)}, u32[]{:S(2)}) copy-start(bf16[768,128]{1,0:T(8,128)(2,1)} %copy-done.2) | copy-start | bytes 589828
  99.3 21.9 %copy-start.4 = (bf16[128,384]{1,0:T(8,128)(2,1)S(1)}, bf16[128,384]{1,0:T(8,128)(2,1)}, u32[]{:S(2)}) copy-start(bf16[128,384]{1,0:T(8,128)(2,1)} %refs_7_.1) | copy-start | bytes 294916
  121.2 3.4 %copy-start.17 = (bf16[8,90,128]{2,1,0:T(8,128)(2,1)S(1)}, bf16[8,90,128]{2,1,0:T(8,128)(2,1)}, u32[]{:S(2)}) copy-start(bf16[8,90,128]{2,1,0:T(8,128)(2,1)} %copy-done.16) | copy-start | bytes 552964
  124.5 48.4 %copy-start.25 = (bf16[112]{0:T(256)(128)(2,1)S(1)}, bf16[112]{0:T(256)(128)(2,1)}, u32[]{:S(2)}) copy-start(bf16[112]{0:T(256)(128)(2,1)} %pad.47.clone) | copy-start | bytes 676
  125.4 17.0 %collective-permute-start.6 = (bf16[8,96,128]{2,1,0:T(8,128)(2,1)}, bf16[8,96,128]{2,1,0:T(8,128)(2,1)S(1)}, u32[]{:S(2)}, u32[]{:S(2)}) collective-permute-start(bf16[8,96,128]{2,1,0:T(8,128)(2,1)} %all-to-all-done.2), channel_id=1, source_target_pairs={{0,64},{64,0},{1,65},{65,1},{2,66},{66,2},{3,67},{67,3},{4,68},{68... | collective-permute-start | bytes 589832 | tf_op jit(solution)/shard_map/ppermute | solution.py:448
  142.3 29.6 %collective-permute-start.7 = (bf16[8,96,128]{2,1,0:T(8,128)(2,1)}, bf16[8,96,128]{2,1,0:T(8,128)(2,1)S(1)}, u32[]{:S(2)}, u32[]{:S(2)}) collective-permute-start(bf16[8,96,128]{2,1,0:T(8,128)(2,1)} %copy-done.10), channel_id=1, source_target_pairs={{0,64},{64,0},{1,65},{65,1},{2,66},{66,2},{3,67},{67,3},{4,68},{68... | collective-permute-start | bytes 589832 | tf_op jit(solution)/shard_map/ppermute | solution.py:454
  155.7 29.8 %copy-start.18 = (bf16[8,128,128]{2,1,0:T(8,128)(2,1)S(1)}, bf16[8,128,128]{2,1,0:T(8,128)(2,1)}, u32[]{:S(2)}) copy-start(bf16[8,128,128]{2,1,0:T(8,128)(2,1)} %pad_maximum_fusion.10) | copy-start | bytes 786436
  173.7 11.8 %all-to-all-start.3 = ((bf16[8,112,128]{2,1,0:T(8,128)(2,1)}), bf16[8,112,128]{2,1,0:T(8,128)(2,1)S(1)}, u32[]{:S(2)}, u32[]{:S(2)}) async-start(bf16[8,112,128]{2,1,0:T(8,128)(2,1)} %bitcast.4), calls=%async_computation.3 | async-start | bytes 458752 | tf_op jit(solution)/shard_map/all_to_all | solution.py:467
  185.6 6.8 %collective-permute-start.9 = (bf16[6,112,128]{2,1,0:T(8,128)(2,1)S(1)}, bf16[6,112,128]{2,1,0:T(8,128)(2,1)S(1)}, u32[]{:S(2)}, u32[]{:S(2)}) collective-permute-start(bf16[6,112,128]{2,1,0:T(8,128)(2,1)S(1)} %pad_maximum_fusion.16), channel_id=1, source_target_pairs={{1,0},{2,1},{3,2},{4,3},{5,4},{6,5},{7,6},{8,7},{9,8},{10,9},{11,1... | collective-permute-start | bytes 516104 | tf_op jit(solution)/shard_map/ppermute | solution.py:52
  187.0 6.7 %copy-start.7 = (bf16[3,3,128,128]{3,2,1,0:T(8,128)(2,1)S(1)}, bf16[3,3,128,128]{3,2,1,0:T(8,128)(2,1)}, u32[]{:S(2)}) copy-start(bf16[3,3,128,128]{3,2,1,0:T(8,128)(2,1)} %near_ref.3) | copy-start | bytes 884740
  187.0 6.7 %copy-start.9 = (bf16[3,3,128,128]{3,2,1,0:T(8,128)(2,1)S(1)}, bf16[3,3,128,128]{3,2,1,0:T(8,128)(2,1)}, u32[]{:S(2)}) copy-start(bf16[3,3,128,128]{3,2,1,0:T(8,128)(2,1)} %dil_ref.1) | copy-start | bytes 884740
  187.0 6.7 %copy-start.13 = (f32[10,112,128]{2,1,0:T(8,128)S(1)}, f32[10,112,128]{2,1,0:T(8,128)}, u32[]{:S(2)}) copy-start(f32[10,112,128]{2,1,0:T(8,128)} %copy-done.12) | copy-start | bytes 1720324
  187.0 6.7 %copy-start.15 = (bf16[16,112,128]{2,1,0:T(8,128)(2,1)S(1)}, bf16[16,112,128]{2,1,0:T(8,128)(2,1)}, u32[]{:S(2)}) copy-start(bf16[16,112,128]{2,1,0:T(8,128)(2,1)} %copy-done.14) | copy-start | bytes 1376260
  187.0 6.5 %collective-permute-start.8 = (bf16[6,112,128]{2,1,0:T(8,128)(2,1)S(1)}, bf16[6,112,128]{2,1,0:T(8,128)(2,1)S(1)}, u32[]{:S(2)}, u32[]{:S(2)}) collective-permute-start(bf16[6,112,128]{2,1,0:T(8,128)(2,1)S(1)} %pad_maximum_fusion.15), channel_id=1, source_target_pairs={{0,1},{1,2},{2,3},{3,4},{4,5},{5,6},{6,7},{7,8},{8,9},{9,10},{10,1... | collective-permute-start | bytes 516104 | tf_op jit(solution)/shard_map/ppermute | solution.py:51
  274.2 19.8 %all-to-all-start.7 = ((bf16[32,88,128]{2,1,0:T(8,128)(2,1)}), bf16[32,88,128]{2,1,0:T(8,128)(2,1)S(1)}, u32[]{:S(2)}, u32[]{:S(2)}) async-start(bf16[32,88,128]{2,1,0:T(8,128)(2,1)} %broadcast_in_dim.31), calls=%async_computation.7 | async-start | bytes 1441792 | tf_op jit(solution)/shard_map/all_to_all | solution.py:395
  (10 other events, 16.2 us)

commit v4 on v3

--- a/solution.py
+++ b/solution.py
@@ -409,48 +409,51 @@
         grown = [jnp.pad(f, ((0, 0), (0, GROWN - f.shape[1]), (0, 0))) for f in fields]
         return lax.all_to_all(jnp.concatenate(grown, axis=1), PLANE, 0, 0, tiled=True)
 
+    blank = jnp.zeros((rows, 1, channels), features.dtype)
+    low, high = exchange_lon(
+        jnp.concatenate([features[:, :10], cotangent[:, :EDGE], blank], axis=1),
+        jnp.concatenate([features[:, -10:], cotangent[:, -EDGE:], blank], axis=1),
+    )
+    low, high, attn_keys, attn_values = lax.optimization_barrier(
+        (low, high, attn_keys, attn_values)
+    )
+
     side = channels // 2
     kv_own = to_rows(
         jnp.concatenate([attn_keys[..., :side], attn_values[..., :side]], axis=2),
         jnp.concatenate([attn_values[..., side:], attn_keys[..., side:]], axis=2),
     )
+
+    feat_x = jnp.concatenate(
+        [low[:, :10], features, high[:, :10], jnp.zeros((rows, 18, channels), features.dtype)],
+        axis=1,
+    )
+    cot_x = jnp.concatenate(
+        [low[:, 10:15], cotangent, high[:, 10:15], jnp.zeros((rows, 28, channels), features.dtype)],
+        axis=1,
+    )
+    low, high = exchange_lat(
+        jnp.concatenate([feat_x[-5:], cot_x[-1:]], axis=0),
+        jnp.concatenate([feat_x[:5], cot_x[:1]], axis=0),
+    )
+    low, high, kv_own, queries = lax.optimization_barrier((low, high, kv_own, queries))
     kv_one, kv_two = kv_own[:, :GROWN], kv_own[:, GROWN:]
     far_one = lax.ppermute(kv_one, "zh", SWAP)
     far_two = lax.ppermute(kv_two, "zh", SWAP)
-
-    features, cotangent, kv_one, kv_two = lax.optimization_barrier(
-        (features, cotangent, kv_one, kv_two)
-    )
-    blank = jnp.zeros((rows, 1, channels), features.dtype)
-    low, high = exchange_lon(
-        jnp.concatenate([features[:, :10], cotangent[:, :EDGE], blank], axis=1),
-        jnp.concatenate([features[:, -10:], cotangent[:, -EDGE:], blank], axis=1),
-    )
     qc_own = to_rows(queries, cotangent)
-    feat_x = jnp.concatenate(
-        [low[:, :10], features, high[:, :10], jnp.zeros((rows, 18, channels), features.dtype)],
-        axis=1,
-    )
-    cot_x = jnp.concatenate(
-        [low[:, 10:15], cotangent, high[:, 10:15], jnp.zeros((rows, 28, channels), features.dtype)],
-        axis=1,
-    )
-    feat_x, far_one = lax.optimization_barrier((feat_x, far_one))
-    low, high = exchange_lat(
-        jnp.concatenate([feat_x[-5:], cot_x[-1:]], axis=0),
-        jnp.concatenate([feat_x[:5], cot_x[:1]], axis=0),
-    )
     feat_x = jnp.concatenate([low[:5], feat_x, high[:5]], axis=0)
     cot_near = jnp.concatenate([low[5:], cot_x, high[5:]], axis=0)[:, :112]
 
     hidden_two, hidden_one, near_slope, wide_slope = forward(lat_at, feat_x, conv_near, conv_wide)
-    hid_own = to_rows(hidden_two)
-    hid_far = lax.ppermute(hid_own, "zh", SWAP)
+    hid_far = lax.ppermute(hidden_two, "zh", SWAP)
+    far_one, hidden_two = lax.optimization_barrier((far_one, hidden_two))
 
     first = attention(qc_own, kv_one, far_one, proj_out, (0, HEADS // 2))
+    first, kv_two = lax.optimization_barrier((first, kv_two))
     second = attention(qc_own, kv_two, far_two, proj_out, (HEADS // 2, HEADS))
     own_part, far_part, sent, out_term, own_qkv, far_kv = combine(first, second, qc_own, proj_qkv)
     sent, hid_far = lax.optimization_barrier((sent, hid_far))
+    hid_rows = to_rows(hidden_two, hid_far)
     from_far = lax.ppermute(sent, "zh", SWAP)
     whole = (own_part + from_far.astype(jnp.float32)).astype(jnp.bfloat16)
     whole = whole.reshape(4, 2, GROWN, channels)
@@ -465,8 +468,8 @@
     blank = jnp.zeros((4, 2, 12, channels), jnp.bfloat16)
     attn_x = jnp.concatenate([left, whole[:, :, :COLS], right, blank], axis=2)
     attn_x = lax.all_to_all(attn_x.reshape(8, 112, channels), PLANE, 0, 0, tiled=True)
-    hid_flat = hid_own.reshape(-1, channels)
-    far_flat = hid_far.reshape(-1, channels)
+    hid_flat = hid_rows[:, :GROWN].reshape(-1, channels)
+    far_flat = hid_rows[:, GROWN:].reshape(-1, channels)
     query_term = contract_rows(hid_flat, own_qkv[:, :channels])
     kv_term = contract_rows(hid_flat, own_qkv[:, channels:]) + contract_rows(far_flat, far_kv)
 

time: 298 us -> 262 us (0.88)
  blocking collectives: 74.1 us -> 56.3 us
  waiting for transfers between devices: 51.3 us -> 44.5 us
  starting transfers between devices: 94.1 us -> 87.7 us
  local copies, waits for them, and re-layouts: 14.3 us -> 10.6 us
    all_to_all x1, blocking collectives: 35.1 us -> 22.9 us  [reduce_all(): lax.all_to_all(terms.reshape(32, part, channels), ('x', 'y', 'core'), 0,...]
    all_to_all x3, waiting for transfers between devices: 7.3 us -> 0.01 us  [to_rows(): lax.all_to_all(jnp.concatenate(grown, axis=1), PLANE, 0, 0, tiled=True)]
    ppermute x2, waiting for transfers between devices: 1.21 us -> 7.65 us  [exchange_lat(): high = lax.ppermute(top, LAT_AXES, [(b, a) for a, b in chain])]
    all_to_all x1, blocking collectives: 25.2 us -> 19.4 us  [reduce_all(): band = lax.all_to_all(band, ('zh', 'zl'), 0, 0, tiled=True)]
    ppermute x1, starting transfers between devices: 12.1 us -> 7.22 us  [on_device(): from_far = lax.ppermute(sent, 'zh', SWAP)]
    ppermute x1, starting transfers between devices: 12.3 us -> 16.8 us  [exchange_lon(): outer = lax.ppermute(jnp.where(at_zero, left, right), LON_AXES, pairs)]
    ppermute x1, waiting for transfers between devices: 16.3 us -> 11.9 us  [on_device(): from_far = lax.ppermute(sent, 'zh', SWAP)]
    ppermute x2, starting transfers between devices: 9.08 us -> 4.71 us  [exchange_lat(): low = lax.ppermute(bottom, LAT_AXES, chain)]
  transfers between devices with their start and end apart: 15 -> 15, of which waited for: 8 -> 9; matrix products, arithmetic and copies ran while one was open for 3% -> 4% of each run, Pallas kernels for 16% -> 18%
where the time goes in v4:
time: 262 us; the launch traced here: 261 us
  starting transfers between devices  87.7 us (33%)
  blocking collectives  56.3 us (21%)
  Pallas kernels  49.6 us (19%)
  waiting for transfers between devices  44.5 us (17%)
  local copies, waits for them, and re-layouts  10.6 us (4%)
  other arithmetic  10.2 us (4%)
    pallas_call x2, Pallas kernels, attention(): pl.pallas_call(functools.partial(attend_rows, heads=heads), out_shape=[ja...  43.6 us
    all_to_all x1, blocking collectives, reduce_all(): lax.all_to_all(terms.reshape(32, part, channels), ('x', 'y', 'core'), 0,...  22.9 us
    all_to_all x1, blocking collectives, reduce_all(): band = lax.all_to_all(band, ('zh', 'zl'), 0, 0, tiled=True)  19.4 us
    ppermute x1, starting transfers between devices, exchange_lon(): outer = lax.ppermute(jnp.where(at_zero, left, right), LON_AXES, pairs)  16.8 us
    all_to_all x3, starting transfers between devices, to_rows(): lax.all_to_all(jnp.concatenate(grown, axis=1), PLANE, 0, 0, tiled=True)  15.7 us
    all_to_all x1, blocking collectives, reduce_all(): lax.all_to_all(jnp.broadcast_to(band[None], (16, piece)), ('zh', 'zl'), 0...  13.9 us
    all_to_all x1, waiting for transfers between devices, reduce_all(): lax.all_to_all(jnp.broadcast_to(band[None], (32, part, channels)), ('x',...  12.8 us
    ppermute x1, waiting for transfers between devices, on_device(): from_far = lax.ppermute(sent, 'zh', SWAP)  11.9 us
  transfers between devices with their start and end apart: 15, of which 9 were waited for; matrix products, arithmetic and copies ran while one was open for 4% of the time, Pallas kernels for 18%

profile of v4, /device:TPU:1, one launch (start us, length us, event | category | flops | bytes accessed | tf_op | source)
XLA Modules:
  0.0 261.3 jit_solution(17817348373887956355)
XLA Ops:
  2.9 16.8 %collective-permute-start = (bf16[8,16,128]{2,1,0:T(8,128)(2,1)S(1)}, bf16[8,16,128]{2,1,0:T(8,128)(2,1)S(1)}, u32[]{:S(2)}, u32[]{:S(2)}) collective-permute-start(bf16[8,16,128]{2,1,0:T(8,128)(2,1)S(1)} %get-tuple-element.121), channel_id=1, source_target_pairs={{0,480},{32,64},{64,32},{96,128},{128,96},{160,192},{192,160},{224... | collective-permute-start | bytes 98312 | tf_op jit(solution)/shard_map/ppermute | solution.py:45
  19.7 3.9 %collective-permute-start.1 = (bf16[8,16,128]{2,1,0:T(8,128)(2,1)S(1)}, bf16[8,16,128]{2,1,0:T(8,128)(2,1)S(1)}, u32[]{:S(2)}, u32[]{:S(2)}) collective-permute-start(bf16[8,16,128]{2,1,0:T(8,128)(2,1)S(1)} %get-tuple-element.120), channel_id=1, source_target_pairs={{0,32},{32,0},{1,33},{33,1},{2,34},{34,2},{3,35},{35,3},{4,36},{36... | collective-permute-start | bytes 98312 | tf_op jit(solution)/shard_map/ppermute | solution.py:43
  25.9 4.7 %all-to-all-start = ((bf16[8,192,128]{2,1,0:T(8,128)(2,1)}), bf16[8,192,128]{2,1,0:T(8,128)(2,1)S(1)}, u32[]{:S(2)}, u32[]{:S(2)}) async-start(bf16[8,192,128]{2,1,0:T(8,128)(2,1)} %pad_maximum_fusion.3), calls=%async_computation | async-start | bytes 786432 | tf_op jit(solution)/shard_map/all_to_all | solution.py:410
  30.8 2.4 collective-permute-start.2
  33.2 1.3 collective-permute-start.3
  36.0 1.5 collective-permute-done.2
  37.5 3.8 %collective-permute-done.3 = bf16[6,128,128]{2,1,0:T(8,128)(2,1)S(1)} collective-permute-done((bf16[6,128,128]{2,1,0:T(8,128)(2,1)S(1)}, bf16[6,128,128]{2,1,0:T(8,128)(2,1)S(1)}, u32[]{:S(2)}, u32[]{:S(2)}) %collective-permute-start.3) | collective-permute-done | bytes 196640 | tf_op jit(solution)/shard_map/ppermute | solution.py:52
  41.4 11.2 %collective-permute-start.4 = (bf16[8,96,128]{2,1,0:T(8,128)(2,1)S(1)}, bf16[8,96,128]{2,1,0:T(8,128)(2,1)S(1)}, u32[]{:S(2)}, u32[]{:S(2)}) collective-permute-start(bf16[8,96,128]{2,1,0:T(8,128)(2,1)S(1)} %get-tuple-element.99.own_ref), channel_id=1, source_target_pairs={{0,64},{64,0},{1,65},{65,1},{2,66},{66,2},{3,67},{67,3},{4,68},{68... | collective-permute-start | bytes 589832 | tf_op jit(solution)/shard_map/ppermute | solution.py:441
  53.4 6.0 %all-to-all-start.1 = ((bf16[8,192,128]{2,1,0:T(8,128)(2,1)}), bf16[8,192,128]{2,1,0:T(8,128)(2,1)S(1)}, u32[]{:S(2)}, u32[]{:S(2)}) async-start(bf16[8,192,128]{2,1,0:T(8,128)(2,1)} %fusion.2), calls=%async_computation.1 | async-start | bytes 786432 | tf_op jit(solution)/shard_map/all_to_all | solution.py:410
  59.4 2.9 %collective-permute-start.5 = (bf16[8,96,128]{2,1,0:T(8,128)(2,1)S(1)}, bf16[8,96,128]{2,1,0:T(8,128)(2,1)S(1)}, u32[]{:S(2)}, u32[]{:S(2)}) collective-permute-start(bf16[8,96,128]{2,1,0:T(8,128)(2,1)S(1)} %get-tuple-element.55.own_ref), channel_id=1, source_target_pairs={{0,64},{64,0},{1,65},{65,1},{2,66},{66,2},{3,67},{67,3},{4,68},{68... | collective-permute-start | bytes 589832 | tf_op jit(solution)/shard_map/ppermute | solution.py:442
  62.4 2.5 forward_block.1
  66.5 11.3 %collective-permute-start.6 = (bf16[8,96,128]{2,1,0:T(8,128)(2,1)S(1)}, bf16[8,96,128]{2,1,0:T(8,128)(2,1)}, u32[]{:S(2)}, u32[]{:S(2)}) collective-permute-start(bf16[8,96,128]{2,1,0:T(8,128)(2,1)S(1)} %get-tuple-element.68), channel_id=1, source_target_pairs={{0,64},{64,0},{1,65},{65,1},{2,66},{66,2},{3,67},{67,3},{4,68},{68... | collective-permute-start | bytes 589832 | tf_op jit(solution)/shard_map/ppermute | solution.py:448
  77.8 21.8 %attend_rows.2 = (bf16[768,128]{1,0:T(8,128)(2,1)S(1)}, bf16[768,384]{1,0:T(8,128)(2,1)S(1)}, bf16[768,256]{1,0:T(8,128)(2,1)S(1)}) custom-call(bf16[8,192,128]{2,1,0:T(8,128)(2,1)S(1)} %all-to-all-done.1.qc_ref.refs_6_, bf16[8,96,128]{2,1,0:T(8,128)(2,1)S(1)} %get-tuple-element.99.own_ref, bf16[8,96,128]{2,1,0:T(8,128)(2,1)S(1)} %collective-permute-done.4.far_ref, ...), custom_call_target="tpu_custom_call" | custom-call | flops 7247757312 | bytes 1572864 | tf_op jit(solution)/shard_map/attend_rows/pallas_call | solution.py:146
  99.6 4.2 %collective-permute-done.5.far_ref = bf16[8,96,128]{2,1,0:T(8,128)(2,1)S(1)} collective-permute-done((bf16[8,96,128]{2,1,0:T(8,128)(2,1)S(1)}, bf16[8,96,128]{2,1,0:T(8,128)(2,1)S(1)}, u32[]{:S(2)}, u32[]{:S(2)}) %collective-permute-start.5) | collective-permute-done | bytes 196640 | tf_op jit(solution)/shard_map/ppermute | solution.py:442
  103.8 21.8 %attend_rows.3 = (bf16[768,128]{1,0:T(8,128)(2,1)S(1)}, bf16[768,384]{1,0:T(8,128)(2,1)S(1)}, bf16[768,256]{1,0:T(8,128)(2,1)S(1)}) custom-call(bf16[8,192,128]{2,1,0:T(8,128)(2,1)S(1)} %all-to-all-done.1.qc_ref.refs_6_, bf16[8,96,128]{2,1,0:T(8,128)(2,1)S(1)} %get-tuple-element.55.own_ref, bf16[8,96,128]{2,1,0:T(8,128)(2,1)S(1)} %collective-permute-done.5.far_ref, ...), custom_call_target="tpu_custom_call" | custom-call | flops 7247757312 | bytes 1572864 | tf_op jit(solution)/shard_map/attend_rows/pallas_call | solution.py:146
  125.7 1.2 combine.1
  126.9 7.2 %collective-permute-start.7 = (bf16[8,96,128]{2,1,0:T(8,128)(2,1)}, bf16[8,96,128]{2,1,0:T(8,128)(2,1)}, u32[]{:S(2)}, u32[]{:S(2)}) collective-permute-start(bf16[8,96,128]{2,1,0:T(8,128)(2,1)} %get-tuple-element.60), channel_id=1, source_target_pairs={{0,64},{64,0},{1,65},{65,1},{2,66},{66,2},{3,67},{67,3},{4,68},{68... | collective-permute-start | bytes 589832 | tf_op jit(solution)/shard_map/ppermute | solution.py:457
  134.3 1.7 pad_maximum_fusion.4
  136.0 5.0 %all-to-all-start.3 = ((bf16[8,192,128]{2,1,0:T(8,128)(2,1)}), bf16[8,192,128]{2,1,0:T(8,128)(2,1)}, u32[]{:S(2)}, u32[]{:S(2)}) async-start(bf16[8,192,128]{2,1,0:T(8,128)(2,1)} %pad_maximum_fusion.4), calls=%async_computation.3 | async-start | bytes 786432 | tf_op jit(solution)/shard_map/all_to_all | solution.py:410
  141.0 11.9 %collective-permute-done.7 = bf16[8,96,128]{2,1,0:T(8,128)(2,1)} collective-permute-done((bf16[8,96,128]{2,1,0:T(8,128)(2,1)}, bf16[8,96,128]{2,1,0:T(8,128)(2,1)}, u32[]{:S(2)}, u32[]{:S(2)}) %collective-permute-start.7) | collective-permute-done | bytes 196640 | tf_op jit(solution)/shard_map/ppermute | solution.py:457
  155.6 5.1 %all-to-all-start.2 = ((bf16[8,112,128]{2,1,0:T(8,128)(2,1)}), bf16[8,112,128]{2,1,0:T(8,128)(2,1)S(1)}, u32[]{:S(2)}, u32[]{:S(2)}) async-start(bf16[8,112,128]{2,1,0:T(8,128)(2,1)} %bitcast.4), calls=%async_computation.2 | async-start | bytes 458752 | tf_op jit(solution)/shard_map/all_to_all | solution.py:470
  162.5 4.4 %all-to-all-done.2 = bf16[8,112,128]{2,1,0:T(8,128)(2,1)S(1)} async-done(((bf16[8,112,128]{2,1,0:T(8,128)(2,1)}), bf16[8,112,128]{2,1,0:T(8,128)(2,1)S(1)}, u32[]{:S(2)}, u32[]{:S(2)}) %all-to-all-start.2) | async-done | bytes 229408 | tf_op jit(solution)/shard_map/all_to_all | solution.py:470
  167.0 2.3 collective-permute-start.8
  169.3 1.3 collective-permute-start.9
  170.7 1.2 collective-permute-done.8
  171.9 3.8 %collective-permute-done.9 = bf16[6,112,128]{2,1,0:T(8,128)(2,1)S(1)} collective-permute-done((bf16[6,112,128]{2,1,0:T(8,128)(2,1)S(1)}, bf16[6,112,128]{2,1,0:T(8,128)(2,1)S(1)}, u32[]{:S(2)}, u32[]{:S(2)}) %collective-permute-start.9) | collective-permute-done | bytes 172064 | tf_op jit(solution)/shard_map/ppermute | solution.py:52
  176.0 2.3 backward_block.1
  178.4 22.9 %all_to_all.46 = bf16[32,88,128]{2,1,0:T(8,128)(2,1)S(1)} all-to-all(bf16[32,88,128]{2,1,0:T(8,128)(2,1)S(1)} %bitcast.22), channel_id=1, replica_groups=mesh['x'=4,'zh'=2,'core'=2,'zl'=8,'y'=4] {'x','y','core'}, dimensions={0} | all-to-all | bytes 1441792 | tf_op jit(solution)/shard_map/all_to_all | solution.py:386
  203.0 19.4 %all_to_all.47 = bf16[16,2,352]{2,1,0:T(2,128)(2,1)S(1)} all-to-all(bf16[16,2,352]{2,1,0:T(2,128)(2,1)S(1)} %reshape.84), channel_id=1, replica_groups=mesh['x'=4,'zh'=2,'core'=2,'zl'=8,'y'=4] {'zh','zl'}, dimensions={0} | all-to-all | bytes 45056 | tf_op jit(solution)/shard_map/all_to_all | solution.py:390
  223.5 13.9 %all_to_all.48 = bf16[16,2,352]{2,1,0:T(2,128)(2,1)S(1)} all-to-all(bf16[16,2,352]{2,1,0:T(2,128)(2,1)S(1)} %reshape.86), channel_id=1, replica_groups=mesh['x'=4,'zh'=2,'core'=2,'zl'=8,'y'=4] {'zh','zl'}, dimensions={0} | all-to-all | bytes 45056 | tf_op jit(solution)/shard_map/all_to_all | solution.py:392
  238.7 6.3 %all-to-all-start.7 = ((bf16[32,88,128]{2,1,0:T(8,128)(2,1)}), bf16[32,88,128]{2,1,0:T(8,128)(2,1)S(1)}, u32[]{:S(2)}, u32[]{:S(2)}) async-start(bf16[32,88,128]{2,1,0:T(8,128)(2,1)} %broadcast_in_dim.31), calls=%async_computation.7 | async-start | bytes 1441792 | tf_op jit(solution)/shard_map/all_to_all | solution.py:395
  245.8 12.8 %all-to-all-done.7 = bf16[32,88,128]{2,1,0:T(8,128)(2,1)S(1)} async-done(((bf16[32,88,128]{2,1,0:T(8,128)(2,1)}), bf16[32,88,128]{2,1,0:T(8,128)(2,1)S(1)}, u32[]{:S(2)}, u32[]{:S(2)}) %all-to-all-start.7) | async-done | bytes 720928 | tf_op jit(solution)/shard_map/all_to_all | solution.py:395
  (131 shorter events, 20.7 us)
Async XLA Ops:
  0.6 23.9 %copy-start.17 = (bf16[8,90,128]{2,0,1:T(8,128)(2,1)S(1)}, bf16[8,90,128]{2,0,1:T(8,128)(2,1)}, u32[]{:S(2)}) copy-start(bf16[8,90,128]{2,0,1:T(8,128)(2,1)} %param.11) | copy-start | bytes 552964
  0.6 24.1 %copy-start.18 = (bf16[8,90,128]{2,0,1:T(8,128)(2,1)S(1)}, bf16[8,90,128]{2,0,1:T(8,128)(2,1)}, u32[]{:S(2)}) copy-start(bf16[8,90,128]{2,0,1:T(8,128)(2,1)} %param.12) | copy-start | bytes 552964
  1.7 51.0 %copy-start.10 = (bf16[8,90,128]{2,1,0:T(8,128)(2,1)}, bf16[8,90,128]{2,1,0:T(8,128)(2,1)S(1)}, u32[]{:S(2)}) copy-start(bf16[8,90,128]{2,1,0:T(8,128)(2,1)S(1)} %copy.41) | copy-start | bytes 552964
  2.9 20.8 %collective-permute-start = (bf16[8,16,128]{2,1,0:T(8,128)(2,1)S(1)}, bf16[8,16,128]{2,1,0:T(8,128)(2,1)S(1)}, u32[]{:S(2)}, u32[]{:S(2)}) collective-permute-start(bf16[8,16,128]{2,1,0:T(8,128)(2,1)S(1)} %get-tuple-element.121), channel_id=1, source_target_pairs={{0,480},{32,64},{64,32},{96,128},{128,96},{160,192},{192,160},{224... | collective-permute-start | bytes 98312 | tf_op jit(solution)/shard_map/ppermute | solution.py:45
  19.7 4.8 %collective-permute-start.1 = (bf16[8,16,128]{2,1,0:T(8,128)(2,1)S(1)}, bf16[8,16,128]{2,1,0:T(8,128)(2,1)S(1)}, u32[]{:S(2)}, u32[]{:S(2)}) collective-permute-start(bf16[8,16,128]{2,1,0:T(8,128)(2,1)S(1)} %get-tuple-element.120), channel_id=1, source_target_pairs={{0,32},{32,0},{1,33},{33,1},{2,34},{34,2},{3,35},{35,3},{4,36},{36... | collective-permute-start | bytes 98312 | tf_op jit(solution)/shard_map/ppermute | solution.py:43
  25.9 15.4 %all-to-all-start = ((bf16[8,192,128]{2,1,0:T(8,128)(2,1)}), bf16[8,192,128]{2,1,0:T(8,128)(2,1)S(1)}, u32[]{:S(2)}, u32[]{:S(2)}) async-start(bf16[8,192,128]{2,1,0:T(8,128)(2,1)} %pad_maximum_fusion.3), calls=%async_computation | async-start | bytes 786432 | tf_op jit(solution)/shard_map/all_to_all | solution.py:410
  30.7 10.5 %copy-start.13 = (bf16[8,5,128]{2,1,0:T(8,128)(2,1)}, bf16[8,5,128]{2,1,0:T(8,128)(2,1)S(1)}, u32[]{:S(2)}) copy-start(bf16[8,5,128]{2,1,0:T(8,128)(2,1)S(1)} %slice.181) | copy-start | bytes 30724
  30.8 21.8 %copy-start.19 = (bf16[8,90,128]{2,0,1:T(8,128)(2,1)S(1)}, bf16[8,90,128]{2,0,1:T(8,128)(2,1)}, u32[]{:S(2)}) copy-start(bf16[8,90,128]{2,0,1:T(8,128)(2,1)} %param.10) | copy-start | bytes 552964
  30.8 6.6 %collective-permute-start.2 = (bf16[6,128,128]{2,1,0:T(8,128)(2,1)S(1)}, bf16[6,128,128]{2,1,0:T(8,128)(2,1)S(1)}, u32[]{:S(2)}, u32[]{:S(2)}) collective-permute-start(bf16[6,128,128]{2,1,0:T(8,128)(2,1)S(1)} %get-tuple-element.101), channel_id=1, source_target_pairs={{0,1},{1,2},{2,3},{3,4},{4,5},{5,6},{6,7},{7,8},{8,9},{9,10},{10,1... | collective-permute-start | bytes 589832 | tf_op jit(solution)/shard_map/ppermute | solution.py:51
  33.2 8.0 %collective-permute-start.3 = (bf16[6,128,128]{2,1,0:T(8,128)(2,1)S(1)}, bf16[6,128,128]{2,1,0:T(8,128)(2,1)S(1)}, u32[]{:S(2)}, u32[]{:S(2)}) collective-permute-start(bf16[6,128,128]{2,1,0:T(8,128)(2,1)S(1)} %get-tuple-element.100), channel_id=1, source_target_pairs={{1,0},{2,1},{3,2},{4,3},{5,4},{6,5},{7,6},{8,7},{9,8},{10,9},{11,1... | collective-permute-start | bytes 589832 | tf_op jit(solution)/shard_map/ppermute | solution.py:52
  37.5 16.0 %copy-start.15 = (bf16[6,128,128]{2,1,0:T(8,128)(2,1)}, bf16[6,128,128]{2,1,0:T(8,128)(2,1)S(1)}, u32[]{:S(2)}) copy-start(bf16[6,128,128]{2,1,0:T(8,128)(2,1)S(1)} %collective-permute-done.2) | copy-start | bytes 589828
  41.3 12.2 %copy-start.16 = (bf16[6,128,128]{2,1,0:T(8,128)(2,1)}, bf16[6,128,128]{2,1,0:T(8,128)(2,1)S(1)}, u32[]{:S(2)}) copy-start(bf16[6,128,128]{2,1,0:T(8,128)(2,1)S(1)} %collective-permute-done.3) | copy-start | bytes 589828
  41.4 36.4 %collective-permute-start.4 = (bf16[8,96,128]{2,1,0:T(8,128)(2,1)S(1)}, bf16[8,96,128]{2,1,0:T(8,128)(2,1)S(1)}, u32[]{:S(2)}, u32[]{:S(2)}) collective-permute-start(bf16[8,96,128]{2,1,0:T(8,128)(2,1)S(1)} %get-tuple-element.99.own_ref), channel_id=1, source_target_pairs={{0,64},{64,0},{1,65},{65,1},{2,66},{66,2},{3,67},{67,3},{4,68},{68... | collective-permute-start | bytes 589832 | tf_op jit(solution)/shard_map/ppermute | solution.py:441
  53.4 9.0 %copy-start.1 = (bf16[3,3,128,128]{3,2,1,0:T(8,128)(2,1)S(1)}, bf16[3,3,128,128]{3,2,1,0:T(8,128)(2,1)}, u32[]{:S(2)}) copy-start(bf16[3,3,128,128]{3,2,1,0:T(8,128)(2,1)} %near_ref.3) | copy-start | bytes 884740
  53.4 9.0 %copy-start.3 = (bf16[3,3,128,128]{3,2,1,0:T(8,128)(2,1)S(1)}, bf16[3,3,128,128]{3,2,1,0:T(8,128)(2,1)}, u32[]{:S(2)}) copy-start(bf16[3,3,128,128]{3,2,1,0:T(8,128)(2,1)} %dil_ref.1) | copy-start | bytes 884740
  53.4 24.3 %all-to-all-start.1 = ((bf16[8,192,128]{2,1,0:T(8,128)(2,1)}), bf16[8,192,128]{2,1,0:T(8,128)(2,1)S(1)}, u32[]{:S(2)}, u32[]{:S(2)}) async-start(bf16[8,192,128]{2,1,0:T(8,128)(2,1)} %fusion.2), calls=%async_computation.1 | async-start | bytes 786432 | tf_op jit(solution)/shard_map/all_to_all | solution.py:410
  59.4 44.4 %collective-permute-start.5 = (bf16[8,96,128]{2,1,0:T(8,128)(2,1)S(1)}, bf16[8,96,128]{2,1,0:T(8,128)(2,1)S(1)}, u32[]{:S(2)}, u32[]{:S(2)}) collective-permute-start(bf16[8,96,128]{2,1,0:T(8,128)(2,1)S(1)} %get-tuple-element.55.own_ref), channel_id=1, source_target_pairs={{0,64},{64,0},{1,65},{65,1},{2,66},{66,2},{3,67},{67,3},{4,68},{68... | collective-permute-start | bytes 589832 | tf_op jit(solution)/shard_map/ppermute | solution.py:442
  62.4 15.4 %copy-start.5 = (bf16[128,128]{1,0:T(8,128)(2,1)S(1)}, bf16[128,128]{1,0:T(8,128)(2,1)}, u32[]{:S(2)}) copy-start(bf16[128,128]{1,0:T(8,128)(2,1)} %proj_ref.3) | copy-start | bytes 98308
  66.5 60.5 %collective-permute-start.6 = (bf16[8,96,128]{2,1,0:T(8,128)(2,1)S(1)}, bf16[8,96,128]{2,1,0:T(8,128)(2,1)}, u32[]{:S(2)}, u32[]{:S(2)}) collective-permute-start(bf16[8,96,128]{2,1,0:T(8,128)(2,1)S(1)} %get-tuple-element.68), channel_id=1, source_target_pairs={{0,64},{64,0},{1,65},{65,1},{2,66},{66,2},{3,67},{67,3},{4,68},{68... | collective-permute-start | bytes 589832 | tf_op jit(solution)/shard_map/ppermute | solution.py:448
  99.6 26.0 %copy-start = (bf16[128,384]{1,0:T(8,128)(2,1)S(1)}, bf16[128,384]{1,0:T(8,128)(2,1)}, u32[]{:S(2)}) copy-start(bf16[128,384]{1,0:T(8,128)(2,1)} %refs_7_.1) | copy-start | bytes 294916
  125.7 8.5 %copy-start.11 = (bf16[8,90,128]{2,1,0:T(8,128)(2,1)S(1)}, bf16[8,90,128]{2,1,0:T(8,128)(2,1)}, u32[]{:S(2)}) copy-start(bf16[8,90,128]{2,1,0:T(8,128)(2,1)} %copy-done.10) | copy-start | bytes 552964
  125.7 8.5 %copy-start.14 = (bf16[8,5,128]{2,1,0:T(8,128)(2,1)S(1)}, bf16[8,5,128]{2,1,0:T(8,128)(2,1)}, u32[]{:S(2)}) copy-start(bf16[8,5,128]{2,1,0:T(8,128)(2,1)} %copy-done.13) | copy-start | bytes 30724
  125.7 8.5 %slice-start = ((bf16[6,128,128]{2,1,0:T(8,128)(2,1)}), bf16[1,128,128]{2,1,0:T(8,128)(2,1)S(1)}, s32[]{:S(2)}) async-start(bf16[6,128,128]{2,1,0:T(8,128)(2,1)} %copy-done.15), calls=%async_computation.8 | async-start | bytes 65536 | tf_op jit(solution)/shard_map/slice | solution.py:445
  125.7 8.5 %slice-start.1 = ((bf16[6,128,128]{2,1,0:T(8,128)(2,1)}), bf16[1,128,128]{2,1,0:T(8,128)(2,1)S(1)}, s32[]{:S(2)}) async-start(bf16[6,128,128]{2,1,0:T(8,128)(2,1)} %copy-done.16), calls=%async_computation.9 | async-start | bytes 65536 | tf_op jit(solution)/shard_map/slice | solution.py:445
  126.9 26.0 %collective-permute-start.7 = (bf16[8,96,128]{2,1,0:T(8,128)(2,1)}, bf16[8,96,128]{2,1,0:T(8,128)(2,1)}, u32[]{:S(2)}, u32[]{:S(2)}) collective-permute-start(bf16[8,96,128]{2,1,0:T(8,128)(2,1)} %get-tuple-element.60), channel_id=1, source_target_pairs={{0,64},{64,0},{1,65},{65,1},{2,66},{66,2},{3,67},{67,3},{4,68},{68... | collective-permute-start | bytes 589832 | tf_op jit(solution)/shard_map/ppermute | solution.py:457
  134.3 20.5 %copy-start.20 = (bf16[112]{0:T(256)(128)(2,1)S(1)}, bf16[112]{0:T(256)(128)(2,1)}, u32[]{:S(2)}) copy-start(bf16[112]{0:T(256)(128)(2,1)} %pad.49.clone) | copy-start | bytes 676
  136.0 19.6 %all-to-all-start.3 = ((bf16[8,192,128]{2,1,0:T(8,128)(2,1)}), bf16[8,192,128]{2,1,0:T(8,128)(2,1)}, u32[]{:S(2)}, u32[]{:S(2)}) async-start(bf16[8,192,128]{2,1,0:T(8,128)(2,1)} %pad_maximum_fusion.4), calls=%async_computation.3 | async-start | bytes 786432 | tf_op jit(solution)/shard_map/all_to_all | solution.py:410
  155.6 11.2 %all-to-all-start.2 = ((bf16[8,112,128]{2,1,0:T(8,128)(2,1)}), bf16[8,112,128]{2,1,0:T(8,128)(2,1)S(1)}, u32[]{:S(2)}, u32[]{:S(2)}) async-start(bf16[8,112,128]{2,1,0:T(8,128)(2,1)} %bitcast.4), calls=%async_computation.2 | async-start | bytes 458752 | tf_op jit(solution)/shard_map/all_to_all | solution.py:470
  167.0 5.0 %collective-permute-start.8 = (bf16[6,112,128]{2,1,0:T(8,128)(2,1)S(1)}, bf16[6,112,128]{2,1,0:T(8,128)(2,1)S(1)}, u32[]{:S(2)}, u32[]{:S(2)}) collective-permute-start(bf16[6,112,128]{2,1,0:T(8,128)(2,1)S(1)} %pad_maximum_fusion.17), channel_id=1, source_target_pairs={{0,1},{1,2},{2,3},{3,4},{4,5},{5,6},{6,7},{7,8},{8,9},{9,10},{10,1... | collective-permute-start | bytes 516104 | tf_op jit(solution)/shard_map/ppermute | solution.py:51
  169.3 6.5 %collective-permute-start.9 = (bf16[6,112,128]{2,1,0:T(8,128)(2,1)S(1)}, bf16[6,112,128]{2,1,0:T(8,128)(2,1)S(1)}, u32[]{:S(2)}, u32[]{:S(2)}) collective-permute-start(bf16[6,112,128]{2,1,0:T(8,128)(2,1)S(1)} %pad_maximum_fusion.18), channel_id=1, source_target_pairs={{1,0},{2,1},{3,2},{4,3},{5,4},{6,5},{7,6},{8,7},{9,8},{10,9},{11,1... | collective-permute-start | bytes 516104 | tf_op jit(solution)/shard_map/ppermute | solution.py:52
  170.7 5.3 %copy-start.2 = (bf16[3,3,128,128]{3,2,1,0:T(8,128)(2,1)S(1)}, bf16[3,3,128,128]{3,2,1,0:T(8,128)(2,1)}, u32[]{:S(2)}) copy-start(bf16[3,3,128,128]{3,2,1,0:T(8,128)(2,1)} %near_ref.3) | copy-start | bytes 884740
  238.7 19.9 %all-to-all-start.7 = ((bf16[32,88,128]{2,1,0:T(8,128)(2,1)}), bf16[32,88,128]{2,1,0:T(8,128)(2,1)S(1)}, u32[]{:S(2)}, u32[]{:S(2)}) async-start(bf16[32,88,128]{2,1,0:T(8,128)(2,1)} %broadcast_in_dim.31), calls=%async_computation.7 | async-start | bytes 1441792 | tf_op jit(solution)/shard_map/all_to_all | solution.py:395
  (6 other events, 22.6 us)

commit v5 on v4

--- a/solution.py
+++ b/solution.py
@@ -53,8 +53,9 @@
     return low, high
 
 
-def attend_rows(qc_ref, own_ref, far_ref, proj_ref, mixed_ref, grad_ref, away_ref,
-                out_s, keep_s, grad_s, pair_s, value_s, key_g, value_g, query_g, mixed_g, *, heads):
+def attend_rows(*refs, heads, last):
+    qc_ref, own_ref, far_ref, proj_ref = refs[:4]
+    out_s, keep_s, grad_s, pair_s, value_s, key_g, value_g, query_g, mixed_g = refs[-9:]
     blocks, wide, channels = own_ref.shape
     rows = blocks * wide
     cols = 2 * rows
@@ -86,68 +87,109 @@
         keys_h = jnp.where(here_k, pair_s[...], spare).astype(low)
         ones = jnp.where((lane_k == first) | (lane_k == first + 1), 1.0, 0.0)
         values_h = jnp.where(here_k, value_s[...], ones).astype(low)
-        query_n, dout_n = [], []
-        for i in range(rows // chunk):
-            at = i * chunk
-            query = rows_of(qc_ref, 0)[at : at + chunk].astype(jnp.float32) * 0.25
+        spots = [slice(at, at + chunk) for at in range(0, rows, chunk)]
+        queries, douts, shares, query_n, dout_n = [], [], [], [], []
+        for spot in spots:
+            query = rows_of(qc_ref, 0)[spot].astype(jnp.float32) * 0.25
             query_h = jnp.where(here_q, query, jnp.where(lane_q == first, 1.0, 0.0)).astype(low)
-            dout = out_s[at : at + chunk, :].astype(low).astype(jnp.float32)
-            dout = jnp.where(here_q, dout, 0.0)
+            queries.append(jnp.where(here_q, query, 0.0))
             scores = lax.dot_general(
                 query_h, keys_h, (((1,), (1,)), ((), ())), preferred_element_type=jnp.float32
             )
             top = jnp.max(scores, axis=1, keepdims=True)
-            raised = jnp.exp(scores - top).astype(low)
-            keep_s[at : at + chunk, :] = raised
-            mixed = jnp.dot(raised, values_h, preferred_element_type=jnp.float32)
+            keep_s[spot, :] = jnp.exp(scores - top).astype(low)
+        for spot in spots:
+            dout = out_s[spot, :].astype(low).astype(jnp.float32)
+            dout = jnp.where(here_q, dout, 0.0)
+            mixed = jnp.dot(keep_s[spot, :], values_h, preferred_element_type=jnp.float32)
             total = jnp.sum(jnp.where(lane_q == first, mixed, 0.0), axis=1, keepdims=True)
             share = 1.0 / total
             mixed = jnp.where(here_q, mixed * share, 0.0)
-            mixed_g[at : at + chunk, :] += mixed
+            mixed_g[spot, :] += mixed
             delta = jnp.sum(dout * mixed, axis=1, keepdims=True)
             high = delta.astype(low).astype(jnp.float32)
-            dout_x = jnp.where(
-                lane_q == first, -high, jnp.where(lane_q == first + 1, high - delta, dout)
-            ).astype(low)
+            douts.append(
+                jnp.where(
+                    lane_q == first, -high, jnp.where(lane_q == first + 1, high - delta, dout)
+                ).astype(low)
+            )
+            shares.append(share)
+            dout_n.append((dout * share).astype(low))
+        value_g[...] += lax.dot_general(
+            keep_s[...], jnp.concatenate(dout_n, axis=0), (((0,), (0,)), ((), ())),
+            preferred_element_type=jnp.float32,
+        )
+        for spot, dout_x in zip(spots, douts):
             prob_grad = lax.dot_general(
                 dout_x, values_h, (((1,), (1,)), ((), ())), preferred_element_type=jnp.float32
             )
-            score_grad = raised * prob_grad.astype(low)
-            grad_s[at : at + chunk, :] = score_grad
-            query_g[at : at + chunk, :] += (
-                jnp.dot(score_grad, keys_h, preferred_element_type=jnp.float32) * (0.25 * share)
+            grad_s[spot, :] = keep_s[spot, :] * prob_grad.astype(low)
+        for spot, query, share in zip(spots, queries, shares):
+            query_g[spot, :] += (
+                jnp.dot(grad_s[spot, :], keys_h, preferred_element_type=jnp.float32)
+                * (0.25 * share)
             )
-            query_n.append((jnp.where(here_q, query, 0.0) * share).astype(low))
-            dout_n.append((dout * share).astype(low))
+            query_n.append((query * share).astype(low))
         key_g[...] += lax.dot_general(
             grad_s[...], jnp.concatenate(query_n, axis=0), (((0,), (0,)), ((), ())),
             preferred_element_type=jnp.float32,
         )
-        value_g[...] += lax.dot_general(
-            keep_s[...], jnp.concatenate(dout_n, axis=0), (((0,), (0,)), ((), ())),
-            preferred_element_type=jnp.float32,
-        )
         return carry
 
     lax.fori_loop(heads[0], heads[1], one_head, 0)
-    mixed_ref[...] = mixed_g[...].astype(low)
-    grad_ref[:, :channels] = query_g[...].astype(low)
-    grad_ref[:, channels : 2 * channels] = key_g[:rows, :].astype(low)
-    grad_ref[:, 2 * channels :] = value_g[:rows, :].astype(low)
-    away_ref[:, :channels] = key_g[rows:, :].astype(low)
-    away_ref[:, channels:] = value_g[rows:, :].astype(low)
-
-
-def attention(qc_own, kv_own, kv_far, proj_out, heads):
+    mixed = mixed_g[...].astype(low)
+    grads = [query_g[...].astype(low)]
+    grads += [ref[:rows, :].astype(low) for ref in (key_g, value_g)]
+    aways = [ref[rows:, :].astype(low) for ref in (key_g, value_g)]
+    if not last:
+        mixed_ref, grad_ref, away_ref = refs[4:7]
+        mixed_ref[...] = mixed
+        grad_ref[...] = jnp.concatenate(grads, axis=1)
+        away_ref[...] = jnp.concatenate(aways, axis=1)
+        return
+    mixed_ref, grad_ref, away_ref, qkv_ref = refs[4:8]
+    part_ref, apart_ref, send_ref, term_ref, all_ref, far_all_ref = refs[8:14]
+    own = jnp.concatenate(grads, axis=1) + grad_ref[...]
+    far = jnp.concatenate(aways, axis=1) + away_ref[...]
+    all_ref[...] = own
+    far_all_ref[...] = far
+    own_part = lax.dot_general(
+        own, qkv_ref[...], (((1,), (1,)), ((), ())), preferred_element_type=jnp.float32
+    )
+    far_part = lax.dot_general(
+        far, qkv_ref[:, channels:], (((1,), (1,)), ((), ())), preferred_element_type=jnp.float32
+    )
+    part_ref[...] = own_part.reshape(blocks, wide, channels)
+    apart_ref[...] = jnp.zeros_like(apart_ref)
+    query_g[...] = far_part
+    for block in range(blocks):
+        edge = 0 if block % 2 == 0 else COLS - EDGE
+        at = block * wide + COLS
+        apart_ref[block, :EDGE, :] = query_g[at - COLS + edge : at - COLS + edge + EDGE, :]
+        query_g[at : at + EDGE, :] = part_ref[block, edge : edge + EDGE, :]
+    send_ref[...] = query_g[...].astype(low).reshape(blocks, wide, channels)
+    term_ref[...] = contract_rows(mixed + mixed_ref[...], rows_of(qc_ref, wide))
+
+
+def attention(qc_own, kv_own, kv_far, proj_out, heads, first=None, proj_qkv=None):
     blocks, wide, channels = kv_own.shape
     rows = blocks * wide
     low = jnp.bfloat16
-    shapes = [(rows, channels), (rows, 3 * channels), (rows, 2 * channels)]
+    operands = [qc_own, kv_own, kv_far, proj_out]
+    shapes = [((rows, channels), low), ((rows, 3 * channels), low), ((rows, 2 * channels), low)]
+    if first is not None:
+        operands += [*first, proj_qkv]
+        shapes = [
+            ((blocks, wide, channels), jnp.float32),
+            ((blocks, 8, channels), jnp.float32),
+            ((blocks, wide, channels), low),
+            ((channels, channels), jnp.float32),
+        ] + shapes[1:]
     return pl.pallas_call(
-        functools.partial(attend_rows, heads=heads),
-        out_shape=[jax.ShapeDtypeStruct(s, low) for s in shapes],
-        in_specs=[pl.BlockSpec(memory_space=pltpu.VMEM)] * 4,
-        out_specs=[pl.BlockSpec(memory_space=pltpu.VMEM)] * 3,
+        functools.partial(attend_rows, heads=heads, last=first is not None),
+        out_shape=[jax.ShapeDtypeStruct(s, t) for s, t in shapes],
+        in_specs=[pl.BlockSpec(memory_space=pltpu.VMEM)] * len(operands),
+        out_specs=[pl.BlockSpec(memory_space=pltpu.VMEM)] * len(shapes),
         scratch_shapes=[
             pltpu.VMEM((rows, channels), jnp.float32),
             pltpu.VMEM((rows, 2 * rows), low),
@@ -166,64 +208,7 @@
             transcendentals=(heads[1] - heads[0]) * rows * 2 * rows,
         ),
         name="attend_rows",
-    )(qc_own, kv_own, kv_far, proj_out)
-
-
-def gather_parts(first_refs, second_refs, cot_ref, qkv_ref, part_ref, away_ref, send_ref, term_ref,
-                 all_ref, far_ref, send_s):
-    channels = cot_ref.shape[2]
-    blocks, wide = cot_ref.shape[0], cot_ref.shape[1] // 2
-    rows = blocks * wide
-    low = jnp.bfloat16
-    mixed, own, far = (a[...] + b[...] for a, b in zip(first_refs, second_refs))
-    all_ref[...] = own
-    far_ref[...] = far
-    own_part = lax.dot_general(
-        own, qkv_ref[...], (((1,), (1,)), ((), ())), preferred_element_type=jnp.float32
-    )
-    far_part = lax.dot_general(
-        far, qkv_ref[:, channels:], (((1,), (1,)), ((), ())), preferred_element_type=jnp.float32
-    )
-    part_ref[...] = own_part.reshape(blocks, wide, channels)
-    away_ref[...] = far_part.reshape(blocks, wide, channels)
-    send_s[...] = far_part.reshape(blocks, wide, channels)
-    for block in range(blocks):
-        edge = 0 if block % 2 == 0 else COLS - EDGE
-        send_s[block, COLS : COLS + EDGE, :] = part_ref[block, edge : edge + EDGE, :]
-    send_ref[...] = send_s[...].astype(low)
-    cot = cot_ref[:, wide:, :].reshape(rows, channels)
-    term_ref[...] = contract_rows(mixed, cot)
-
-
-def combine(first, second, qc_own, proj_qkv):
-    blocks, double, channels = qc_own.shape
-    wide = double // 2
-    rows = blocks * wide
-    low = jnp.bfloat16
-    shapes = [
-        ((blocks, wide, channels), jnp.float32),
-        ((blocks, wide, channels), jnp.float32),
-        ((blocks, wide, channels), low),
-        ((channels, channels), jnp.float32),
-        ((rows, 3 * channels), low),
-        ((rows, 2 * channels), low),
-    ]
-
-    def body(*refs):
-        gather_parts(refs[:3], refs[3:6], *refs[6:])
-
-    return pl.pallas_call(
-        body,
-        out_shape=[jax.ShapeDtypeStruct(s, t) for s, t in shapes],
-        in_specs=[pl.BlockSpec(memory_space=pltpu.VMEM)] * 8,
-        out_specs=[pl.BlockSpec(memory_space=pltpu.VMEM)] * 6,
-        scratch_shapes=[pltpu.VMEM((blocks, wide, channels), jnp.float32)],
-        compiler_params=pltpu.CompilerParams(vmem_limit_bytes=24 * 1024 * 1024),
-        cost_estimate=pl.CostEstimate(
-            flops=12 * rows * channels * channels, bytes_accessed=5 * 10**6, transcendentals=0
-        ),
-        name="combine",
-    )(*first, *second, qc_own, proj_qkv)
+    )(*operands)
 
 
 def row_inside(lat_ref, shape, width):
@@ -448,19 +433,20 @@
     hid_far = lax.ppermute(hidden_two, "zh", SWAP)
     far_one, hidden_two = lax.optimization_barrier((far_one, hidden_two))
 
-    first = attention(qc_own, kv_one, far_one, proj_out, (0, HEADS // 2))
+    half = HEADS // 2
+    first = attention(qc_own, kv_one, far_one, proj_out, (0, half))
     first, kv_two = lax.optimization_barrier((first, kv_two))
-    second = attention(qc_own, kv_two, far_two, proj_out, (HEADS // 2, HEADS))
-    own_part, far_part, sent, out_term, own_qkv, far_kv = combine(first, second, qc_own, proj_qkv)
+    own_part, far_edge, sent, out_term, own_qkv, far_kv = attention(
+        qc_own, kv_two, far_two, proj_out, (half, HEADS), first, proj_qkv
+    )
     sent, hid_far = lax.optimization_barrier((sent, hid_far))
     hid_rows = to_rows(hidden_two, hid_far)
     from_far = lax.ppermute(sent, "zh", SWAP)
     whole = (own_part + from_far.astype(jnp.float32)).astype(jnp.bfloat16)
     whole = whole.reshape(4, 2, GROWN, channels)
-    away = far_part.reshape(4, 2, GROWN, channels)
     edge = from_far.reshape(4, 2, GROWN, channels)[:, :, COLS : COLS + EDGE].astype(jnp.float32)
-    edge_low = (edge[:, 0] + away[:, 0, :EDGE]).astype(jnp.bfloat16)
-    edge_high = (edge[:, 1] + away[:, 1, COLS - EDGE : COLS]).astype(jnp.bfloat16)
+    edge = (edge + far_edge.reshape(4, 2, 8, channels)[:, :, :EDGE]).astype(jnp.bfloat16)
+    edge_low, edge_high = edge[:, 0], edge[:, 1]
     left = jnp.where(half_at == 1, edge_high, jnp.roll(edge_high, 1, axis=0))
     right = jnp.where(half_at == 0, edge_low, jnp.roll(edge_low, -1, axis=0))
     left = jnp.stack([left, whole[:, 0, COLS - EDGE : COLS]], axis=1)

time: 262 us -> 252 us (0.962)
  Pallas kernels: 49.6 us -> 40.6 us
    pallas_call x3 -> x2, Pallas kernels: 44.8 us -> 35.8 us  [attention(): pl.pallas_call(functools.partial(attend_rows, heads=heads, last=first is...]
    ppermute x1, waiting for transfers between devices: 11.9 us -> 7.09 us  [on_device(): from_far = lax.ppermute(sent, 'zh', SWAP)]
    ppermute x1, waiting for transfers between devices: 4.2 us -> 8.7 us  [on_device(): far_two = lax.ppermute(kv_two, 'zh', SWAP)]
    unnamed x49 -> x53, local copies, waits for them, and re-layouts: 4.83 us -> 5.73 us
  transfers between devices with their start and end apart: 15 -> 15, of which waited for: 9 -> 10; matrix products, arithmetic and copies ran while one was open for 4% -> 3% of each run, Pallas kernels for 18% -> 15%
where the time goes in v5:
time: 252 us; the launch traced here: 251 us
  starting transfers between devices  87.6 us (35%)
  blocking collectives  56.6 us (22%)
  waiting for transfers between devices  44.1 us (18%)
  Pallas kernels  40.6 us (16%)
  local copies, waits for them, and re-layouts  11.5 us (5%)
  other arithmetic  8.62 us (3%)
    pallas_call x2, Pallas kernels, attention(): pl.pallas_call(functools.partial(attend_rows, heads=heads, last=first is...  35.8 us
    all_to_all x1, blocking collectives, reduce_all(): lax.all_to_all(terms.reshape(32, part, channels), ('x', 'y', 'core'), 0,...  23 us
    all_to_all x1, blocking collectives, reduce_all(): band = lax.all_to_all(band, ('zh', 'zl'), 0, 0, tiled=True)  19.7 us
    ppermute x1, starting transfers between devices, exchange_lon(): outer = lax.ppermute(jnp.where(at_zero, left, right), LON_AXES, pairs)  16.8 us
    all_to_all x3, starting transfers between devices, to_rows(): lax.all_to_all(jnp.concatenate(grown, axis=1), PLANE, 0, 0, tiled=True)  15.7 us
    all_to_all x1, blocking collectives, reduce_all(): lax.all_to_all(jnp.broadcast_to(band[None], (16, piece)), ('zh', 'zl'), 0...  13.9 us
    all_to_all x1, waiting for transfers between devices, reduce_all(): lax.all_to_all(jnp.broadcast_to(band[None], (32, part, channels)), ('x',...  12.8 us
    ppermute x1, starting transfers between devices, on_device(): hid_far = lax.ppermute(hidden_two, 'zh', SWAP)  11.3 us
  transfers between devices with their start and end apart: 15, of which 10 were waited for; matrix products, arithmetic and copies ran while one was open for 3% of the time, Pallas kernels for 15%

profile of v5, /device:TPU:1, one launch (start us, length us, event | category | flops | bytes accessed | tf_op | source)
XLA Modules:
  0.0 251.2 jit_solution(14592567548587843914)
XLA Ops:
  2.9 16.8 %collective-permute-start = (bf16[8,16,128]{2,1,0:T(8,128)(2,1)S(1)}, bf16[8,16,128]{2,1,0:T(8,128)(2,1)S(1)}, u32[]{:S(2)}, u32[]{:S(2)}) collective-permute-start(bf16[8,16,128]{2,1,0:T(8,128)(2,1)S(1)} %get-tuple-element.113), channel_id=1, source_target_pairs={{0,480},{32,64},{64,32},{96,128},{128,96},{160,192},{192,160},{224... | collective-permute-start | bytes 98312 | tf_op jit(solution)/shard_map/ppermute | solution.py:45
  19.7 3.9 %collective-permute-start.1 = (bf16[8,16,128]{2,1,0:T(8,128)(2,1)S(1)}, bf16[8,16,128]{2,1,0:T(8,128)(2,1)S(1)}, u32[]{:S(2)}, u32[]{:S(2)}) collective-permute-start(bf16[8,16,128]{2,1,0:T(8,128)(2,1)S(1)} %get-tuple-element.112), channel_id=1, source_target_pairs={{0,32},{32,0},{1,33},{33,1},{2,34},{34,2},{3,35},{35,3},{4,36},{36... | collective-permute-start | bytes 98312 | tf_op jit(solution)/shard_map/ppermute | solution.py:43
  25.9 4.7 %all-to-all-start = ((bf16[8,192,128]{2,1,0:T(8,128)(2,1)}), bf16[8,192,128]{2,1,0:T(8,128)(2,1)S(1)}, u32[]{:S(2)}, u32[]{:S(2)}) async-start(bf16[8,192,128]{2,1,0:T(8,128)(2,1)} %pad_maximum_fusion.3), calls=%async_computation | async-start | bytes 786432 | tf_op jit(solution)/shard_map/all_to_all | solution.py:395
  30.8 2.4 collective-permute-start.2
  33.3 1.3 collective-permute-start.3
  36.0 1.4 collective-permute-done.2
  37.5 3.8 %collective-permute-done.3 = bf16[6,128,128]{2,1,0:T(8,128)(2,1)S(1)} collective-permute-done((bf16[6,128,128]{2,1,0:T(8,128)(2,1)S(1)}, bf16[6,128,128]{2,1,0:T(8,128)(2,1)S(1)}, u32[]{:S(2)}, u32[]{:S(2)}) %collective-permute-start.3) | collective-permute-done | bytes 196640 | tf_op jit(solution)/shard_map/ppermute | solution.py:52
  41.4 11.2 %collective-permute-start.4 = (bf16[8,96,128]{2,1,0:T(8,128)(2,1)S(1)}, bf16[8,96,128]{2,1,0:T(8,128)(2,1)S(1)}, u32[]{:S(2)}, u32[]{:S(2)}) collective-permute-start(bf16[8,96,128]{2,1,0:T(8,128)(2,1)S(1)} %get-tuple-element.91.refs_1_), channel_id=1, source_target_pairs={{0,64},{64,0},{1,65},{65,1},{2,66},{66,2},{3,67},{67,3},{4,68},{68... | collective-permute-start | bytes 589832 | tf_op jit(solution)/shard_map/ppermute | solution.py:426
  53.5 6.0 %all-to-all-start.1 = ((bf16[8,192,128]{2,1,0:T(8,128)(2,1)}), bf16[8,192,128]{2,1,0:T(8,128)(2,1)S(1)}, u32[]{:S(2)}, u32[]{:S(2)}) async-start(bf16[8,192,128]{2,1,0:T(8,128)(2,1)} %fusion.2), calls=%async_computation.1 | async-start | bytes 786432 | tf_op jit(solution)/shard_map/all_to_all | solution.py:395
  59.4 2.9 %collective-permute-start.5 = (bf16[8,96,128]{2,1,0:T(8,128)(2,1)S(1)}, bf16[8,96,128]{2,1,0:T(8,128)(2,1)S(1)}, u32[]{:S(2)}, u32[]{:S(2)}) collective-permute-start(bf16[8,96,128]{2,1,0:T(8,128)(2,1)S(1)} %get-tuple-element.49.refs_1_), channel_id=1, source_target_pairs={{0,64},{64,0},{1,65},{65,1},{2,66},{66,2},{3,67},{67,3},{4,68},{68... | collective-permute-start | bytes 589832 | tf_op jit(solution)/shard_map/ppermute | solution.py:427
  62.4 2.5 forward_block.1
  66.5 11.3 %collective-permute-start.6 = (bf16[8,96,128]{2,1,0:T(8,128)(2,1)S(1)}, bf16[8,96,128]{2,1,0:T(8,128)(2,1)}, u32[]{:S(2)}, u32[]{:S(2)}) collective-permute-start(bf16[8,96,128]{2,1,0:T(8,128)(2,1)S(1)} %get-tuple-element.62), channel_id=1, source_target_pairs={{0,64},{64,0},{1,65},{65,1},{2,66},{66,2},{3,67},{67,3},{4,68},{68... | collective-permute-start | bytes 589832 | tf_op jit(solution)/shard_map/ppermute | solution.py:433
  77.8 17.4 %attend_rows.2 = (bf16[768,128]{1,0:T(8,128)(2,1)S(1)}, bf16[768,384]{1,0:T(8,128)(2,1)S(1)}, bf16[768,256]{1,0:T(8,128)(2,1)S(1)}) custom-call(bf16[8,192,128]{2,1,0:T(8,128)(2,1)S(1)} %all-to-all-done.1.refs_0_, bf16[8,96,128]{2,1,0:T(8,128)(2,1)S(1)} %get-tuple-element.91.refs_1_, bf16[8,96,128]{2,1,0:T(8,128)(2,1)S(1)} %collective-permute-done.4.refs_2_, ...), custom_call_target="tpu_custom_call" | custom-call | flops 7247757312 | bytes 1572864 | tf_op jit(solution)/shard_map/attend_rows/pallas_call | solution.py:188
  95.2 8.7 %collective-permute-done.5.refs_2_ = bf16[8,96,128]{2,1,0:T(8,128)(2,1)S(1)} collective-permute-done((bf16[8,96,128]{2,1,0:T(8,128)(2,1)S(1)}, bf16[8,96,128]{2,1,0:T(8,128)(2,1)S(1)}, u32[]{:S(2)}, u32[]{:S(2)}) %collective-permute-start.5) | collective-permute-done | bytes 196640 | tf_op jit(solution)/shard_map/ppermute | solution.py:427
  104.8 18.4 %attend_rows.3 = (f32[8,96,128]{2,1,0:T(8,128)S(1)}, f32[8,8,128]{2,1,0:T(8,128)S(1)}, bf16[8,96,128]{2,1,0:T(8,128)(2,1)}, f32[128,128]{1,0:T(8,128)S(1)}, bf16...) custom-call(bf16[8,192,128]{2,1,0:T(8,128)(2,1)S(1)} %all-to-all-done.1.refs_0_, ...), custom_call_target="tpu_custom_call" | custom-call | flops 7247757312 | bytes 1572864 | tf_op jit(solution)/shard_map/attend_rows/pallas_call | solution.py:188
  123.2 7.2 %collective-permute-start.7 = (bf16[8,96,128]{2,1,0:T(8,128)(2,1)}, bf16[8,96,128]{2,1,0:T(8,128)(2,1)S(1)}, u32[]{:S(2)}, u32[]{:S(2)}) collective-permute-start(bf16[8,96,128]{2,1,0:T(8,128)(2,1)} %get-tuple-element.54), channel_id=1, source_target_pairs={{0,64},{64,0},{1,65},{65,1},{2,66},{66,2},{3,67},{67,3},{4,68},{68... | collective-permute-start | bytes 589832 | tf_op jit(solution)/shard_map/ppermute | solution.py:444
  130.5 1.7 pad_maximum_fusion.4
  132.3 5.1 %all-to-all-start.3 = ((bf16[8,192,128]{2,1,0:T(8,128)(2,1)}), bf16[8,192,128]{2,1,0:T(8,128)(2,1)}, u32[]{:S(2)}, u32[]{:S(2)}) async-start(bf16[8,192,128]{2,1,0:T(8,128)(2,1)} %pad_maximum_fusion.4), calls=%async_computation.3 | async-start | bytes 786432 | tf_op jit(solution)/shard_map/all_to_all | solution.py:395
  137.3 7.1 %collective-permute-done.7 = bf16[8,96,128]{2,1,0:T(8,128)(2,1)S(1)} collective-permute-done((bf16[8,96,128]{2,1,0:T(8,128)(2,1)}, bf16[8,96,128]{2,1,0:T(8,128)(2,1)S(1)}, u32[]{:S(2)}, u32[]{:S(2)}) %collective-permute-start.7) | collective-permute-done | bytes 196640 | tf_op jit(solution)/shard_map/ppermute | solution.py:444
  145.5 5.1 %all-to-all-start.2 = ((bf16[8,112,128]{2,1,0:T(8,128)(2,1)}), bf16[8,112,128]{2,1,0:T(8,128)(2,1)S(1)}, u32[]{:S(2)}, u32[]{:S(2)}) async-start(bf16[8,112,128]{2,1,0:T(8,128)(2,1)} %bitcast.4), calls=%async_computation.2 | async-start | bytes 458752 | tf_op jit(solution)/shard_map/all_to_all | solution.py:456
  150.6 1.0 fusion.25
  152.4 4.3 %all-to-all-done.2 = bf16[8,112,128]{2,1,0:T(8,128)(2,1)S(1)} async-done(((bf16[8,112,128]{2,1,0:T(8,128)(2,1)}), bf16[8,112,128]{2,1,0:T(8,128)(2,1)S(1)}, u32[]{:S(2)}, u32[]{:S(2)}) %all-to-all-start.2) | async-done | bytes 229408 | tf_op jit(solution)/shard_map/all_to_all | solution.py:456
  157.0 2.0 collective-permute-start.8
  158.9 1.5 collective-permute-start.9
  161.6 3.8 %collective-permute-done.9 = bf16[6,112,128]{2,1,0:T(8,128)(2,1)S(1)} collective-permute-done((bf16[6,112,128]{2,1,0:T(8,128)(2,1)S(1)}, bf16[6,112,128]{2,1,0:T(8,128)(2,1)S(1)}, u32[]{:S(2)}, u32[]{:S(2)}) %collective-permute-start.9) | collective-permute-done | bytes 172064 | tf_op jit(solution)/shard_map/ppermute | solution.py:52
  165.6 2.3 backward_block.1
  168.0 23.0 %all_to_all.46 = bf16[32,88,128]{2,1,0:T(8,128)(2,1)S(1)} all-to-all(bf16[32,88,128]{2,1,0:T(8,128)(2,1)S(1)} %bitcast.22), channel_id=1, replica_groups=mesh['x'=4,'zh'=2,'core'=2,'zl'=8,'y'=4] {'x','y','core'}, dimensions={0} | all-to-all | bytes 1441792 | tf_op jit(solution)/shard_map/all_to_all | solution.py:371
  192.6 19.7 %all_to_all.47 = bf16[16,2,352]{2,1,0:T(2,128)(2,1)S(1)} all-to-all(bf16[16,2,352]{2,1,0:T(2,128)(2,1)S(1)} %reshape.80), channel_id=1, replica_groups=mesh['x'=4,'zh'=2,'core'=2,'zl'=8,'y'=4] {'zh','zl'}, dimensions={0} | all-to-all | bytes 45056 | tf_op jit(solution)/shard_map/all_to_all | solution.py:375
  213.4 13.9 %all_to_all.48 = bf16[16,2,352]{2,1,0:T(2,128)(2,1)S(1)} all-to-all(bf16[16,2,352]{2,1,0:T(2,128)(2,1)S(1)} %reshape.82), channel_id=1, replica_groups=mesh['x'=4,'zh'=2,'core'=2,'zl'=8,'y'=4] {'zh','zl'}, dimensions={0} | all-to-all | bytes 45056 | tf_op jit(solution)/shard_map/all_to_all | solution.py:377
  228.7 6.3 %all-to-all-start.7 = ((bf16[32,88,128]{2,1,0:T(8,128)(2,1)}), bf16[32,88,128]{2,1,0:T(8,128)(2,1)S(1)}, u32[]{:S(2)}, u32[]{:S(2)}) async-start(bf16[32,88,128]{2,1,0:T(8,128)(2,1)} %broadcast_in_dim.31), calls=%async_computation.7 | async-start | bytes 1441792 | tf_op jit(solution)/shard_map/all_to_all | solution.py:380
  235.8 12.8 %all-to-all-done.7 = bf16[32,88,128]{2,1,0:T(8,128)(2,1)S(1)} async-done(((bf16[32,88,128]{2,1,0:T(8,128)(2,1)}), bf16[32,88,128]{2,1,0:T(8,128)(2,1)S(1)}, u32[]{:S(2)}, u32[]{:S(2)}) %all-to-all-start.7) | async-done | bytes 720928 | tf_op jit(solution)/shard_map/all_to_all | solution.py:380
  249.4 1.1 fusion.24
  (130 shorter events, 19.1 us)
Async XLA Ops:
  0.6 23.9 %copy-start.19 = (bf16[8,90,128]{2,0,1:T(8,128)(2,1)S(1)}, bf16[8,90,128]{2,0,1:T(8,128)(2,1)}, u32[]{:S(2)}) copy-start(bf16[8,90,128]{2,0,1:T(8,128)(2,1)} %param.11) | copy-start | bytes 552964
  0.6 24.1 %copy-start.20 = (bf16[8,90,128]{2,0,1:T(8,128)(2,1)S(1)}, bf16[8,90,128]{2,0,1:T(8,128)(2,1)}, u32[]{:S(2)}) copy-start(bf16[8,90,128]{2,0,1:T(8,128)(2,1)} %param.12) | copy-start | bytes 552964
  1.7 51.0 %copy-start.10 = (bf16[8,90,128]{2,1,0:T(8,128)(2,1)}, bf16[8,90,128]{2,1,0:T(8,128)(2,1)S(1)}, u32[]{:S(2)}) copy-start(bf16[8,90,128]{2,1,0:T(8,128)(2,1)S(1)} %copy.41) | copy-start | bytes 552964
  2.9 20.8 %collective-permute-start = (bf16[8,16,128]{2,1,0:T(8,128)(2,1)S(1)}, bf16[8,16,128]{2,1,0:T(8,128)(2,1)S(1)}, u32[]{:S(2)}, u32[]{:S(2)}) collective-permute-start(bf16[8,16,128]{2,1,0:T(8,128)(2,1)S(1)} %get-tuple-element.113), channel_id=1, source_target_pairs={{0,480},{32,64},{64,32},{96,128},{128,96},{160,192},{192,160},{224... | collective-permute-start | bytes 98312 | tf_op jit(solution)/shard_map/ppermute | solution.py:45
  19.7 4.8 %collective-permute-start.1 = (bf16[8,16,128]{2,1,0:T(8,128)(2,1)S(1)}, bf16[8,16,128]{2,1,0:T(8,128)(2,1)S(1)}, u32[]{:S(2)}, u32[]{:S(2)}) collective-permute-start(bf16[8,16,128]{2,1,0:T(8,128)(2,1)S(1)} %get-tuple-element.112), channel_id=1, source_target_pairs={{0,32},{32,0},{1,33},{33,1},{2,34},{34,2},{3,35},{35,3},{4,36},{36... | collective-permute-start | bytes 98312 | tf_op jit(solution)/shard_map/ppermute | solution.py:43
  25.9 15.4 %all-to-all-start = ((bf16[8,192,128]{2,1,0:T(8,128)(2,1)}), bf16[8,192,128]{2,1,0:T(8,128)(2,1)S(1)}, u32[]{:S(2)}, u32[]{:S(2)}) async-start(bf16[8,192,128]{2,1,0:T(8,128)(2,1)} %pad_maximum_fusion.3), calls=%async_computation | async-start | bytes 786432 | tf_op jit(solution)/shard_map/all_to_all | solution.py:395
  30.7 10.6 %copy-start.15 = (bf16[8,5,128]{2,1,0:T(8,128)(2,1)}, bf16[8,5,128]{2,1,0:T(8,128)(2,1)S(1)}, u32[]{:S(2)}) copy-start(bf16[8,5,128]{2,1,0:T(8,128)(2,1)S(1)} %slice.182) | copy-start | bytes 30724
  30.8 10.6 %copy-start.12 = (bf16[8,28,128]{2,1,0:T(8,128)(2,1)}, bf16[8,28,128]{2,1,0:T(8,128)(2,1)S(1)}, u32[]{:S(2)}) copy-start(bf16[8,28,128]{2,1,0:T(8,128)(2,1)S(1)} %broadcast_in_dim.26) | copy-start | bytes 172036
  30.8 21.8 %copy-start.21 = (bf16[8,90,128]{2,0,1:T(8,128)(2,1)S(1)}, bf16[8,90,128]{2,0,1:T(8,128)(2,1)}, u32[]{:S(2)}) copy-start(bf16[8,90,128]{2,0,1:T(8,128)(2,1)} %param.10) | copy-start | bytes 552964
  30.8 6.6 %collective-permute-start.2 = (bf16[6,128,128]{2,1,0:T(8,128)(2,1)S(1)}, bf16[6,128,128]{2,1,0:T(8,128)(2,1)S(1)}, u32[]{:S(2)}, u32[]{:S(2)}) collective-permute-start(bf16[6,128,128]{2,1,0:T(8,128)(2,1)S(1)} %get-tuple-element.93), channel_id=1, source_target_pairs={{0,1},{1,2},{2,3},{3,4},{4,5},{5,6},{6,7},{7,8},{8,9},{9,10},{10,1... | collective-permute-start | bytes 589832 | tf_op jit(solution)/shard_map/ppermute | solution.py:51
  33.3 8.0 %collective-permute-start.3 = (bf16[6,128,128]{2,1,0:T(8,128)(2,1)S(1)}, bf16[6,128,128]{2,1,0:T(8,128)(2,1)S(1)}, u32[]{:S(2)}, u32[]{:S(2)}) collective-permute-start(bf16[6,128,128]{2,1,0:T(8,128)(2,1)S(1)} %get-tuple-element.92), channel_id=1, source_target_pairs={{1,0},{2,1},{3,2},{4,3},{5,4},{6,5},{7,6},{8,7},{9,8},{10,9},{11,1... | collective-permute-start | bytes 589832 | tf_op jit(solution)/shard_map/ppermute | solution.py:52
  41.3 12.2 %copy-start.18 = (bf16[6,128,128]{2,1,0:T(8,128)(2,1)}, bf16[6,128,128]{2,1,0:T(8,128)(2,1)S(1)}, u32[]{:S(2)}) copy-start(bf16[6,128,128]{2,1,0:T(8,128)(2,1)S(1)} %collective-permute-done.3) | copy-start | bytes 589828
  41.4 36.4 %collective-permute-start.4 = (bf16[8,96,128]{2,1,0:T(8,128)(2,1)S(1)}, bf16[8,96,128]{2,1,0:T(8,128)(2,1)S(1)}, u32[]{:S(2)}, u32[]{:S(2)}) collective-permute-start(bf16[8,96,128]{2,1,0:T(8,128)(2,1)S(1)} %get-tuple-element.91.refs_1_), channel_id=1, source_target_pairs={{0,64},{64,0},{1,65},{65,1},{2,66},{66,2},{3,67},{67,3},{4,68},{68... | collective-permute-start | bytes 589832 | tf_op jit(solution)/shard_map/ppermute | solution.py:426
  53.5 8.9 %copy-start = (bf16[3,3,128,128]{3,2,1,0:T(8,128)(2,1)S(1)}, bf16[3,3,128,128]{3,2,1,0:T(8,128)(2,1)}, u32[]{:S(2)}) copy-start(bf16[3,3,128,128]{3,2,1,0:T(8,128)(2,1)} %near_ref.3) | copy-start | bytes 884740
  53.5 8.9 %copy-start.2 = (bf16[3,3,128,128]{3,2,1,0:T(8,128)(2,1)S(1)}, bf16[3,3,128,128]{3,2,1,0:T(8,128)(2,1)}, u32[]{:S(2)}) copy-start(bf16[3,3,128,128]{3,2,1,0:T(8,128)(2,1)} %dil_ref.1) | copy-start | bytes 884740
  53.5 24.3 %all-to-all-start.1 = ((bf16[8,192,128]{2,1,0:T(8,128)(2,1)}), bf16[8,192,128]{2,1,0:T(8,128)(2,1)S(1)}, u32[]{:S(2)}, u32[]{:S(2)}) async-start(bf16[8,192,128]{2,1,0:T(8,128)(2,1)} %fusion.2), calls=%async_computation.1 | async-start | bytes 786432 | tf_op jit(solution)/shard_map/all_to_all | solution.py:395
  59.4 44.5 %collective-permute-start.5 = (bf16[8,96,128]{2,1,0:T(8,128)(2,1)S(1)}, bf16[8,96,128]{2,1,0:T(8,128)(2,1)S(1)}, u32[]{:S(2)}, u32[]{:S(2)}) collective-permute-start(bf16[8,96,128]{2,1,0:T(8,128)(2,1)S(1)} %get-tuple-element.49.refs_1_), channel_id=1, source_target_pairs={{0,64},{64,0},{1,65},{65,1},{2,66},{66,2},{3,67},{67,3},{4,68},{68... | collective-permute-start | bytes 589832 | tf_op jit(solution)/shard_map/ppermute | solution.py:427
  62.4 15.4 %copy-start.5 = (bf16[128,128]{1,0:T(8,128)(2,1)S(1)}, bf16[128,128]{1,0:T(8,128)(2,1)}, u32[]{:S(2)}) copy-start(bf16[128,128]{1,0:T(8,128)(2,1)} %refs_3_.3) | copy-start | bytes 98308
  66.5 56.7 %collective-permute-start.6 = (bf16[8,96,128]{2,1,0:T(8,128)(2,1)S(1)}, bf16[8,96,128]{2,1,0:T(8,128)(2,1)}, u32[]{:S(2)}, u32[]{:S(2)}) collective-permute-start(bf16[8,96,128]{2,1,0:T(8,128)(2,1)S(1)} %get-tuple-element.62), channel_id=1, source_target_pairs={{0,64},{64,0},{1,65},{65,1},{2,66},{66,2},{3,67},{67,3},{4,68},{68... | collective-permute-start | bytes 589832 | tf_op jit(solution)/shard_map/ppermute | solution.py:433
  104.8 25.6 %copy-start.11 = (bf16[8,90,128]{2,1,0:T(8,128)(2,1)S(1)}, bf16[8,90,128]{2,1,0:T(8,128)(2,1)}, u32[]{:S(2)}) copy-start(bf16[8,90,128]{2,1,0:T(8,128)(2,1)} %copy-done.10) | copy-start | bytes 552964
  104.8 25.6 %copy-start.13 = (bf16[8,28,128]{2,1,0:T(8,128)(2,1)S(1)}, bf16[8,28,128]{2,1,0:T(8,128)(2,1)}, u32[]{:S(2)}) copy-start(bf16[8,28,128]{2,1,0:T(8,128)(2,1)} %copy-done.12) | copy-start | bytes 172036
  104.8 25.6 %copy-start.16 = (bf16[8,5,128]{2,1,0:T(8,128)(2,1)S(1)}, bf16[8,5,128]{2,1,0:T(8,128)(2,1)}, u32[]{:S(2)}) copy-start(bf16[8,5,128]{2,1,0:T(8,128)(2,1)} %copy-done.15) | copy-start | bytes 30724
  104.8 25.6 %slice-start = ((bf16[6,128,128]{2,1,0:T(8,128)(2,1)}), bf16[1,128,128]{2,1,0:T(8,128)(2,1)S(1)}, s32[]{:S(2)}) async-start(bf16[6,128,128]{2,1,0:T(8,128)(2,1)} %copy-done.17), calls=%async_computation.8 | async-start | bytes 65536 | tf_op jit(solution)/shard_map/slice | solution.py:430
  104.8 25.6 %slice-start.1 = ((bf16[6,128,128]{2,1,0:T(8,128)(2,1)}), bf16[1,128,128]{2,1,0:T(8,128)(2,1)S(1)}, s32[]{:S(2)}) async-start(bf16[6,128,128]{2,1,0:T(8,128)(2,1)} %copy-done.18), calls=%async_computation.9 | async-start | bytes 65536 | tf_op jit(solution)/shard_map/slice | solution.py:430
  123.2 21.2 %collective-permute-start.7 = (bf16[8,96,128]{2,1,0:T(8,128)(2,1)}, bf16[8,96,128]{2,1,0:T(8,128)(2,1)S(1)}, u32[]{:S(2)}, u32[]{:S(2)}) collective-permute-start(bf16[8,96,128]{2,1,0:T(8,128)(2,1)} %get-tuple-element.54), channel_id=1, source_target_pairs={{0,64},{64,0},{1,65},{65,1},{2,66},{66,2},{3,67},{67,3},{4,68},{68... | collective-permute-start | bytes 589832 | tf_op jit(solution)/shard_map/ppermute | solution.py:444
  130.5 14.0 %copy-start.22 = (bf16[112]{0:T(256)(128)(2,1)S(1)}, bf16[112]{0:T(256)(128)(2,1)}, u32[]{:S(2)}) copy-start(bf16[112]{0:T(256)(128)(2,1)} %pad.49.clone) | copy-start | bytes 676
  132.3 13.3 %all-to-all-start.3 = ((bf16[8,192,128]{2,1,0:T(8,128)(2,1)}), bf16[8,192,128]{2,1,0:T(8,128)(2,1)}, u32[]{:S(2)}, u32[]{:S(2)}) async-start(bf16[8,192,128]{2,1,0:T(8,128)(2,1)} %pad_maximum_fusion.4), calls=%async_computation.3 | async-start | bytes 786432 | tf_op jit(solution)/shard_map/all_to_all | solution.py:395
  145.5 11.3 %all-to-all-start.2 = ((bf16[8,112,128]{2,1,0:T(8,128)(2,1)}), bf16[8,112,128]{2,1,0:T(8,128)(2,1)S(1)}, u32[]{:S(2)}, u32[]{:S(2)}) async-start(bf16[8,112,128]{2,1,0:T(8,128)(2,1)} %bitcast.4), calls=%async_computation.2 | async-start | bytes 458752 | tf_op jit(solution)/shard_map/all_to_all | solution.py:456
  151.6 5.1 %copy-start.14 = (bf16[8,128,128]{2,1,0:T(8,128)(2,1)S(1)}, bf16[8,128,128]{2,1,0:T(8,128)(2,1)}, u32[]{:S(2)}) copy-start(bf16[8,128,128]{2,1,0:T(8,128)(2,1)} %pad_maximum_fusion.11) | copy-start | bytes 786436
  157.0 4.6 %collective-permute-start.8 = (bf16[6,112,128]{2,1,0:T(8,128)(2,1)S(1)}, bf16[6,112,128]{2,1,0:T(8,128)(2,1)S(1)}, u32[]{:S(2)}, u32[]{:S(2)}) collective-permute-start(bf16[6,112,128]{2,1,0:T(8,128)(2,1)S(1)} %pad_maximum_fusion.17), channel_id=1, source_target_pairs={{0,1},{1,2},{2,3},{3,4},{4,5},{5,6},{6,7},{7,8},{8,9},{9,10},{10,1... | collective-permute-start | bytes 516104 | tf_op jit(solution)/shard_map/ppermute | solution.py:51
  158.9 6.5 %collective-permute-start.9 = (bf16[6,112,128]{2,1,0:T(8,128)(2,1)S(1)}, bf16[6,112,128]{2,1,0:T(8,128)(2,1)S(1)}, u32[]{:S(2)}, u32[]{:S(2)}) collective-permute-start(bf16[6,112,128]{2,1,0:T(8,128)(2,1)S(1)} %pad_maximum_fusion.18), channel_id=1, source_target_pairs={{1,0},{2,1},{3,2},{4,3},{5,4},{6,5},{7,6},{8,7},{9,8},{10,9},{11,1... | collective-permute-start | bytes 516104 | tf_op jit(solution)/shard_map/ppermute | solution.py:52
  228.7 19.9 %all-to-all-start.7 = ((bf16[32,88,128]{2,1,0:T(8,128)(2,1)}), bf16[32,88,128]{2,1,0:T(8,128)(2,1)S(1)}, u32[]{:S(2)}, u32[]{:S(2)}) async-start(bf16[32,88,128]{2,1,0:T(8,128)(2,1)} %broadcast_in_dim.31), calls=%async_computation.7 | async-start | bytes 1441792 | tf_op jit(solution)/shard_map/all_to_all | solution.py:380
  (8 other events, 26.6 us)

commit v6 on v5

--- a/solution.py
+++ b/solution.py
@@ -54,11 +54,12 @@
 
 
 def attend_rows(*refs, heads, last):
-    qc_ref, own_ref, far_ref, proj_ref = refs[:4]
+    own_ref, far_ref, proj_ref = refs[:3]
     out_s, keep_s, grad_s, pair_s, value_s, key_g, value_g, query_g, mixed_g = refs[-9:]
-    blocks, wide, channels = own_ref.shape
+    blocks, wide, channels = far_ref.shape
     rows = blocks * wide
     cols = 2 * rows
+    pair_at, query_at, cot_at = (wide if last else 0), 2 * wide, 3 * wide
     width = channels // HEADS
     chunk = CHUNK
     low = jnp.bfloat16
@@ -67,10 +68,10 @@
         return ref[:, at : at + wide, :].reshape(rows, channels)
 
     out_s[...] = lax.dot_general(
-        rows_of(qc_ref, wide), proj_ref[...], (((1,), (1,)), ((), ())),
+        rows_of(own_ref, cot_at), proj_ref[...], (((1,), (1,)), ((), ())),
         preferred_element_type=jnp.float32,
     )
-    pair = jnp.concatenate([rows_of(own_ref, 0), rows_of(far_ref, 0)], axis=0).astype(jnp.float32)
+    pair = jnp.concatenate([rows_of(own_ref, pair_at), rows_of(far_ref, 0)], axis=0).astype(jnp.float32)
     pair_s[...] = pair
     value_s[...] = pltpu.roll(pair, channels // 2, 1)
     for ref in (key_g, value_g, query_g, mixed_g):
@@ -90,7 +91,7 @@
         spots = [slice(at, at + chunk) for at in range(0, rows, chunk)]
         queries, douts, shares, query_n, dout_n = [], [], [], [], []
         for spot in spots:
-            query = rows_of(qc_ref, 0)[spot].astype(jnp.float32) * 0.25
+            query = rows_of(own_ref, query_at)[spot].astype(jnp.float32) * 0.25
             query_h = jnp.where(here_q, query, jnp.where(lane_q == first, 1.0, 0.0)).astype(low)
             queries.append(jnp.where(here_q, query, 0.0))
             scores = lax.dot_general(
@@ -142,13 +143,13 @@
     grads += [ref[:rows, :].astype(low) for ref in (key_g, value_g)]
     aways = [ref[rows:, :].astype(low) for ref in (key_g, value_g)]
     if not last:
-        mixed_ref, grad_ref, away_ref = refs[4:7]
+        mixed_ref, grad_ref, away_ref = refs[3:6]
         mixed_ref[...] = mixed
         grad_ref[...] = jnp.concatenate(grads, axis=1)
         away_ref[...] = jnp.concatenate(aways, axis=1)
         return
-    mixed_ref, grad_ref, away_ref, qkv_ref = refs[4:8]
-    part_ref, apart_ref, send_ref, term_ref, all_ref, far_all_ref = refs[8:14]
+    mixed_ref, grad_ref, away_ref, qkv_ref = refs[3:7]
+    part_ref, apart_ref, send_ref, term_ref, all_ref, far_all_ref = refs[7:13]
     own = jnp.concatenate(grads, axis=1) + grad_ref[...]
     far = jnp.concatenate(aways, axis=1) + away_ref[...]
     all_ref[...] = own
@@ -168,14 +169,14 @@
         apart_ref[block, :EDGE, :] = query_g[at - COLS + edge : at - COLS + edge + EDGE, :]
         query_g[at : at + EDGE, :] = part_ref[block, edge : edge + EDGE, :]
     send_ref[...] = query_g[...].astype(low).reshape(blocks, wide, channels)
-    term_ref[...] = contract_rows(mixed + mixed_ref[...], rows_of(qc_ref, wide))
-
-
-def attention(qc_own, kv_own, kv_far, proj_out, heads, first=None, proj_qkv=None):
-    blocks, wide, channels = kv_own.shape
+    term_ref[...] = contract_rows(mixed + mixed_ref[...], rows_of(own_ref, cot_at))
+
+
+def attention(own_rows, kv_far, proj_out, heads, first=None, proj_qkv=None):
+    blocks, wide, channels = kv_far.shape
     rows = blocks * wide
     low = jnp.bfloat16
-    operands = [qc_own, kv_own, kv_far, proj_out]
+    operands = [own_rows, kv_far, proj_out]
     shapes = [((rows, channels), low), ((rows, 3 * channels), low), ((rows, 2 * channels), low)]
     if first is not None:
         operands += [*first, proj_qkv]
@@ -404,9 +405,11 @@
     )
 
     side = channels // 2
-    kv_own = to_rows(
+    own_rows = to_rows(
         jnp.concatenate([attn_keys[..., :side], attn_values[..., :side]], axis=2),
         jnp.concatenate([attn_values[..., side:], attn_keys[..., side:]], axis=2),
+        queries,
+        cotangent,
     )
 
     feat_x = jnp.concatenate(
@@ -421,11 +424,9 @@
         jnp.concatenate([feat_x[-5:], cot_x[-1:]], axis=0),
         jnp.concatenate([feat_x[:5], cot_x[:1]], axis=0),
     )
-    low, high, kv_own, queries = lax.optimization_barrier((low, high, kv_own, queries))
-    kv_one, kv_two = kv_own[:, :GROWN], kv_own[:, GROWN:]
-    far_one = lax.ppermute(kv_one, "zh", SWAP)
-    far_two = lax.ppermute(kv_two, "zh", SWAP)
-    qc_own = to_rows(queries, cotangent)
+    low, high, own_rows = lax.optimization_barrier((low, high, own_rows))
+    far_one = lax.ppermute(own_rows[:, :GROWN], "zh", SWAP)
+    far_two = lax.ppermute(own_rows[:, GROWN : 2 * GROWN], "zh", SWAP)
     feat_x = jnp.concatenate([low[:5], feat_x, high[:5]], axis=0)
     cot_near = jnp.concatenate([low[5:], cot_x, high[5:]], axis=0)[:, :112]
 
@@ -434,10 +435,10 @@
     far_one, hidden_two = lax.optimization_barrier((far_one, hidden_two))
 
     half = HEADS // 2
-    first = attention(qc_own, kv_one, far_one, proj_out, (0, half))
-    first, kv_two = lax.optimization_barrier((first, kv_two))
+    first = attention(own_rows, far_one, proj_out, (0, half))
+    first, proj_out = lax.optimization_barrier((first, proj_out))
     own_part, far_edge, sent, out_term, own_qkv, far_kv = attention(
-        qc_own, kv_two, far_two, proj_out, (half, HEADS), first, proj_qkv
+        own_rows, far_two, proj_out, (half, HEADS), first, proj_qkv
     )
     sent, hid_far = lax.optimization_barrier((sent, hid_far))
     hid_rows = to_rows(hidden_two, hid_far)

time: 252 us -> 262 us (1.040)
  blocking collectives: 56.6 us -> 80.8 us
  waiting for transfers between devices: 44.1 us -> 35.1 us
  starting transfers between devices: 87.6 us -> 82.8 us
    all_to_all x1, blocking collectives: 23 us -> 39.4 us  [reduce_all(): lax.all_to_all(terms.reshape(32, part, channels), ('x', 'y', 'core'), 0,...]
    ppermute x2, waiting for transfers between devices: 8.71 us -> 0.01 us  [the longest x1 0.01 us: on_device(): far_one = lax.ppermute(own_rows[:, :GROWN], 'zh', SWAP)]
    all_to_all x1, blocking collectives: 19.7 us -> 27.5 us  [reduce_all(): band = lax.all_to_all(band, ('zh', 'zl'), 0, 0, tiled=True)]
    all_to_all x3 -> x2, waiting for transfers between devices: 0.16 us -> 5.8 us  [to_rows(): lax.all_to_all(jnp.concatenate(grown, axis=1), PLANE, 0, 0, tiled=True)]
    ppermute x1, waiting for transfers between devices: 7.09 us -> 1.46 us  [on_device(): from_far = lax.ppermute(sent, 'zh', SWAP)]
    ppermute x1, starting transfers between devices: 7.15 us -> 3.93 us  [on_device(): from_far = lax.ppermute(sent, 'zh', SWAP)]
    all_to_all x3 -> x2, starting transfers between devices: 15.7 us -> 13.7 us  [to_rows(): lax.all_to_all(jnp.concatenate(grown, axis=1), PLANE, 0, 0, tiled=True)]
    unnamed x53 -> x48, local copies, waits for them, and re-layouts: 5.73 us -> 5.75 us
  transfers between devices with their start and end apart: 15 -> 14, of which waited for: 10 -> 9; matrix products, arithmetic and copies ran while one was open for 3% -> 3% of each run, Pallas kernels for 15% -> 14%
where the time goes in v6:
time: 262 us; the launch traced here: 261 us
  starting transfers between devices  82.8 us (32%)
  blocking collectives  80.8 us (31%)
  Pallas kernels  39.9 us (15%)
  waiting for transfers between devices  35.1 us (13%)
  local copies, waits for them, and re-layouts  11 us (4%)
  other arithmetic  8.69 us (3%)
    all_to_all x1, blocking collectives, reduce_all(): lax.all_to_all(terms.reshape(32, part, channels), ('x', 'y', 'core'), 0,...  39.4 us
    pallas_call x2, Pallas kernels, attention(): pl.pallas_call(functools.partial(attend_rows, heads=heads, last=first is...  35.1 us
    all_to_all x1, blocking collectives, reduce_all(): band = lax.all_to_all(band, ('zh', 'zl'), 0, 0, tiled=True)  27.5 us
    ppermute x1, starting transfers between devices, exchange_lon(): outer = lax.ppermute(jnp.where(at_zero, left, right), LON_AXES, pairs)  16.8 us
    all_to_all x1, blocking collectives, reduce_all(): lax.all_to_all(jnp.broadcast_to(band[None], (16, piece)), ('zh', 'zl'), 0...  13.9 us
    all_to_all x2, starting transfers between devices, to_rows(): lax.all_to_all(jnp.concatenate(grown, axis=1), PLANE, 0, 0, tiled=True)  13.7 us
    all_to_all x1, waiting for transfers between devices, reduce_all(): lax.all_to_all(jnp.broadcast_to(band[None], (32, part, channels)), ('x',...  12.8 us
    ppermute x1, starting transfers between devices, on_device(): hid_far = lax.ppermute(hidden_two, 'zh', SWAP)  10.4 us
  transfers between devices with their start and end apart: 14, of which 9 were waited for; matrix products, arithmetic and copies ran while one was open for 3% of the time, Pallas kernels for 14%

profile of v6, /device:TPU:1, one launch (start us, length us, event | category | flops | bytes accessed | tf_op | source)
XLA Modules:
  0.0 260.5 jit_solution(17057343211002188043)
XLA Ops:
  1.7 1.0 copy.40
  2.9 16.8 %collective-permute-start = (bf16[8,16,128]{2,1,0:T(8,128)(2,1)S(1)}, bf16[8,16,128]{2,1,0:T(8,128)(2,1)S(1)}, u32[]{:S(2)}, u32[]{:S(2)}) collective-permute-start(bf16[8,16,128]{2,1,0:T(8,128)(2,1)S(1)} %get-tuple-element.111), channel_id=1, source_target_pairs={{0,480},{32,64},{64,32},{96,128},{128,96},{160,192},{192,160},{224... | collective-permute-start | bytes 98312 | tf_op jit(solution)/shard_map/ppermute | solution.py:45
  19.7 3.9 %collective-permute-start.1 = (bf16[8,16,128]{2,1,0:T(8,128)(2,1)S(1)}, bf16[8,16,128]{2,1,0:T(8,128)(2,1)S(1)}, u32[]{:S(2)}, u32[]{:S(2)}) collective-permute-start(bf16[8,16,128]{2,1,0:T(8,128)(2,1)S(1)} %get-tuple-element.110), channel_id=1, source_target_pairs={{0,32},{32,0},{1,33},{33,1},{2,34},{34,2},{3,35},{35,3},{4,36},{36... | collective-permute-start | bytes 98312 | tf_op jit(solution)/shard_map/ppermute | solution.py:43
  26.2 4.6 %all-to-all-start = ((bf16[8,384,128]{2,1,0:T(8,128)(2,1)}), bf16[8,384,128]{2,1,0:T(8,128)(2,1)S(1)}, u32[]{:S(2)}, u32[]{:S(2)}) async-start(bf16[8,384,128]{2,1,0:T(8,128)(2,1)} %fusion.4), calls=%async_computation | async-start | bytes 1572864 | tf_op jit(solution)/shard_map/all_to_all | solution.py:396
  31.1 2.3 collective-permute-start.2
  33.4 1.3 collective-permute-start.3
  35.6 2.0 collective-permute-done.2
  37.6 3.8 %collective-permute-done.3 = bf16[6,128,128]{2,1,0:T(8,128)(2,1)S(1)} collective-permute-done((bf16[6,128,128]{2,1,0:T(8,128)(2,1)S(1)}, bf16[6,128,128]{2,1,0:T(8,128)(2,1)S(1)}, u32[]{:S(2)}, u32[]{:S(2)}) %collective-permute-start.3) | collective-permute-done | bytes 196640 | tf_op jit(solution)/shard_map/ppermute | solution.py:52
  41.4 1.7 all-to-all-done.refs_0_
  43.2 10.1 %collective-permute-start.5 = (bf16[8,96,128]{2,1,0:T(8,128)(2,1)S(1)}, bf16[8,96,128]{2,1,0:T(8,128)(2,1)S(1)}, u32[]{:S(2)}, u32[]{:S(2)}) collective-permute-start(bf16[8,96,128]{2,1,0:T(8,128)(2,1)S(1)} %get-tuple-element.86), channel_id=1, source_target_pairs={{0,64},{64,0},{1,65},{65,1},{2,66},{66,2},{3,67},{67,3},{4,68},{68... | collective-permute-start | bytes 589832 | tf_op jit(solution)/shard_map/ppermute | solution.py:428
  53.3 3.9 %collective-permute-start.4 = (bf16[8,96,128]{2,1,0:T(8,128)(2,1)S(1)}, bf16[8,96,128]{2,1,0:T(8,128)(2,1)S(1)}, u32[]{:S(2)}, u32[]{:S(2)}) collective-permute-start(bf16[8,96,128]{2,1,0:T(8,128)(2,1)S(1)} %get-tuple-element.87), channel_id=1, source_target_pairs={{0,64},{64,0},{1,65},{65,1},{2,66},{66,2},{3,67},{67,3},{4,68},{68... | collective-permute-start | bytes 589832 | tf_op jit(solution)/shard_map/ppermute | solution.py:429
  57.4 2.5 forward_block.1
  60.7 10.4 %collective-permute-start.6 = (bf16[8,96,128]{2,1,0:T(8,128)(2,1)S(1)}, bf16[8,96,128]{2,1,0:T(8,128)(2,1)S(1)}, u32[]{:S(2)}, u32[]{:S(2)}) collective-permute-start(bf16[8,96,128]{2,1,0:T(8,128)(2,1)S(1)} %get-tuple-element.60), channel_id=1, source_target_pairs={{0,64},{64,0},{1,65},{65,1},{2,66},{66,2},{3,67},{67,3},{4,68},{68... | collective-permute-start | bytes 589832 | tf_op jit(solution)/shard_map/ppermute | solution.py:434
  71.1 17.4 %attend_rows.2 = (bf16[768,128]{1,0:T(8,128)(2,1)S(1)}, bf16[768,384]{1,0:T(8,128)(2,1)S(1)}, bf16[768,256]{1,0:T(8,128)(2,1)S(1)}) custom-call(bf16[8,384,128]{2,1,0:T(8,128)(2,1)S(1)} %all-to-all-done.refs_0_, bf16[8,96,128]{2,1,0:T(8,128)(2,1)S(1)} %collective-permute-done.5.refs_1_, bf16[128,128]{1,0:T(8,128)(2,1)S(1)} %copy-done.5), custom_call_target="tpu_custom_call" | custom-call | flops 7247757312 | bytes 1572864 | tf_op jit(solution)/shard_map/attend_rows/pallas_call | solution.py:189
  88.5 17.7 %attend_rows.3 = (f32[8,96,128]{2,1,0:T(8,128)S(1)}, f32[8,8,128]{2,1,0:T(8,128)S(1)}, bf16[8,96,128]{2,1,0:T(8,128)(2,1)S(1)}, f32[128,128]{1,0:T(8,128)S(1)}, ...) custom-call(bf16[8,384,128]{2,1,0:T(8,128)(2,1)S(1)} %all-to-all-done.refs_0_, ...), custom_call_target="tpu_custom_call" | custom-call | flops 7247757312 | bytes 1572864 | tf_op jit(solution)/shard_map/attend_rows/pallas_call | solution.py:189
  106.3 3.9 %collective-permute-start.7 = (bf16[8,96,128]{2,1,0:T(8,128)(2,1)S(1)}, bf16[8,96,128]{2,1,0:T(8,128)(2,1)}, u32[]{:S(2)}, u32[]{:S(2)}) collective-permute-start(bf16[8,96,128]{2,1,0:T(8,128)(2,1)S(1)} %get-tuple-element.52), channel_id=1, source_target_pairs={{0,64},{64,0},{1,65},{65,1},{2,66},{66,2},{3,67},{67,3},{4,68},{68... | collective-permute-start | bytes 589832 | tf_op jit(solution)/shard_map/ppermute | solution.py:445
  111.1 9.0 %all-to-all-start.2 = ((bf16[8,192,128]{2,1,0:T(8,128)(2,1)}), bf16[8,192,128]{2,1,0:T(8,128)(2,1)S(1)}, u32[]{:S(2)}, u32[]{:S(2)}) async-start(bf16[8,192,128]{2,1,0:T(8,128)(2,1)} %pad_maximum_fusion.3), calls=%async_computation.2 | async-start | bytes 786432 | tf_op jit(solution)/shard_map/all_to_all | solution.py:396
  120.1 1.5 collective-permute-done.7
  124.2 4.1 %all-to-all-done.2 = bf16[8,192,128]{2,1,0:T(8,128)(2,1)S(1)} async-done(((bf16[8,192,128]{2,1,0:T(8,128)(2,1)}), bf16[8,192,128]{2,1,0:T(8,128)(2,1)S(1)}, u32[]{:S(2)}, u32[]{:S(2)}) %all-to-all-start.2) | async-done | bytes 393248 | tf_op jit(solution)/shard_map/all_to_all | solution.py:396
  129.0 7.2 %all-to-all-start.1 = ((bf16[8,112,128]{2,1,0:T(8,128)(2,1)}), bf16[8,112,128]{2,1,0:T(8,128)(2,1)S(1)}, u32[]{:S(2)}, u32[]{:S(2)}) async-start(bf16[8,112,128]{2,1,0:T(8,128)(2,1)} %bitcast.4), calls=%async_computation.1 | async-start | bytes 458752 | tf_op jit(solution)/shard_map/all_to_all | solution.py:457
  136.2 1.1 fusion.28
  138.0 4.3 %all-to-all-done.1 = bf16[8,112,128]{2,1,0:T(8,128)(2,1)S(1)} async-done(((bf16[8,112,128]{2,1,0:T(8,128)(2,1)}), bf16[8,112,128]{2,1,0:T(8,128)(2,1)S(1)}, u32[]{:S(2)}, u32[]{:S(2)}) %all-to-all-start.1) | async-done | bytes 229408 | tf_op jit(solution)/shard_map/all_to_all | solution.py:457
  142.5 1.4 collective-permute-start.8
  144.0 1.6 collective-permute-start.9
  146.5 4.0 %collective-permute-done.9 = bf16[6,112,128]{2,1,0:T(8,128)(2,1)S(1)} collective-permute-done((bf16[6,112,128]{2,1,0:T(8,128)(2,1)S(1)}, bf16[6,112,128]{2,1,0:T(8,128)(2,1)S(1)}, u32[]{:S(2)}, u32[]{:S(2)}) %collective-permute-start.9) | collective-permute-done | bytes 172064 | tf_op jit(solution)/shard_map/ppermute | solution.py:52
  150.8 2.3 backward_block.1
  153.2 39.4 %all_to_all.41 = bf16[32,88,128]{2,1,0:T(8,128)(2,1)S(1)} all-to-all(bf16[32,88,128]{2,1,0:T(8,128)(2,1)S(1)} %bitcast.22), channel_id=1, replica_groups=mesh['x'=4,'zh'=2,'core'=2,'zl'=8,'y'=4] {'x','y','core'}, dimensions={0} | all-to-all | bytes 1441792 | tf_op jit(solution)/shard_map/all_to_all | solution.py:372
  194.2 27.5 %all_to_all.42 = bf16[16,2,352]{2,1,0:T(2,128)(2,1)S(1)} all-to-all(bf16[16,2,352]{2,1,0:T(2,128)(2,1)S(1)} %reshape.80), channel_id=1, replica_groups=mesh['x'=4,'zh'=2,'core'=2,'zl'=8,'y'=4] {'zh','zl'}, dimensions={0} | all-to-all | bytes 45056 | tf_op jit(solution)/shard_map/all_to_all | solution.py:376
  222.7 13.9 %all_to_all.43 = bf16[16,2,352]{2,1,0:T(2,128)(2,1)S(1)} all-to-all(bf16[16,2,352]{2,1,0:T(2,128)(2,1)S(1)} %reshape.82), channel_id=1, replica_groups=mesh['x'=4,'zh'=2,'core'=2,'zl'=8,'y'=4] {'zh','zl'}, dimensions={0} | all-to-all | bytes 45056 | tf_op jit(solution)/shard_map/all_to_all | solution.py:378
  238.0 6.3 %all-to-all-start.6 = ((bf16[32,88,128]{2,1,0:T(8,128)(2,1)}), bf16[32,88,128]{2,1,0:T(8,128)(2,1)S(1)}, u32[]{:S(2)}, u32[]{:S(2)}) async-start(bf16[32,88,128]{2,1,0:T(8,128)(2,1)} %broadcast_in_dim.31), calls=%async_computation.6 | async-start | bytes 1441792 | tf_op jit(solution)/shard_map/all_to_all | solution.py:381
  245.1 12.8 %all-to-all-done.6 = bf16[32,88,128]{2,1,0:T(8,128)(2,1)S(1)} async-done(((bf16[32,88,128]{2,1,0:T(8,128)(2,1)}), bf16[32,88,128]{2,1,0:T(8,128)(2,1)S(1)}, u32[]{:S(2)}, u32[]{:S(2)}) %all-to-all-start.6) | async-done | bytes 720928 | tf_op jit(solution)/shard_map/all_to_all | solution.py:381
  258.7 1.1 fusion.26
  (121 shorter events, 18.2 us)
Async XLA Ops:
  0.6 24.0 %copy-start.18 = (bf16[8,90,128]{2,0,1:T(8,128)(2,1)S(1)}, bf16[8,90,128]{2,0,1:T(8,128)(2,1)}, u32[]{:S(2)}) copy-start(bf16[8,90,128]{2,0,1:T(8,128)(2,1)} %param.11) | copy-start | bytes 552964
  0.6 24.2 %copy-start.19 = (bf16[8,90,128]{2,0,1:T(8,128)(2,1)S(1)}, bf16[8,90,128]{2,0,1:T(8,128)(2,1)}, u32[]{:S(2)}) copy-start(bf16[8,90,128]{2,0,1:T(8,128)(2,1)} %param.12) | copy-start | bytes 552964
  1.7 33.1 %copy-start.10 = (bf16[8,90,128]{2,1,0:T(8,128)(2,1)}, bf16[8,90,128]{2,1,0:T(8,128)(2,1)S(1)}, u32[]{:S(2)}) copy-start(bf16[8,90,128]{2,1,0:T(8,128)(2,1)S(1)} %copy.41) | copy-start | bytes 552964
  2.9 21.7 %collective-permute-start = (bf16[8,16,128]{2,1,0:T(8,128)(2,1)S(1)}, bf16[8,16,128]{2,1,0:T(8,128)(2,1)S(1)}, u32[]{:S(2)}, u32[]{:S(2)}) collective-permute-start(bf16[8,16,128]{2,1,0:T(8,128)(2,1)S(1)} %get-tuple-element.111), channel_id=1, source_target_pairs={{0,480},{32,64},{64,32},{96,128},{128,96},{160,192},{192,160},{224... | collective-permute-start | bytes 98312 | tf_op jit(solution)/shard_map/ppermute | solution.py:45
  19.7 4.9 %collective-permute-start.1 = (bf16[8,16,128]{2,1,0:T(8,128)(2,1)S(1)}, bf16[8,16,128]{2,1,0:T(8,128)(2,1)S(1)}, u32[]{:S(2)}, u32[]{:S(2)}) collective-permute-start(bf16[8,16,128]{2,1,0:T(8,128)(2,1)S(1)} %get-tuple-element.110), channel_id=1, source_target_pairs={{0,32},{32,0},{1,33},{33,1},{2,34},{34,2},{3,35},{35,3},{4,36},{36... | collective-permute-start | bytes 98312 | tf_op jit(solution)/shard_map/ppermute | solution.py:43
  26.2 16.9 %all-to-all-start = ((bf16[8,384,128]{2,1,0:T(8,128)(2,1)}), bf16[8,384,128]{2,1,0:T(8,128)(2,1)S(1)}, u32[]{:S(2)}, u32[]{:S(2)}) async-start(bf16[8,384,128]{2,1,0:T(8,128)(2,1)} %fusion.4), calls=%async_computation | async-start | bytes 1572864 | tf_op jit(solution)/shard_map/all_to_all | solution.py:396
  31.0 12.2 %copy-start.13 = (bf16[8,28,128]{2,1,0:T(8,128)(2,1)}, bf16[8,28,128]{2,1,0:T(8,128)(2,1)S(1)}, u32[]{:S(2)}) copy-start(bf16[8,28,128]{2,1,0:T(8,128)(2,1)S(1)} %broadcast_in_dim.26) | copy-start | bytes 172036
  31.1 6.5 %collective-permute-start.2 = (bf16[6,128,128]{2,1,0:T(8,128)(2,1)S(1)}, bf16[6,128,128]{2,1,0:T(8,128)(2,1)S(1)}, u32[]{:S(2)}, u32[]{:S(2)}) collective-permute-start(bf16[6,128,128]{2,1,0:T(8,128)(2,1)S(1)} %get-tuple-element.91), channel_id=1, source_target_pairs={{0,1},{1,2},{2,3},{3,4},{4,5},{5,6},{6,7},{7,8},{8,9},{9,10},{10,1... | collective-permute-start | bytes 589832 | tf_op jit(solution)/shard_map/ppermute | solution.py:51
  33.4 8.0 %collective-permute-start.3 = (bf16[6,128,128]{2,1,0:T(8,128)(2,1)S(1)}, bf16[6,128,128]{2,1,0:T(8,128)(2,1)S(1)}, u32[]{:S(2)}, u32[]{:S(2)}) collective-permute-start(bf16[6,128,128]{2,1,0:T(8,128)(2,1)S(1)} %get-tuple-element.90), channel_id=1, source_target_pairs={{1,0},{2,1},{3,2},{4,3},{5,4},{6,5},{7,6},{8,7},{9,8},{10,9},{11,1... | collective-permute-start | bytes 589832 | tf_op jit(solution)/shard_map/ppermute | solution.py:52
  35.6 21.8 %copy-start = (bf16[3,3,128,128]{3,2,1,0:T(8,128)(2,1)S(1)}, bf16[3,3,128,128]{3,2,1,0:T(8,128)(2,1)}, u32[]{:S(2)}) copy-start(bf16[3,3,128,128]{3,2,1,0:T(8,128)(2,1)} %near_ref.3) | copy-start | bytes 884740
  35.6 21.8 %copy-start.2 = (bf16[3,3,128,128]{3,2,1,0:T(8,128)(2,1)S(1)}, bf16[3,3,128,128]{3,2,1,0:T(8,128)(2,1)}, u32[]{:S(2)}) copy-start(bf16[3,3,128,128]{3,2,1,0:T(8,128)(2,1)} %dil_ref.1) | copy-start | bytes 884740
  37.6 15.7 %copy-start.16 = (bf16[6,128,128]{2,1,0:T(8,128)(2,1)}, bf16[6,128,128]{2,1,0:T(8,128)(2,1)S(1)}, u32[]{:S(2)}) copy-start(bf16[6,128,128]{2,1,0:T(8,128)(2,1)S(1)} %collective-permute-done.2) | copy-start | bytes 589828
  41.4 16.0 %copy-start.17 = (bf16[6,128,128]{2,1,0:T(8,128)(2,1)}, bf16[6,128,128]{2,1,0:T(8,128)(2,1)S(1)}, u32[]{:S(2)}) copy-start(bf16[6,128,128]{2,1,0:T(8,128)(2,1)S(1)} %collective-permute-done.3) | copy-start | bytes 589828
  43.2 27.8 %collective-permute-start.5 = (bf16[8,96,128]{2,1,0:T(8,128)(2,1)S(1)}, bf16[8,96,128]{2,1,0:T(8,128)(2,1)S(1)}, u32[]{:S(2)}, u32[]{:S(2)}) collective-permute-start(bf16[8,96,128]{2,1,0:T(8,128)(2,1)S(1)} %get-tuple-element.86), channel_id=1, source_target_pairs={{0,64},{64,0},{1,65},{65,1},{2,66},{66,2},{3,67},{67,3},{4,68},{68... | collective-permute-start | bytes 589832 | tf_op jit(solution)/shard_map/ppermute | solution.py:428
  53.3 35.2 %collective-permute-start.4 = (bf16[8,96,128]{2,1,0:T(8,128)(2,1)S(1)}, bf16[8,96,128]{2,1,0:T(8,128)(2,1)S(1)}, u32[]{:S(2)}, u32[]{:S(2)}) collective-permute-start(bf16[8,96,128]{2,1,0:T(8,128)(2,1)S(1)} %get-tuple-element.87), channel_id=1, source_target_pairs={{0,64},{64,0},{1,65},{65,1},{2,66},{66,2},{3,67},{67,3},{4,68},{68... | collective-permute-start | bytes 589832 | tf_op jit(solution)/shard_map/ppermute | solution.py:429
  57.4 13.7 %copy-start.5 = (bf16[128,128]{1,0:T(8,128)(2,1)S(1)}, bf16[128,128]{1,0:T(8,128)(2,1)}, u32[]{:S(2)}) copy-start(bf16[128,128]{1,0:T(8,128)(2,1)} %refs_2_.2) | copy-start | bytes 98308
  60.7 27.8 %copy-start.8 = (bf16[16,112,128]{2,1,0:T(8,128)(2,1)}, bf16[16,112,128]{2,1,0:T(8,128)(2,1)S(1)}, u32[]{:S(2)}) copy-start(bf16[16,112,128]{2,1,0:T(8,128)(2,1)S(1)} %get-tuple-element.57.one_ref) | copy-start | bytes 1376260
  60.7 27.8 %copy-start.4 = (bf16[128,384]{1,0:T(8,128)(2,1)S(1)}, bf16[128,384]{1,0:T(8,128)(2,1)}, u32[]{:S(2)}) copy-start(bf16[128,384]{1,0:T(8,128)(2,1)} %refs_6_.1) | copy-start | bytes 294916
  60.7 45.6 %collective-permute-start.6 = (bf16[8,96,128]{2,1,0:T(8,128)(2,1)S(1)}, bf16[8,96,128]{2,1,0:T(8,128)(2,1)S(1)}, u32[]{:S(2)}, u32[]{:S(2)}) collective-permute-start(bf16[8,96,128]{2,1,0:T(8,128)(2,1)S(1)} %get-tuple-element.60), channel_id=1, source_target_pairs={{0,64},{64,0},{1,65},{65,1},{2,66},{66,2},{3,67},{67,3},{4,68},{68... | collective-permute-start | bytes 589832 | tf_op jit(solution)/shard_map/ppermute | solution.py:434
  88.5 21.7 %copy-start.11 = (bf16[8,90,128]{2,1,0:T(8,128)(2,1)S(1)}, bf16[8,90,128]{2,1,0:T(8,128)(2,1)}, u32[]{:S(2)}) copy-start(bf16[8,90,128]{2,1,0:T(8,128)(2,1)} %copy-done.10) | copy-start | bytes 552964
  88.5 21.7 %copy-start.14 = (bf16[8,28,128]{2,1,0:T(8,128)(2,1)S(1)}, bf16[8,28,128]{2,1,0:T(8,128)(2,1)}, u32[]{:S(2)}) copy-start(bf16[8,28,128]{2,1,0:T(8,128)(2,1)} %copy-done.13) | copy-start | bytes 172036
  88.5 21.7 %slice-start = ((bf16[6,128,128]{2,1,0:T(8,128)(2,1)}), bf16[1,128,128]{2,1,0:T(8,128)(2,1)S(1)}, s32[]{:S(2)}) async-start(bf16[6,128,128]{2,1,0:T(8,128)(2,1)} %copy-done.16), calls=%async_computation.7 | async-start | bytes 65536 | tf_op jit(solution)/shard_map/slice | solution.py:431
  88.5 21.7 %slice-start.1 = ((bf16[6,128,128]{2,1,0:T(8,128)(2,1)}), bf16[1,128,128]{2,1,0:T(8,128)(2,1)S(1)}, s32[]{:S(2)}) async-start(bf16[6,128,128]{2,1,0:T(8,128)(2,1)} %copy-done.17), calls=%async_computation.8 | async-start | bytes 65536 | tf_op jit(solution)/shard_map/slice | solution.py:431
  106.3 15.3 %collective-permute-start.7 = (bf16[8,96,128]{2,1,0:T(8,128)(2,1)S(1)}, bf16[8,96,128]{2,1,0:T(8,128)(2,1)}, u32[]{:S(2)}, u32[]{:S(2)}) collective-permute-start(bf16[8,96,128]{2,1,0:T(8,128)(2,1)S(1)} %get-tuple-element.52), channel_id=1, source_target_pairs={{0,64},{64,0},{1,65},{65,1},{2,66},{66,2},{3,67},{67,3},{4,68},{68... | collective-permute-start | bytes 589832 | tf_op jit(solution)/shard_map/ppermute | solution.py:445
  111.1 17.1 %all-to-all-start.2 = ((bf16[8,192,128]{2,1,0:T(8,128)(2,1)}), bf16[8,192,128]{2,1,0:T(8,128)(2,1)S(1)}, u32[]{:S(2)}, u32[]{:S(2)}) async-start(bf16[8,192,128]{2,1,0:T(8,128)(2,1)} %pad_maximum_fusion.3), calls=%async_computation.2 | async-start | bytes 786432 | tf_op jit(solution)/shard_map/all_to_all | solution.py:396
  129.0 13.4 %all-to-all-start.1 = ((bf16[8,112,128]{2,1,0:T(8,128)(2,1)}), bf16[8,112,128]{2,1,0:T(8,128)(2,1)S(1)}, u32[]{:S(2)}, u32[]{:S(2)}) async-start(bf16[8,112,128]{2,1,0:T(8,128)(2,1)} %bitcast.4), calls=%async_computation.1 | async-start | bytes 458752 | tf_op jit(solution)/shard_map/all_to_all | solution.py:457
  142.5 4.0 %collective-permute-start.8 = (bf16[6,112,128]{2,1,0:T(8,128)(2,1)S(1)}, bf16[6,112,128]{2,1,0:T(8,128)(2,1)S(1)}, u32[]{:S(2)}, u32[]{:S(2)}) collective-permute-start(bf16[6,112,128]{2,1,0:T(8,128)(2,1)S(1)} %pad_maximum_fusion.16), channel_id=1, source_target_pairs={{0,1},{1,2},{2,3},{3,4},{4,5},{5,6},{6,7},{7,8},{8,9},{9,10},{10,1... | collective-permute-start | bytes 516104 | tf_op jit(solution)/shard_map/ppermute | solution.py:51
  143.9 6.8 %copy-start.1 = (bf16[3,3,128,128]{3,2,1,0:T(8,128)(2,1)S(1)}, bf16[3,3,128,128]{3,2,1,0:T(8,128)(2,1)}, u32[]{:S(2)}) copy-start(bf16[3,3,128,128]{3,2,1,0:T(8,128)(2,1)} %near_ref.3) | copy-start | bytes 884740
  143.9 6.8 %copy-start.3 = (bf16[3,3,128,128]{3,2,1,0:T(8,128)(2,1)S(1)}, bf16[3,3,128,128]{3,2,1,0:T(8,128)(2,1)}, u32[]{:S(2)}) copy-start(bf16[3,3,128,128]{3,2,1,0:T(8,128)(2,1)} %dil_ref.1) | copy-start | bytes 884740
  143.9 6.8 %copy-start.7 = (f32[10,112,128]{2,1,0:T(8,128)S(1)}, f32[10,112,128]{2,1,0:T(8,128)}, u32[]{:S(2)}) copy-start(f32[10,112,128]{2,1,0:T(8,128)} %copy-done.6) | copy-start | bytes 1720324
  144.0 6.6 %collective-permute-start.9 = (bf16[6,112,128]{2,1,0:T(8,128)(2,1)S(1)}, bf16[6,112,128]{2,1,0:T(8,128)(2,1)S(1)}, u32[]{:S(2)}, u32[]{:S(2)}) collective-permute-start(bf16[6,112,128]{2,1,0:T(8,128)(2,1)S(1)} %pad_maximum_fusion.17), channel_id=1, source_target_pairs={{1,0},{2,1},{3,2},{4,3},{5,4},{6,5},{7,6},{8,7},{9,8},{10,9},{11,1... | collective-permute-start | bytes 516104 | tf_op jit(solution)/shard_map/ppermute | solution.py:52
  238.0 19.9 %all-to-all-start.6 = ((bf16[32,88,128]{2,1,0:T(8,128)(2,1)}), bf16[32,88,128]{2,1,0:T(8,128)(2,1)S(1)}, u32[]{:S(2)}, u32[]{:S(2)}) async-start(bf16[32,88,128]{2,1,0:T(8,128)(2,1)} %broadcast_in_dim.31), calls=%async_computation.6 | async-start | bytes 1441792 | tf_op jit(solution)/shard_map/all_to_all | solution.py:381
  (4 other events, 14.6 us)

commit v7 on v6

--- a/solution.py
+++ b/solution.py
@@ -440,9 +440,8 @@
     own_part, far_edge, sent, out_term, own_qkv, far_kv = attention(
         own_rows, far_two, proj_out, (half, HEADS), first, proj_qkv
     )
-    sent, hid_far = lax.optimization_barrier((sent, hid_far))
-    hid_rows = to_rows(hidden_two, hid_far)
     from_far = lax.ppermute(sent, "zh", SWAP)
+    from_far, hid_far = lax.optimization_barrier((from_far, hid_far))
     whole = (own_part + from_far.astype(jnp.float32)).astype(jnp.bfloat16)
     whole = whole.reshape(4, 2, GROWN, channels)
     edge = from_far.reshape(4, 2, GROWN, channels)[:, :, COLS : COLS + EDGE].astype(jnp.float32)
@@ -455,6 +454,7 @@
     blank = jnp.zeros((4, 2, 12, channels), jnp.bfloat16)
     attn_x = jnp.concatenate([left, whole[:, :, :COLS], right, blank], axis=2)
     attn_x = lax.all_to_all(attn_x.reshape(8, 112, channels), PLANE, 0, 0, tiled=True)
+    hid_rows = to_rows(hidden_two, hid_far)
     hid_flat = hid_rows[:, :GROWN].reshape(-1, channels)
     far_flat = hid_rows[:, GROWN:].reshape(-1, channels)
     query_term = contract_rows(hid_flat, own_qkv[:, :channels])

time: 262 us -> 269 us (1.027)
    all_to_all x1, blocking collectives: 27.5 us -> 33.4 us  [reduce_all(): band = lax.all_to_all(band, ('zh', 'zl'), 0, 0, tiled=True)]
    ppermute x1, waiting for transfers between devices: 1.46 us -> 6.91 us  [on_device(): from_far = lax.ppermute(sent, 'zh', SWAP)]
    all_to_all x1, blocking collectives: 39.4 us -> 34.4 us  [reduce_all(): lax.all_to_all(terms.reshape(32, part, channels), ('x', 'y', 'core'), 0,...]
    all_to_all x1, starting transfers between devices: 7.19 us -> 11.5 us  [on_device(): lax.all_to_all(attn_x.reshape(8, 112, channels), PLANE, 0, 0, tiled=True)]
    all_to_all x2, starting transfers between devices: 13.7 us -> 9.59 us  [to_rows(): lax.all_to_all(jnp.concatenate(grown, axis=1), PLANE, 0, 0, tiled=True)]
    ppermute x2, waiting for transfers between devices: 7.83 us -> 4.38 us  [exchange_lat(): high = lax.ppermute(top, LAT_AXES, [(b, a) for a, b in chain])]
    slice x4 -> x2, local copies, waits for them, and re-layouts: 0.01 us -> 2.74 us  [on_device(): cot_near = jnp.concatenate([low[5:], cot_x, high[5:]], axis=0)[:, :112]]
  transfers between devices with their start and end apart: 14 -> 14, of which waited for: 9 -> 8; matrix products, arithmetic and copies ran while one was open for 3% -> 5% of each run, Pallas kernels for 14% -> 14%
where the time goes in v7:
time: 269 us; the launch traced here: 267 us
  starting transfers between devices  83.2 us (31%)
  blocking collectives  81.7 us (30%)
  Pallas kernels  40.5 us (15%)
  waiting for transfers between devices  36.2 us (13%)
  local copies, waits for them, and re-layouts  12.7 us (5%)
  other arithmetic  11 us (4%)
    pallas_call x2, Pallas kernels, attention(): pl.pallas_call(functools.partial(attend_rows, heads=heads, last=first is...  35.8 us
    all_to_all x1, blocking collectives, reduce_all(): lax.all_to_all(terms.reshape(32, part, channels), ('x', 'y', 'core'), 0,...  34.4 us
    all_to_all x1, blocking collectives, reduce_all(): band = lax.all_to_all(band, ('zh', 'zl'), 0, 0, tiled=True)  33.4 us
    ppermute x1, starting transfers between devices, exchange_lon(): outer = lax.ppermute(jnp.where(at_zero, left, right), LON_AXES, pairs)  16.8 us
    all_to_all x1, blocking collectives, reduce_all(): lax.all_to_all(jnp.broadcast_to(band[None], (16, piece)), ('zh', 'zl'), 0...  13.9 us
    all_to_all x1, waiting for transfers between devices, reduce_all(): lax.all_to_all(jnp.broadcast_to(band[None], (32, part, channels)), ('x',...  12.8 us
    all_to_all x1, starting transfers between devices, on_device(): lax.all_to_all(attn_x.reshape(8, 112, channels), PLANE, 0, 0, tiled=True)  11.5 us
    ppermute x1, starting transfers between devices, on_device(): hid_far = lax.ppermute(hidden_two, 'zh', SWAP)  10.4 us
  transfers between devices with their start and end apart: 14, of which 8 were waited for; matrix products, arithmetic and copies ran while one was open for 5% of the time, Pallas kernels for 14%

profile of v7, /device:TPU:1, one launch (start us, length us, event | category | flops | bytes accessed | tf_op | source)
XLA Modules:
  0.0 267.4 jit_solution(12502778658052778894)
XLA Ops:
  2.9 16.8 %collective-permute-start = (bf16[8,16,128]{2,1,0:T(8,128)(2,1)S(1)}, bf16[8,16,128]{2,1,0:T(8,128)(2,1)S(1)}, u32[]{:S(2)}, u32[]{:S(2)}) collective-permute-start(bf16[8,16,128]{2,1,0:T(8,128)(2,1)S(1)} %get-tuple-element.111), channel_id=1, source_target_pairs={{0,480},{32,64},{64,32},{96,128},{128,96},{160,192},{192,160},{224... | collective-permute-start | bytes 98312 | tf_op jit(solution)/shard_map/ppermute | solution.py:45
  19.7 3.9 %collective-permute-start.1 = (bf16[8,16,128]{2,1,0:T(8,128)(2,1)S(1)}, bf16[8,16,128]{2,1,0:T(8,128)(2,1)S(1)}, u32[]{:S(2)}, u32[]{:S(2)}) collective-permute-start(bf16[8,16,128]{2,1,0:T(8,128)(2,1)S(1)} %get-tuple-element.110), channel_id=1, source_target_pairs={{0,32},{32,0},{1,33},{33,1},{2,34},{34,2},{3,35},{35,3},{4,36},{36... | collective-permute-start | bytes 98312 | tf_op jit(solution)/shard_map/ppermute | solution.py:43
  26.2 4.6 %all-to-all-start = ((bf16[8,384,128]{2,1,0:T(8,128)(2,1)}), bf16[8,384,128]{2,1,0:T(8,128)(2,1)S(1)}, u32[]{:S(2)}, u32[]{:S(2)}) async-start(bf16[8,384,128]{2,1,0:T(8,128)(2,1)} %fusion.4), calls=%async_computation | async-start | bytes 1572864 | tf_op jit(solution)/shard_map/all_to_all | solution.py:396
  31.1 2.4 collective-permute-start.2
  33.6 1.3 collective-permute-start.3
  34.9 2.9 %collective-permute-done.2 = bf16[6,128,128]{2,1,0:T(8,128)(2,1)S(1)} collective-permute-done((bf16[6,128,128]{2,1,0:T(8,128)(2,1)S(1)}, bf16[6,128,128]{2,1,0:T(8,128)(2,1)S(1)}, u32[]{:S(2)}, u32[]{:S(2)}) %collective-permute-start.2) | collective-permute-done | bytes 196640 | tf_op jit(solution)/shard_map/ppermute | solution.py:51
  37.8 3.8 %collective-permute-done.3 = bf16[6,128,128]{2,1,0:T(8,128)(2,1)S(1)} collective-permute-done((bf16[6,128,128]{2,1,0:T(8,128)(2,1)S(1)}, bf16[6,128,128]{2,1,0:T(8,128)(2,1)S(1)}, u32[]{:S(2)}, u32[]{:S(2)}) %collective-permute-start.3) | collective-permute-done | bytes 196640 | tf_op jit(solution)/shard_map/ppermute | solution.py:52
  41.6 1.6 all-to-all-done.refs_0_
  43.2 10.1 %collective-permute-start.5 = (bf16[8,96,128]{2,1,0:T(8,128)(2,1)S(1)}, bf16[8,96,128]{2,1,0:T(8,128)(2,1)S(1)}, u32[]{:S(2)}, u32[]{:S(2)}) collective-permute-start(bf16[8,96,128]{2,1,0:T(8,128)(2,1)S(1)} %get-tuple-element.86), channel_id=1, source_target_pairs={{0,64},{64,0},{1,65},{65,1},{2,66},{66,2},{3,67},{67,3},{4,68},{68... | collective-permute-start | bytes 589832 | tf_op jit(solution)/shard_map/ppermute | solution.py:428
  53.3 3.9 %collective-permute-start.4 = (bf16[8,96,128]{2,1,0:T(8,128)(2,1)S(1)}, bf16[8,96,128]{2,1,0:T(8,128)(2,1)S(1)}, u32[]{:S(2)}, u32[]{:S(2)}) collective-permute-start(bf16[8,96,128]{2,1,0:T(8,128)(2,1)S(1)} %get-tuple-element.87), channel_id=1, source_target_pairs={{0,64},{64,0},{1,65},{65,1},{2,66},{66,2},{3,67},{67,3},{4,68},{68... | collective-permute-start | bytes 589832 | tf_op jit(solution)/shard_map/ppermute | solution.py:429
  57.4 2.5 forward_block.1
  59.9 10.4 %collective-permute-start.7 = (bf16[8,96,128]{2,1,0:T(8,128)(2,1)S(1)}, bf16[8,96,128]{2,1,0:T(8,128)(2,1)}, u32[]{:S(2)}, u32[]{:S(2)}) collective-permute-start(bf16[8,96,128]{2,1,0:T(8,128)(2,1)S(1)} %get-tuple-element.60), channel_id=1, source_target_pairs={{0,64},{64,0},{1,65},{65,1},{2,66},{66,2},{3,67},{67,3},{4,68},{68... | collective-permute-start | bytes 589832 | tf_op jit(solution)/shard_map/ppermute | solution.py:434
  70.3 17.4 %attend_rows.2 = (bf16[768,128]{1,0:T(8,128)(2,1)S(1)}, bf16[768,384]{1,0:T(8,128)(2,1)S(1)}, bf16[768,256]{1,0:T(8,128)(2,1)S(1)}) custom-call(bf16[8,384,128]{2,1,0:T(8,128)(2,1)S(1)} %all-to-all-done.refs_0_, bf16[8,96,128]{2,1,0:T(8,128)(2,1)S(1)} %collective-permute-done.5.refs_1_, bf16[128,128]{1,0:T(8,128)(2,1)S(1)} %copy-done.5), custom_call_target="tpu_custom_call" | custom-call | flops 7247757312 | bytes 1572864 | tf_op jit(solution)/shard_map/attend_rows/pallas_call | solution.py:189
  87.7 18.4 %attend_rows.3 = (f32[8,96,128]{2,1,0:T(8,128)S(1)}, f32[8,8,128]{2,1,0:T(8,128)S(1)}, bf16[8,96,128]{2,1,0:T(8,128)(2,1)}, f32[128,128]{1,0:T(8,128)S(1)}, bf16...) custom-call(bf16[8,384,128]{2,1,0:T(8,128)(2,1)S(1)} %all-to-all-done.refs_0_, ...), custom_call_target="tpu_custom_call" | custom-call | flops 7247757312 | bytes 1572864 | tf_op jit(solution)/shard_map/attend_rows/pallas_call | solution.py:189
  106.2 4.0 %collective-permute-start.6 = (bf16[8,96,128]{2,1,0:T(8,128)(2,1)}, bf16[8,96,128]{2,1,0:T(8,128)(2,1)S(1)}, u32[]{:S(2)}, u32[]{:S(2)}) collective-permute-start(bf16[8,96,128]{2,1,0:T(8,128)(2,1)} %get-tuple-element.51), channel_id=1, source_target_pairs={{0,64},{64,0},{1,65},{65,1},{2,66},{66,2},{3,67},{67,3},{4,68},{68... | collective-permute-start | bytes 589832 | tf_op jit(solution)/shard_map/ppermute | solution.py:443
  110.3 1.8 pad_maximum_fusion.10
  112.1 1.4 slice.217
  113.4 1.4 slice.218
  114.8 6.9 %collective-permute-done.6 = bf16[8,96,128]{2,1,0:T(8,128)(2,1)S(1)} collective-permute-done((bf16[8,96,128]{2,1,0:T(8,128)(2,1)}, bf16[8,96,128]{2,1,0:T(8,128)(2,1)S(1)}, u32[]{:S(2)}, u32[]{:S(2)}) %collective-permute-start.6) | collective-permute-done | bytes 196640 | tf_op jit(solution)/shard_map/ppermute | solution.py:443
  122.6 11.5 %all-to-all-start.1 = ((bf16[8,112,128]{2,1,0:T(8,128)(2,1)}), bf16[8,112,128]{2,1,0:T(8,128)(2,1)S(1)}, u32[]{:S(2)}, u32[]{:S(2)}) async-start(bf16[8,112,128]{2,1,0:T(8,128)(2,1)} %bitcast.4), calls=%async_computation.1 | async-start | bytes 458752 | tf_op jit(solution)/shard_map/all_to_all | solution.py:456
  135.0 1.7 pad_maximum_fusion.3
  136.7 3.6 %all-to-all-done.1 = bf16[8,112,128]{2,1,0:T(8,128)(2,1)S(1)} async-done(((bf16[8,112,128]{2,1,0:T(8,128)(2,1)}), bf16[8,112,128]{2,1,0:T(8,128)(2,1)S(1)}, u32[]{:S(2)}, u32[]{:S(2)}) %all-to-all-start.1) | async-done | bytes 229408 | tf_op jit(solution)/shard_map/all_to_all | solution.py:456
  140.4 5.0 %all-to-all-start.2 = ((bf16[8,192,128]{2,1,0:T(8,128)(2,1)}), bf16[8,192,128]{2,1,0:T(8,128)(2,1)}, u32[]{:S(2)}, u32[]{:S(2)}) async-start(bf16[8,192,128]{2,1,0:T(8,128)(2,1)} %pad_maximum_fusion.3), calls=%async_computation.2 | async-start | bytes 786432 | tf_op jit(solution)/shard_map/all_to_all | solution.py:396
  146.2 1.3 collective-permute-start.8
  148.2 1.5 collective-permute-start.9
  149.7 3.9 %all-to-all-done.2 = bf16[8,192,128]{2,1,0:T(8,128)(2,1)} async-done(((bf16[8,192,128]{2,1,0:T(8,128)(2,1)}), bf16[8,192,128]{2,1,0:T(8,128)(2,1)}, u32[]{:S(2)}, u32[]{:S(2)}) %all-to-all-start.2) | async-done | bytes 393248 | tf_op jit(solution)/shard_map/all_to_all | solution.py:396
  156.8 2.3 backward_block.1
  159.1 34.4 %all_to_all.41 = bf16[32,88,128]{2,1,0:T(8,128)(2,1)S(1)} all-to-all(bf16[32,88,128]{2,1,0:T(8,128)(2,1)S(1)} %bitcast.22), channel_id=1, replica_groups=mesh['x'=4,'zh'=2,'core'=2,'zl'=8,'y'=4] {'x','y','core'}, dimensions={0} | all-to-all | bytes 1441792 | tf_op jit(solution)/shard_map/all_to_all | solution.py:372
  195.1 33.4 %all_to_all.42 = bf16[16,2,352]{2,1,0:T(2,128)(2,1)S(1)} all-to-all(bf16[16,2,352]{2,1,0:T(2,128)(2,1)S(1)} %reshape.80), channel_id=1, replica_groups=mesh['x'=4,'zh'=2,'core'=2,'zl'=8,'y'=4] {'zh','zl'}, dimensions={0} | all-to-all | bytes 45056 | tf_op jit(solution)/shard_map/all_to_all | solution.py:376
  229.6 13.9 %all_to_all.43 = bf16[16,2,352]{2,1,0:T(2,128)(2,1)S(1)} all-to-all(bf16[16,2,352]{2,1,0:T(2,128)(2,1)S(1)} %reshape.82), channel_id=1, replica_groups=mesh['x'=4,'zh'=2,'core'=2,'zl'=8,'y'=4] {'zh','zl'}, dimensions={0} | all-to-all | bytes 45056 | tf_op jit(solution)/shard_map/all_to_all | solution.py:378
  244.9 6.3 %all-to-all-start.6 = ((bf16[32,88,128]{2,1,0:T(8,128)(2,1)}), bf16[32,88,128]{2,1,0:T(8,128)(2,1)S(1)}, u32[]{:S(2)}, u32[]{:S(2)}) async-start(bf16[32,88,128]{2,1,0:T(8,128)(2,1)} %broadcast_in_dim.31), calls=%async_computation.6 | async-start | bytes 1441792 | tf_op jit(solution)/shard_map/all_to_all | solution.py:381
  252.0 12.8 %all-to-all-done.6 = bf16[32,88,128]{2,1,0:T(8,128)(2,1)S(1)} async-done(((bf16[32,88,128]{2,1,0:T(8,128)(2,1)}), bf16[32,88,128]{2,1,0:T(8,128)(2,1)S(1)}, u32[]{:S(2)}, u32[]{:S(2)}) %all-to-all-start.6) | async-done | bytes 720928 | tf_op jit(solution)/shard_map/all_to_all | solution.py:381
  (119 shorter events, 18.9 us)
Async XLA Ops:
  0.6 24.0 %copy-start.17 = (bf16[8,90,128]{2,0,1:T(8,128)(2,1)S(1)}, bf16[8,90,128]{2,0,1:T(8,128)(2,1)}, u32[]{:S(2)}) copy-start(bf16[8,90,128]{2,0,1:T(8,128)(2,1)} %param.11) | copy-start | bytes 552964
  0.6 24.2 %copy-start.18 = (bf16[8,90,128]{2,0,1:T(8,128)(2,1)S(1)}, bf16[8,90,128]{2,0,1:T(8,128)(2,1)}, u32[]{:S(2)}) copy-start(bf16[8,90,128]{2,0,1:T(8,128)(2,1)} %param.12) | copy-start | bytes 552964
  1.7 29.4 %copy-start.10 = (bf16[8,90,128]{2,1,0:T(8,128)(2,1)}, bf16[8,90,128]{2,1,0:T(8,128)(2,1)S(1)}, u32[]{:S(2)}) copy-start(bf16[8,90,128]{2,1,0:T(8,128)(2,1)S(1)} %copy.41) | copy-start | bytes 552964
  2.9 21.7 %collective-permute-start = (bf16[8,16,128]{2,1,0:T(8,128)(2,1)S(1)}, bf16[8,16,128]{2,1,0:T(8,128)(2,1)S(1)}, u32[]{:S(2)}, u32[]{:S(2)}) collective-permute-start(bf16[8,16,128]{2,1,0:T(8,128)(2,1)S(1)} %get-tuple-element.111), channel_id=1, source_target_pairs={{0,480},{32,64},{64,32},{96,128},{128,96},{160,192},{192,160},{224... | collective-permute-start | bytes 98312 | tf_op jit(solution)/shard_map/ppermute | solution.py:45
  19.7 4.9 %collective-permute-start.1 = (bf16[8,16,128]{2,1,0:T(8,128)(2,1)S(1)}, bf16[8,16,128]{2,1,0:T(8,128)(2,1)S(1)}, u32[]{:S(2)}, u32[]{:S(2)}) collective-permute-start(bf16[8,16,128]{2,1,0:T(8,128)(2,1)S(1)} %get-tuple-element.110), channel_id=1, source_target_pairs={{0,32},{32,0},{1,33},{33,1},{2,34},{34,2},{3,35},{35,3},{4,36},{36... | collective-permute-start | bytes 98312 | tf_op jit(solution)/shard_map/ppermute | solution.py:43
  26.2 16.9 %all-to-all-start = ((bf16[8,384,128]{2,1,0:T(8,128)(2,1)}), bf16[8,384,128]{2,1,0:T(8,128)(2,1)S(1)}, u32[]{:S(2)}, u32[]{:S(2)}) async-start(bf16[8,384,128]{2,1,0:T(8,128)(2,1)} %fusion.4), calls=%async_computation | async-start | bytes 1572864 | tf_op jit(solution)/shard_map/all_to_all | solution.py:396
  31.1 22.2 %copy-start.12 = (bf16[8,28,128]{2,1,0:T(8,128)(2,1)}, bf16[8,28,128]{2,1,0:T(8,128)(2,1)S(1)}, u32[]{:S(2)}) copy-start(bf16[8,28,128]{2,1,0:T(8,128)(2,1)S(1)} %broadcast_in_dim.26) | copy-start | bytes 172036
  31.1 26.3 %copy-start = (bf16[3,3,128,128]{3,2,1,0:T(8,128)(2,1)S(1)}, bf16[3,3,128,128]{3,2,1,0:T(8,128)(2,1)}, u32[]{:S(2)}) copy-start(bf16[3,3,128,128]{3,2,1,0:T(8,128)(2,1)} %near_ref.3) | copy-start | bytes 884740
  31.1 26.3 %copy-start.2 = (bf16[3,3,128,128]{3,2,1,0:T(8,128)(2,1)S(1)}, bf16[3,3,128,128]{3,2,1,0:T(8,128)(2,1)}, u32[]{:S(2)}) copy-start(bf16[3,3,128,128]{3,2,1,0:T(8,128)(2,1)} %dil_ref.1) | copy-start | bytes 884740
  31.1 6.6 %collective-permute-start.2 = (bf16[6,128,128]{2,1,0:T(8,128)(2,1)S(1)}, bf16[6,128,128]{2,1,0:T(8,128)(2,1)S(1)}, u32[]{:S(2)}, u32[]{:S(2)}) collective-permute-start(bf16[6,128,128]{2,1,0:T(8,128)(2,1)S(1)} %get-tuple-element.91), channel_id=1, source_target_pairs={{0,1},{1,2},{2,3},{3,4},{4,5},{5,6},{6,7},{7,8},{8,9},{9,10},{10,1... | collective-permute-start | bytes 589832 | tf_op jit(solution)/shard_map/ppermute | solution.py:51
  33.6 8.0 %collective-permute-start.3 = (bf16[6,128,128]{2,1,0:T(8,128)(2,1)S(1)}, bf16[6,128,128]{2,1,0:T(8,128)(2,1)S(1)}, u32[]{:S(2)}, u32[]{:S(2)}) collective-permute-start(bf16[6,128,128]{2,1,0:T(8,128)(2,1)S(1)} %get-tuple-element.90), channel_id=1, source_target_pairs={{1,0},{2,1},{3,2},{4,3},{5,4},{6,5},{7,6},{8,7},{9,8},{10,9},{11,1... | collective-permute-start | bytes 589832 | tf_op jit(solution)/shard_map/ppermute | solution.py:52
  37.8 15.5 %copy-start.15 = (bf16[6,128,128]{2,1,0:T(8,128)(2,1)}, bf16[6,128,128]{2,1,0:T(8,128)(2,1)S(1)}, u32[]{:S(2)}) copy-start(bf16[6,128,128]{2,1,0:T(8,128)(2,1)S(1)} %collective-permute-done.2) | copy-start | bytes 589828
  41.6 11.8 %copy-start.16 = (bf16[6,128,128]{2,1,0:T(8,128)(2,1)}, bf16[6,128,128]{2,1,0:T(8,128)(2,1)S(1)}, u32[]{:S(2)}) copy-start(bf16[6,128,128]{2,1,0:T(8,128)(2,1)S(1)} %collective-permute-done.3) | copy-start | bytes 589828
  43.2 27.1 %collective-permute-start.5 = (bf16[8,96,128]{2,1,0:T(8,128)(2,1)S(1)}, bf16[8,96,128]{2,1,0:T(8,128)(2,1)S(1)}, u32[]{:S(2)}, u32[]{:S(2)}) collective-permute-start(bf16[8,96,128]{2,1,0:T(8,128)(2,1)S(1)} %get-tuple-element.86), channel_id=1, source_target_pairs={{0,64},{64,0},{1,65},{65,1},{2,66},{66,2},{3,67},{67,3},{4,68},{68... | collective-permute-start | bytes 589832 | tf_op jit(solution)/shard_map/ppermute | solution.py:428
  53.3 34.4 %collective-permute-start.4 = (bf16[8,96,128]{2,1,0:T(8,128)(2,1)S(1)}, bf16[8,96,128]{2,1,0:T(8,128)(2,1)S(1)}, u32[]{:S(2)}, u32[]{:S(2)}) collective-permute-start(bf16[8,96,128]{2,1,0:T(8,128)(2,1)S(1)} %get-tuple-element.87), channel_id=1, source_target_pairs={{0,64},{64,0},{1,65},{65,1},{2,66},{66,2},{3,67},{67,3},{4,68},{68... | collective-permute-start | bytes 589832 | tf_op jit(solution)/shard_map/ppermute | solution.py:429
  57.4 12.9 %copy-start.5 = (bf16[128,128]{1,0:T(8,128)(2,1)S(1)}, bf16[128,128]{1,0:T(8,128)(2,1)}, u32[]{:S(2)}) copy-start(bf16[128,128]{1,0:T(8,128)(2,1)} %refs_2_.2) | copy-start | bytes 98308
  59.9 27.8 %copy-start.6 = (f32[10,112,128]{2,1,0:T(8,128)}, f32[10,112,128]{2,1,0:T(8,128)S(1)}, u32[]{:S(2)}) copy-start(f32[10,112,128]{2,1,0:T(8,128)S(1)} %get-tuple-element.56.nslope_ref) | copy-start | bytes 1720324
  59.9 27.8 %copy-start.8 = (bf16[16,112,128]{2,1,0:T(8,128)(2,1)}, bf16[16,112,128]{2,1,0:T(8,128)(2,1)S(1)}, u32[]{:S(2)}) copy-start(bf16[16,112,128]{2,1,0:T(8,128)(2,1)S(1)} %get-tuple-element.57.one_ref) | copy-start | bytes 1376260
  59.9 27.8 %copy-start.4 = (bf16[128,384]{1,0:T(8,128)(2,1)S(1)}, bf16[128,384]{1,0:T(8,128)(2,1)}, u32[]{:S(2)}) copy-start(bf16[128,384]{1,0:T(8,128)(2,1)} %refs_6_.1) | copy-start | bytes 294916
  59.9 54.9 %collective-permute-start.7 = (bf16[8,96,128]{2,1,0:T(8,128)(2,1)S(1)}, bf16[8,96,128]{2,1,0:T(8,128)(2,1)}, u32[]{:S(2)}, u32[]{:S(2)}) collective-permute-start(bf16[8,96,128]{2,1,0:T(8,128)(2,1)S(1)} %get-tuple-element.60), channel_id=1, source_target_pairs={{0,64},{64,0},{1,65},{65,1},{2,66},{66,2},{3,67},{67,3},{4,68},{68... | collective-permute-start | bytes 589832 | tf_op jit(solution)/shard_map/ppermute | solution.py:434
  106.2 28.0 %copy-start.11 = (bf16[8,90,128]{2,1,0:T(8,128)(2,1)S(1)}, bf16[8,90,128]{2,1,0:T(8,128)(2,1)}, u32[]{:S(2)}) copy-start(bf16[8,90,128]{2,1,0:T(8,128)(2,1)} %copy-done.10) | copy-start | bytes 552964
  106.2 28.0 %copy-start.13 = (bf16[8,28,128]{2,1,0:T(8,128)(2,1)S(1)}, bf16[8,28,128]{2,1,0:T(8,128)(2,1)}, u32[]{:S(2)}) copy-start(bf16[8,28,128]{2,1,0:T(8,128)(2,1)} %copy-done.12) | copy-start | bytes 172036
  106.2 15.6 %collective-permute-start.6 = (bf16[8,96,128]{2,1,0:T(8,128)(2,1)}, bf16[8,96,128]{2,1,0:T(8,128)(2,1)S(1)}, u32[]{:S(2)}, u32[]{:S(2)}) collective-permute-start(bf16[8,96,128]{2,1,0:T(8,128)(2,1)} %get-tuple-element.51), channel_id=1, source_target_pairs={{0,64},{64,0},{1,65},{65,1},{2,66},{66,2},{3,67},{67,3},{4,68},{68... | collective-permute-start | bytes 589832 | tf_op jit(solution)/shard_map/ppermute | solution.py:443
  121.7 12.5 %copy-start.19 = (bf16[1,128,128]{2,1,0:T(8,128)(2,1)S(1)}, bf16[1,128,128]{2,1,0:T(8,128)(2,1)}, u32[]{:S(2)}) copy-start(bf16[1,128,128]{2,1,0:T(8,128)(2,1)} %slice.217) | copy-start | bytes 98308
  122.6 22.7 %copy-start.14 = (bf16[8,128,128]{2,1,0:T(8,128)(2,1)S(1)}, bf16[8,128,128]{2,1,0:T(8,128)(2,1)}, u32[]{:S(2)}) copy-start(bf16[8,128,128]{2,1,0:T(8,128)(2,1)} %pad_maximum_fusion.10) | copy-start | bytes 786436
  122.6 17.7 %all-to-all-start.1 = ((bf16[8,112,128]{2,1,0:T(8,128)(2,1)}), bf16[8,112,128]{2,1,0:T(8,128)(2,1)S(1)}, u32[]{:S(2)}, u32[]{:S(2)}) async-start(bf16[8,112,128]{2,1,0:T(8,128)(2,1)} %bitcast.4), calls=%async_computation.1 | async-start | bytes 458752 | tf_op jit(solution)/shard_map/all_to_all | solution.py:456
  140.4 13.2 %all-to-all-start.2 = ((bf16[8,192,128]{2,1,0:T(8,128)(2,1)}), bf16[8,192,128]{2,1,0:T(8,128)(2,1)}, u32[]{:S(2)}, u32[]{:S(2)}) async-start(bf16[8,192,128]{2,1,0:T(8,128)(2,1)} %pad_maximum_fusion.3), calls=%async_computation.2 | async-start | bytes 786432 | tf_op jit(solution)/shard_map/all_to_all | solution.py:396
  146.2 9.3 %collective-permute-start.8 = (bf16[6,112,128]{2,1,0:T(8,128)(2,1)}, bf16[6,112,128]{2,1,0:T(8,128)(2,1)S(1)}, u32[]{:S(2)}, u32[]{:S(2)}) collective-permute-start(bf16[6,112,128]{2,1,0:T(8,128)(2,1)} %pad_maximum_fusion.16), channel_id=1, source_target_pairs={{0,1},{1,2},{2,3},{3,4},{4,5},{5,6},{6,7},{7,8},{8,9},{9,10},{10,1... | collective-permute-start | bytes 516104 | tf_op jit(solution)/shard_map/ppermute | solution.py:51
  148.2 7.9 %collective-permute-start.9 = (bf16[6,112,128]{2,1,0:T(8,128)(2,1)}, bf16[6,112,128]{2,1,0:T(8,128)(2,1)S(1)}, u32[]{:S(2)}, u32[]{:S(2)}) collective-permute-start(bf16[6,112,128]{2,1,0:T(8,128)(2,1)} %pad_maximum_fusion.17), channel_id=1, source_target_pairs={{1,0},{2,1},{3,2},{4,3},{5,4},{6,5},{7,6},{8,7},{9,8},{10,9},{11,1... | collective-permute-start | bytes 516104 | tf_op jit(solution)/shard_map/ppermute | solution.py:52
  155.4 1.2 copy-start.7
  155.4 1.3 copy-start.9
  244.9 19.9 %all-to-all-start.6 = ((bf16[32,88,128]{2,1,0:T(8,128)(2,1)}), bf16[32,88,128]{2,1,0:T(8,128)(2,1)S(1)}, u32[]{:S(2)}, u32[]{:S(2)}) async-start(bf16[32,88,128]{2,1,0:T(8,128)(2,1)} %broadcast_in_dim.31), calls=%async_computation.6 | async-start | bytes 1441792 | tf_op jit(solution)/shard_map/all_to_all | solution.py:381
  (2 other events, 2.0 us)

commit v8 on v6

--- a/solution.py
+++ b/solution.py
@@ -431,12 +431,12 @@
     cot_near = jnp.concatenate([low[5:], cot_x, high[5:]], axis=0)[:, :112]
 
     hidden_two, hidden_one, near_slope, wide_slope = forward(lat_at, feat_x, conv_near, conv_wide)
-    hid_far = lax.ppermute(hidden_two, "zh", SWAP)
     far_one, hidden_two = lax.optimization_barrier((far_one, hidden_two))
 
     half = HEADS // 2
     first = attention(own_rows, far_one, proj_out, (0, half))
-    first, proj_out = lax.optimization_barrier((first, proj_out))
+    first, proj_out, hidden_two = lax.optimization_barrier((first, proj_out, hidden_two))
+    hid_far = lax.ppermute(hidden_two, "zh", SWAP)
     own_part, far_edge, sent, out_term, own_qkv, far_kv = attention(
         own_rows, far_two, proj_out, (half, HEADS), first, proj_qkv
     )

time: 262 us -> 261 us (level)
  starting transfers between devices: 82.8 us -> 98.6 us
  blocking collectives: 80.8 us -> 65.5 us
    ppermute x2, starting transfers between devices: 3.63 us -> 17.6 us  [exchange_lat(): low = lax.ppermute(bottom, LAT_AXES, chain)]
    all_to_all x1, blocking collectives: 39.4 us -> 31 us  [reduce_all(): lax.all_to_all(terms.reshape(32, part, channels), ('x', 'y', 'core'), 0,...]
    ppermute x1, starting transfers between devices: 16.8 us -> 9.97 us  [exchange_lon(): outer = lax.ppermute(jnp.where(at_zero, left, right), LON_AXES, pairs)]
    all_to_all x1, blocking collectives: 27.5 us -> 20.7 us  [reduce_all(): band = lax.all_to_all(band, ('zh', 'zl'), 0, 0, tiled=True)]
    ppermute x1, starting transfers between devices: 3.94 us -> 8.79 us  [exchange_lon(): inner = lax.ppermute(jnp.where(at_zero, right, left), 'core', SWAP)]
    ppermute x2, waiting for transfers between devices: 7.83 us -> 3.66 us  [exchange_lat(): high = lax.ppermute(top, LAT_AXES, [(b, a) for a, b in chain])]
    ppermute x1, waiting for transfers between devices: 0.01 us -> 3.01 us  [exchange_lon(): outer = lax.ppermute(jnp.where(at_zero, left, right), LON_AXES, pairs)]
    all_to_all x2, starting transfers between devices: 13.7 us -> 16.4 us  [to_rows(): lax.all_to_all(jnp.concatenate(grown, axis=1), PLANE, 0, 0, tiled=True)]
  transfers between devices with their start and end apart: 14 -> 14, of which waited for: 9 -> 10; matrix products, arithmetic and copies ran while one was open for 3% -> 3% of each run, Pallas kernels for 14% -> 14%
where the time goes in v8:
time: 261 us; the launch traced here: 260 us
  starting transfers between devices  98.6 us (38%)
  blocking collectives  65.5 us (25%)
  Pallas kernels  39.9 us (15%)
  waiting for transfers between devices  34.2 us (13%)
  local copies, waits for them, and re-layouts  11 us (4%)
  other arithmetic  8.69 us (3%)
    pallas_call x2, Pallas kernels, attention(): pl.pallas_call(functools.partial(attend_rows, heads=heads, last=first is...  35.1 us
    all_to_all x1, blocking collectives, reduce_all(): lax.all_to_all(terms.reshape(32, part, channels), ('x', 'y', 'core'), 0,...  31 us
    all_to_all x1, blocking collectives, reduce_all(): band = lax.all_to_all(band, ('zh', 'zl'), 0, 0, tiled=True)  20.7 us
    ppermute x2, starting transfers between devices, exchange_lat(): low = lax.ppermute(bottom, LAT_AXES, chain)  17.6 us
    all_to_all x2, starting transfers between devices, to_rows(): lax.all_to_all(jnp.concatenate(grown, axis=1), PLANE, 0, 0, tiled=True)  16.4 us
    all_to_all x1, blocking collectives, reduce_all(): lax.all_to_all(jnp.broadcast_to(band[None], (16, piece)), ('zh', 'zl'), 0...  13.8 us
    all_to_all x1, waiting for transfers between devices, reduce_all(): lax.all_to_all(jnp.broadcast_to(band[None], (32, part, channels)), ('x',...  12.8 us
    ppermute x1, starting transfers between devices, on_device(): hid_far = lax.ppermute(hidden_two, 'zh', SWAP)  11 us
  transfers between devices with their start and end apart: 14, of which 10 were waited for; matrix products, arithmetic and copies ran while one was open for 3% of the time, Pallas kernels for 14%

profile of v8, /device:TPU:1, one launch (start us, length us, event | category | flops | bytes accessed | tf_op | source)
XLA Modules:
  0.0 260.1 jit_solution(2638626050734624656)
XLA Ops:
  2.9 8.8 %collective-permute-start.1 = (bf16[8,16,128]{2,1,0:T(8,128)(2,1)S(1)}, bf16[8,16,128]{2,1,0:T(8,128)(2,1)S(1)}, u32[]{:S(2)}, u32[]{:S(2)}) collective-permute-start(bf16[8,16,128]{2,1,0:T(8,128)(2,1)S(1)} %get-tuple-element.112), channel_id=1, source_target_pairs={{0,32},{32,0},{1,33},{33,1},{2,34},{34,2},{3,35},{35,3},{4,36},{36... | collective-permute-start | bytes 98312 | tf_op jit(solution)/shard_map/ppermute | solution.py:43
  11.7 10.0 %collective-permute-start = (bf16[8,16,128]{2,1,0:T(8,128)(2,1)S(1)}, bf16[8,16,128]{2,1,0:T(8,128)(2,1)S(1)}, u32[]{:S(2)}, u32[]{:S(2)}) collective-permute-start(bf16[8,16,128]{2,1,0:T(8,128)(2,1)S(1)} %get-tuple-element.113), channel_id=1, source_target_pairs={{0,480},{32,64},{64,32},{96,128},{128,96},{160,192},{192,160},{224... | collective-permute-start | bytes 98312 | tf_op jit(solution)/shard_map/ppermute | solution.py:45
  22.7 3.0 %collective-permute-done = bf16[8,16,128]{2,1,0:T(8,128)(2,1)S(1)} collective-permute-done((bf16[8,16,128]{2,1,0:T(8,128)(2,1)S(1)}, bf16[8,16,128]{2,1,0:T(8,128)(2,1)S(1)}, u32[]{:S(2)}, u32[]{:S(2)}) %collective-permute-start) | collective-permute-done | bytes 32800 | tf_op jit(solution)/shard_map/ppermute | solution.py:45
  27.2 5.6 %all-to-all-start = ((bf16[8,384,128]{2,1,0:T(8,128)(2,1)}), bf16[8,384,128]{2,1,0:T(8,128)(2,1)S(1)}, u32[]{:S(2)}, u32[]{:S(2)}) async-start(bf16[8,384,128]{2,1,0:T(8,128)(2,1)} %fusion.4), calls=%async_computation | async-start | bytes 1572864 | tf_op jit(solution)/shard_map/all_to_all | solution.py:396
  33.0 1.3 collective-permute-start.3
  34.3 4.0 %collective-permute-start.2 = (bf16[6,128,128]{2,1,0:T(8,128)(2,1)S(1)}, bf16[6,128,128]{2,1,0:T(8,128)(2,1)S(1)}, u32[]{:S(2)}, u32[]{:S(2)}) collective-permute-start(bf16[6,128,128]{2,1,0:T(8,128)(2,1)S(1)} %get-tuple-element.93), channel_id=1, source_target_pairs={{0,1},{1,2},{2,3},{3,4},{4,5},{5,6},{6,7},{7,8},{8,9},{9,10},{10,1... | collective-permute-start | bytes 589832 | tf_op jit(solution)/shard_map/ppermute | solution.py:51
  39.3 2.1 collective-permute-done.3
  42.3 2.8 %all-to-all-done.refs_0_ = bf16[8,384,128]{2,1,0:T(8,128)(2,1)S(1)} async-done(((bf16[8,384,128]{2,1,0:T(8,128)(2,1)}), bf16[8,384,128]{2,1,0:T(8,128)(2,1)S(1)}, u32[]{:S(2)}, u32[]{:S(2)}) %all-to-all-start) | async-done | bytes 786464 | tf_op jit(solution)/shard_map/all_to_all | solution.py:396
  45.2 10.7 %collective-permute-start.5 = (bf16[8,96,128]{2,1,0:T(8,128)(2,1)S(1)}, bf16[8,96,128]{2,1,0:T(8,128)(2,1)S(1)}, u32[]{:S(2)}, u32[]{:S(2)}) collective-permute-start(bf16[8,96,128]{2,1,0:T(8,128)(2,1)S(1)} %get-tuple-element.88), channel_id=1, source_target_pairs={{0,64},{64,0},{1,65},{65,1},{2,66},{66,2},{3,67},{67,3},{4,68},{68... | collective-permute-start | bytes 589832 | tf_op jit(solution)/shard_map/ppermute | solution.py:428
  55.9 3.3 %collective-permute-start.4 = (bf16[8,96,128]{2,1,0:T(8,128)(2,1)S(1)}, bf16[8,96,128]{2,1,0:T(8,128)(2,1)S(1)}, u32[]{:S(2)}, u32[]{:S(2)}) collective-permute-start(bf16[8,96,128]{2,1,0:T(8,128)(2,1)S(1)} %get-tuple-element.89), channel_id=1, source_target_pairs={{0,64},{64,0},{1,65},{65,1},{2,66},{66,2},{3,67},{67,3},{4,68},{68... | collective-permute-start | bytes 589832 | tf_op jit(solution)/shard_map/ppermute | solution.py:429
  59.3 2.5 forward_block.1
  62.6 17.4 %attend_rows.2 = (bf16[768,128]{1,0:T(8,128)(2,1)S(1)}, bf16[768,384]{1,0:T(8,128)(2,1)S(1)}, bf16[768,256]{1,0:T(8,128)(2,1)S(1)}) custom-call(bf16[8,384,128]{2,1,0:T(8,128)(2,1)S(1)} %all-to-all-done.refs_0_, bf16[8,96,128]{2,1,0:T(8,128)(2,1)S(1)} %collective-permute-done.5.refs_1_, bf16[128,128]{1,0:T(8,128)(2,1)S(1)} %copy-done.5), custom_call_target="tpu_custom_call" | custom-call | flops 7247757312 | bytes 1572864 | tf_op jit(solution)/shard_map/attend_rows/pallas_call | solution.py:189
  80.1 11.0 %collective-permute-start.6 = (bf16[8,96,128]{2,1,0:T(8,128)(2,1)S(1)}, bf16[8,96,128]{2,1,0:T(8,128)(2,1)S(1)}, u32[]{:S(2)}, u32[]{:S(2)}) collective-permute-start(bf16[8,96,128]{2,1,0:T(8,128)(2,1)S(1)} %get-tuple-element.54), channel_id=1, source_target_pairs={{0,64},{64,0},{1,65},{65,1},{2,66},{66,2},{3,67},{67,3},{4,68},{68... | collective-permute-start | bytes 589832 | tf_op jit(solution)/shard_map/ppermute | solution.py:439
  91.1 17.7 %attend_rows.3 = (f32[8,96,128]{2,1,0:T(8,128)S(1)}, f32[8,8,128]{2,1,0:T(8,128)S(1)}, bf16[8,96,128]{2,1,0:T(8,128)(2,1)S(1)}, f32[128,128]{1,0:T(8,128)S(1)}, ...) custom-call(bf16[8,384,128]{2,1,0:T(8,128)(2,1)S(1)} %all-to-all-done.refs_0_, ...), custom_call_target="tpu_custom_call" | custom-call | flops 7247757312 | bytes 1572864 | tf_op jit(solution)/shard_map/attend_rows/pallas_call | solution.py:189
  108.9 3.3 %collective-permute-start.7 = (bf16[8,96,128]{2,1,0:T(8,128)(2,1)S(1)}, bf16[8,96,128]{2,1,0:T(8,128)(2,1)}, u32[]{:S(2)}, u32[]{:S(2)}) collective-permute-start(bf16[8,96,128]{2,1,0:T(8,128)(2,1)S(1)} %get-tuple-element.55), channel_id=1, source_target_pairs={{0,64},{64,0},{1,65},{65,1},{2,66},{66,2},{3,67},{67,3},{4,68},{68... | collective-permute-start | bytes 589832 | tf_op jit(solution)/shard_map/ppermute | solution.py:445
  113.0 10.9 %all-to-all-start.2 = ((bf16[8,192,128]{2,1,0:T(8,128)(2,1)}), bf16[8,192,128]{2,1,0:T(8,128)(2,1)S(1)}, u32[]{:S(2)}, u32[]{:S(2)}) async-start(bf16[8,192,128]{2,1,0:T(8,128)(2,1)} %pad_maximum_fusion.3), calls=%async_computation.2 | async-start | bytes 786432 | tf_op jit(solution)/shard_map/all_to_all | solution.py:396
  123.9 3.4 %collective-permute-done.7 = bf16[8,96,128]{2,1,0:T(8,128)(2,1)} collective-permute-done((bf16[8,96,128]{2,1,0:T(8,128)(2,1)S(1)}, bf16[8,96,128]{2,1,0:T(8,128)(2,1)}, u32[]{:S(2)}, u32[]{:S(2)}) %collective-permute-start.7) | collective-permute-done | bytes 196640 | tf_op jit(solution)/shard_map/ppermute | solution.py:445
  129.8 2.3 all-to-all-done.2
  132.9 8.7 %all-to-all-start.1 = ((bf16[8,112,128]{2,1,0:T(8,128)(2,1)}), bf16[8,112,128]{2,1,0:T(8,128)(2,1)S(1)}, u32[]{:S(2)}, u32[]{:S(2)}) async-start(bf16[8,112,128]{2,1,0:T(8,128)(2,1)} %bitcast.4), calls=%async_computation.1 | async-start | bytes 458752 | tf_op jit(solution)/shard_map/all_to_all | solution.py:457
  141.5 1.1 fusion.28
  143.4 4.3 %all-to-all-done.1 = bf16[8,112,128]{2,1,0:T(8,128)(2,1)S(1)} async-done(((bf16[8,112,128]{2,1,0:T(8,128)(2,1)}), bf16[8,112,128]{2,1,0:T(8,128)(2,1)S(1)}, u32[]{:S(2)}, u32[]{:S(2)}) %all-to-all-start.1) | async-done | bytes 229408 | tf_op jit(solution)/shard_map/all_to_all | solution.py:457
  147.9 1.3 collective-permute-start.9
  149.3 13.5 %collective-permute-start.8 = (bf16[6,112,128]{2,1,0:T(8,128)(2,1)S(1)}, bf16[6,112,128]{2,1,0:T(8,128)(2,1)S(1)}, u32[]{:S(2)}, u32[]{:S(2)}) collective-permute-start(bf16[6,112,128]{2,1,0:T(8,128)(2,1)S(1)} %pad_maximum_fusion.16), channel_id=1, source_target_pairs={{0,1},{1,2},{2,3},{3,4},{4,5},{5,6},{6,7},{7,8},{8,9},{9,10},{10,1... | collective-permute-start | bytes 516104 | tf_op jit(solution)/shard_map/ppermute | solution.py:51
  162.9 1.5 collective-permute-done.9
  164.4 1.1 collective-permute-done.8
  165.7 2.3 backward_block.1
  168.1 31.0 %all_to_all.41 = bf16[32,88,128]{2,1,0:T(8,128)(2,1)S(1)} all-to-all(bf16[32,88,128]{2,1,0:T(8,128)(2,1)S(1)} %bitcast.22), channel_id=1, replica_groups=mesh['x'=4,'zh'=2,'core'=2,'zl'=8,'y'=4] {'x','y','core'}, dimensions={0} | all-to-all | bytes 1441792 | tf_op jit(solution)/shard_map/all_to_all | solution.py:372
  200.7 20.7 %all_to_all.42 = bf16[16,2,352]{2,1,0:T(2,128)(2,1)S(1)} all-to-all(bf16[16,2,352]{2,1,0:T(2,128)(2,1)S(1)} %reshape.80), channel_id=1, replica_groups=mesh['x'=4,'zh'=2,'core'=2,'zl'=8,'y'=4] {'zh','zl'}, dimensions={0} | all-to-all | bytes 45056 | tf_op jit(solution)/shard_map/all_to_all | solution.py:376
  222.5 13.8 %all_to_all.43 = bf16[16,2,352]{2,1,0:T(2,128)(2,1)S(1)} all-to-all(bf16[16,2,352]{2,1,0:T(2,128)(2,1)S(1)} %reshape.82), channel_id=1, replica_groups=mesh['x'=4,'zh'=2,'core'=2,'zl'=8,'y'=4] {'zh','zl'}, dimensions={0} | all-to-all | bytes 45056 | tf_op jit(solution)/shard_map/all_to_all | solution.py:378
  237.7 6.3 %all-to-all-start.6 = ((bf16[32,88,128]{2,1,0:T(8,128)(2,1)}), bf16[32,88,128]{2,1,0:T(8,128)(2,1)S(1)}, u32[]{:S(2)}, u32[]{:S(2)}) async-start(bf16[32,88,128]{2,1,0:T(8,128)(2,1)} %broadcast_in_dim.31), calls=%async_computation.6 | async-start | bytes 1441792 | tf_op jit(solution)/shard_map/all_to_all | solution.py:381
  244.7 12.8 %all-to-all-done.6 = bf16[32,88,128]{2,1,0:T(8,128)(2,1)S(1)} async-done(((bf16[32,88,128]{2,1,0:T(8,128)(2,1)}), bf16[32,88,128]{2,1,0:T(8,128)(2,1)S(1)}, u32[]{:S(2)}, u32[]{:S(2)}) %all-to-all-start.6) | async-done | bytes 720928 | tf_op jit(solution)/shard_map/all_to_all | solution.py:381
  258.3 1.1 fusion.26
  (121 shorter events, 19.2 us)
Async XLA Ops:
  0.6 25.1 %copy-start.19 = (bf16[8,90,128]{2,0,1:T(8,128)(2,1)S(1)}, bf16[8,90,128]{2,0,1:T(8,128)(2,1)}, u32[]{:S(2)}) copy-start(bf16[8,90,128]{2,0,1:T(8,128)(2,1)} %param.12) | copy-start | bytes 552964
  0.6 25.0 %copy-start.18 = (bf16[8,90,128]{2,0,1:T(8,128)(2,1)S(1)}, bf16[8,90,128]{2,0,1:T(8,128)(2,1)}, u32[]{:S(2)}) copy-start(bf16[8,90,128]{2,0,1:T(8,128)(2,1)} %param.11) | copy-start | bytes 552964
  1.7 36.8 %copy-start.10 = (bf16[8,90,128]{2,1,0:T(8,128)(2,1)}, bf16[8,90,128]{2,1,0:T(8,128)(2,1)S(1)}, u32[]{:S(2)}) copy-start(bf16[8,90,128]{2,1,0:T(8,128)(2,1)S(1)} %copy.41) | copy-start | bytes 552964
  2.9 19.7 %collective-permute-start.1 = (bf16[8,16,128]{2,1,0:T(8,128)(2,1)S(1)}, bf16[8,16,128]{2,1,0:T(8,128)(2,1)S(1)}, u32[]{:S(2)}, u32[]{:S(2)}) collective-permute-start(bf16[8,16,128]{2,1,0:T(8,128)(2,1)S(1)} %get-tuple-element.112), channel_id=1, source_target_pairs={{0,32},{32,0},{1,33},{33,1},{2,34},{34,2},{3,35},{35,3},{4,36},{36... | collective-permute-start | bytes 98312 | tf_op jit(solution)/shard_map/ppermute | solution.py:43
  11.7 13.9 %collective-permute-start = (bf16[8,16,128]{2,1,0:T(8,128)(2,1)S(1)}, bf16[8,16,128]{2,1,0:T(8,128)(2,1)S(1)}, u32[]{:S(2)}, u32[]{:S(2)}) collective-permute-start(bf16[8,16,128]{2,1,0:T(8,128)(2,1)S(1)} %get-tuple-element.113), channel_id=1, source_target_pairs={{0,480},{32,64},{64,32},{96,128},{128,96},{160,192},{192,160},{224... | collective-permute-start | bytes 98312 | tf_op jit(solution)/shard_map/ppermute | solution.py:45
  27.2 17.9 %all-to-all-start = ((bf16[8,384,128]{2,1,0:T(8,128)(2,1)}), bf16[8,384,128]{2,1,0:T(8,128)(2,1)S(1)}, u32[]{:S(2)}, u32[]{:S(2)}) async-start(bf16[8,384,128]{2,1,0:T(8,128)(2,1)} %fusion.4), calls=%async_computation | async-start | bytes 1572864 | tf_op jit(solution)/shard_map/all_to_all | solution.py:396
  33.0 12.2 %copy-start.13 = (bf16[8,28,128]{2,1,0:T(8,128)(2,1)}, bf16[8,28,128]{2,1,0:T(8,128)(2,1)S(1)}, u32[]{:S(2)}) copy-start(bf16[8,28,128]{2,1,0:T(8,128)(2,1)S(1)} %broadcast_in_dim.26) | copy-start | bytes 172036
  33.0 8.4 %collective-permute-start.3 = (bf16[6,128,128]{2,1,0:T(8,128)(2,1)S(1)}, bf16[6,128,128]{2,1,0:T(8,128)(2,1)S(1)}, u32[]{:S(2)}, u32[]{:S(2)}) collective-permute-start(bf16[6,128,128]{2,1,0:T(8,128)(2,1)S(1)} %get-tuple-element.92), channel_id=1, source_target_pairs={{1,0},{2,1},{3,2},{4,3},{5,4},{6,5},{7,6},{8,7},{9,8},{10,9},{11,1... | collective-permute-start | bytes 589832 | tf_op jit(solution)/shard_map/ppermute | solution.py:52
  34.3 7.9 %collective-permute-start.2 = (bf16[6,128,128]{2,1,0:T(8,128)(2,1)S(1)}, bf16[6,128,128]{2,1,0:T(8,128)(2,1)S(1)}, u32[]{:S(2)}, u32[]{:S(2)}) collective-permute-start(bf16[6,128,128]{2,1,0:T(8,128)(2,1)S(1)} %get-tuple-element.93), channel_id=1, source_target_pairs={{0,1},{1,2},{2,3},{3,4},{4,5},{5,6},{6,7},{7,8},{8,9},{9,10},{10,1... | collective-permute-start | bytes 589832 | tf_op jit(solution)/shard_map/ppermute | solution.py:51
  39.3 20.0 %copy-start = (bf16[3,3,128,128]{3,2,1,0:T(8,128)(2,1)S(1)}, bf16[3,3,128,128]{3,2,1,0:T(8,128)(2,1)}, u32[]{:S(2)}) copy-start(bf16[3,3,128,128]{3,2,1,0:T(8,128)(2,1)} %near_ref.3) | copy-start | bytes 884740
  39.3 20.0 %copy-start.2 = (bf16[3,3,128,128]{3,2,1,0:T(8,128)(2,1)S(1)}, bf16[3,3,128,128]{3,2,1,0:T(8,128)(2,1)}, u32[]{:S(2)}) copy-start(bf16[3,3,128,128]{3,2,1,0:T(8,128)(2,1)} %dil_ref.1) | copy-start | bytes 884740
  41.4 14.5 %copy-start.16 = (bf16[6,128,128]{2,1,0:T(8,128)(2,1)}, bf16[6,128,128]{2,1,0:T(8,128)(2,1)S(1)}, u32[]{:S(2)}) copy-start(bf16[6,128,128]{2,1,0:T(8,128)(2,1)S(1)} %collective-permute-done.3) | copy-start | bytes 589828
  42.3 17.0 %copy-start.17 = (bf16[6,128,128]{2,1,0:T(8,128)(2,1)}, bf16[6,128,128]{2,1,0:T(8,128)(2,1)S(1)}, u32[]{:S(2)}) copy-start(bf16[6,128,128]{2,1,0:T(8,128)(2,1)S(1)} %collective-permute-done.2) | copy-start | bytes 589828
  45.2 17.5 %collective-permute-start.5 = (bf16[8,96,128]{2,1,0:T(8,128)(2,1)S(1)}, bf16[8,96,128]{2,1,0:T(8,128)(2,1)S(1)}, u32[]{:S(2)}, u32[]{:S(2)}) collective-permute-start(bf16[8,96,128]{2,1,0:T(8,128)(2,1)S(1)} %get-tuple-element.88), channel_id=1, source_target_pairs={{0,64},{64,0},{1,65},{65,1},{2,66},{66,2},{3,67},{67,3},{4,68},{68... | collective-permute-start | bytes 589832 | tf_op jit(solution)/shard_map/ppermute | solution.py:428
  55.9 35.2 %collective-permute-start.4 = (bf16[8,96,128]{2,1,0:T(8,128)(2,1)S(1)}, bf16[8,96,128]{2,1,0:T(8,128)(2,1)S(1)}, u32[]{:S(2)}, u32[]{:S(2)}) collective-permute-start(bf16[8,96,128]{2,1,0:T(8,128)(2,1)S(1)} %get-tuple-element.89), channel_id=1, source_target_pairs={{0,64},{64,0},{1,65},{65,1},{2,66},{66,2},{3,67},{67,3},{4,68},{68... | collective-permute-start | bytes 589832 | tf_op jit(solution)/shard_map/ppermute | solution.py:429
  62.6 17.4 %copy-start.8 = (bf16[16,112,128]{2,1,0:T(8,128)(2,1)}, bf16[16,112,128]{2,1,0:T(8,128)(2,1)S(1)}, u32[]{:S(2)}) copy-start(bf16[16,112,128]{2,1,0:T(8,128)(2,1)S(1)} %get-tuple-element.60.one_ref) | copy-start | bytes 1376260
  62.6 28.5 %copy-start.4 = (bf16[128,384]{1,0:T(8,128)(2,1)S(1)}, bf16[128,384]{1,0:T(8,128)(2,1)}, u32[]{:S(2)}) copy-start(bf16[128,384]{1,0:T(8,128)(2,1)} %refs_6_.1) | copy-start | bytes 294916
  80.0 32.1 %copy-start.11 = (bf16[8,90,128]{2,1,0:T(8,128)(2,1)S(1)}, bf16[8,90,128]{2,1,0:T(8,128)(2,1)}, u32[]{:S(2)}) copy-start(bf16[8,90,128]{2,1,0:T(8,128)(2,1)} %copy-done.10) | copy-start | bytes 552964
  80.0 32.1 %copy-start.14 = (bf16[8,28,128]{2,1,0:T(8,128)(2,1)S(1)}, bf16[8,28,128]{2,1,0:T(8,128)(2,1)}, u32[]{:S(2)}) copy-start(bf16[8,28,128]{2,1,0:T(8,128)(2,1)} %copy-done.13) | copy-start | bytes 172036
  80.0 32.1 %slice-start = ((bf16[6,128,128]{2,1,0:T(8,128)(2,1)}), bf16[1,128,128]{2,1,0:T(8,128)(2,1)S(1)}, s32[]{:S(2)}) async-start(bf16[6,128,128]{2,1,0:T(8,128)(2,1)} %copy-done.16), calls=%async_computation.7 | async-start | bytes 65536 | tf_op jit(solution)/shard_map/slice | solution.py:431
  80.0 32.1 %slice-start.1 = ((bf16[6,128,128]{2,1,0:T(8,128)(2,1)}), bf16[1,128,128]{2,1,0:T(8,128)(2,1)S(1)}, s32[]{:S(2)}) async-start(bf16[6,128,128]{2,1,0:T(8,128)(2,1)} %copy-done.17), calls=%async_computation.8 | async-start | bytes 65536 | tf_op jit(solution)/shard_map/slice | solution.py:431
  80.1 28.8 %collective-permute-start.6 = (bf16[8,96,128]{2,1,0:T(8,128)(2,1)S(1)}, bf16[8,96,128]{2,1,0:T(8,128)(2,1)S(1)}, u32[]{:S(2)}, u32[]{:S(2)}) collective-permute-start(bf16[8,96,128]{2,1,0:T(8,128)(2,1)S(1)} %get-tuple-element.54), channel_id=1, source_target_pairs={{0,64},{64,0},{1,65},{65,1},{2,66},{66,2},{3,67},{67,3},{4,68},{68... | collective-permute-start | bytes 589832 | tf_op jit(solution)/shard_map/ppermute | solution.py:439
  108.9 18.4 %collective-permute-start.7 = (bf16[8,96,128]{2,1,0:T(8,128)(2,1)S(1)}, bf16[8,96,128]{2,1,0:T(8,128)(2,1)}, u32[]{:S(2)}, u32[]{:S(2)}) collective-permute-start(bf16[8,96,128]{2,1,0:T(8,128)(2,1)S(1)} %get-tuple-element.55), channel_id=1, source_target_pairs={{0,64},{64,0},{1,65},{65,1},{2,66},{66,2},{3,67},{67,3},{4,68},{68... | collective-permute-start | bytes 589832 | tf_op jit(solution)/shard_map/ppermute | solution.py:445
  113.0 19.1 %all-to-all-start.2 = ((bf16[8,192,128]{2,1,0:T(8,128)(2,1)}), bf16[8,192,128]{2,1,0:T(8,128)(2,1)S(1)}, u32[]{:S(2)}, u32[]{:S(2)}) async-start(bf16[8,192,128]{2,1,0:T(8,128)(2,1)} %pad_maximum_fusion.3), calls=%async_computation.2 | async-start | bytes 786432 | tf_op jit(solution)/shard_map/all_to_all | solution.py:396
  132.9 14.9 %all-to-all-start.1 = ((bf16[8,112,128]{2,1,0:T(8,128)(2,1)}), bf16[8,112,128]{2,1,0:T(8,128)(2,1)S(1)}, u32[]{:S(2)}, u32[]{:S(2)}) async-start(bf16[8,112,128]{2,1,0:T(8,128)(2,1)} %bitcast.4), calls=%async_computation.1 | async-start | bytes 458752 | tf_op jit(solution)/shard_map/all_to_all | solution.py:457
  147.9 16.5 %collective-permute-start.9 = (bf16[6,112,128]{2,1,0:T(8,128)(2,1)S(1)}, bf16[6,112,128]{2,1,0:T(8,128)(2,1)S(1)}, u32[]{:S(2)}, u32[]{:S(2)}) collective-permute-start(bf16[6,112,128]{2,1,0:T(8,128)(2,1)S(1)} %pad_maximum_fusion.17), channel_id=1, source_target_pairs={{1,0},{2,1},{3,2},{4,3},{5,4},{6,5},{7,6},{8,7},{9,8},{10,9},{11,1... | collective-permute-start | bytes 516104 | tf_op jit(solution)/shard_map/ppermute | solution.py:52
  149.3 16.4 %copy-start.1 = (bf16[3,3,128,128]{3,2,1,0:T(8,128)(2,1)S(1)}, bf16[3,3,128,128]{3,2,1,0:T(8,128)(2,1)}, u32[]{:S(2)}) copy-start(bf16[3,3,128,128]{3,2,1,0:T(8,128)(2,1)} %near_ref.3) | copy-start | bytes 884740
  149.3 16.4 %copy-start.3 = (bf16[3,3,128,128]{3,2,1,0:T(8,128)(2,1)S(1)}, bf16[3,3,128,128]{3,2,1,0:T(8,128)(2,1)}, u32[]{:S(2)}) copy-start(bf16[3,3,128,128]{3,2,1,0:T(8,128)(2,1)} %dil_ref.1) | copy-start | bytes 884740
  149.3 16.4 %copy-start.7 = (f32[10,112,128]{2,1,0:T(8,128)S(1)}, f32[10,112,128]{2,1,0:T(8,128)}, u32[]{:S(2)}) copy-start(f32[10,112,128]{2,1,0:T(8,128)} %copy-done.6) | copy-start | bytes 1720324
  149.3 16.4 %copy-start.9 = (bf16[16,112,128]{2,1,0:T(8,128)(2,1)S(1)}, bf16[16,112,128]{2,1,0:T(8,128)(2,1)}, u32[]{:S(2)}) copy-start(bf16[16,112,128]{2,1,0:T(8,128)(2,1)} %copy-done.8) | copy-start | bytes 1376260
  149.3 16.2 %collective-permute-start.8 = (bf16[6,112,128]{2,1,0:T(8,128)(2,1)S(1)}, bf16[6,112,128]{2,1,0:T(8,128)(2,1)S(1)}, u32[]{:S(2)}, u32[]{:S(2)}) collective-permute-start(bf16[6,112,128]{2,1,0:T(8,128)(2,1)S(1)} %pad_maximum_fusion.16), channel_id=1, source_target_pairs={{0,1},{1,2},{2,3},{3,4},{4,5},{5,6},{6,7},{7,8},{8,9},{9,10},{10,1... | collective-permute-start | bytes 516104 | tf_op jit(solution)/shard_map/ppermute | solution.py:51
  237.7 19.8 %all-to-all-start.6 = ((bf16[32,88,128]{2,1,0:T(8,128)(2,1)}), bf16[32,88,128]{2,1,0:T(8,128)(2,1)S(1)}, u32[]{:S(2)}, u32[]{:S(2)}) async-start(bf16[32,88,128]{2,1,0:T(8,128)(2,1)} %broadcast_in_dim.31), calls=%async_computation.6 | async-start | bytes 1441792 | tf_op jit(solution)/shard_map/all_to_all | solution.py:381
  (4 other events, 11.1 us)
